TPU v7x, 256 devices: a whole 4x4x8 slice. The times are simulated.
256 devices in a mesh: sp: 32 (over x, z_lo, core), dp: 8 (over y, z_hi).
Axes of the slice: x: 4, y: 4, z: 8 (z_hi: 2, z_lo: 4; z = z_hi * 4 + z_lo), core: 2. Of those that a mesh axis runs over, the one named last changes fastest.
Arguments:
- queries: bfloat16 [8, 4096, 8192], P('dp', 'sp'), may hold values from -12.5 to 12.5
- key_before_rotary: bfloat16 [8, 4096, 1024], P('dp', 'sp'), may hold values from -5 to 5
- value_inputs: bfloat16 [8, 4096, 1024], P('dp', 'sp'), may hold values from -6 to 6
- out_grad: bfloat16 [8, 4096, 8192], P('dp', 'sp'), may hold values from -6 to 6
- layer_input: bfloat16 [8, 4096, 4096], P('dp', 'sp'), may hold values from -6 to 6
- group_first: int32 [8, 32], P('dp'), may hold values from 0 to 24, as said below
- seq_length: int32 [8, 32], P('dp'), may hold values from 512 to 2048, as said below
- pos_offset: int32 [8, 32], P('dp'), may hold values from 0 to 4095, as said below
Outputs:
- query_grad: bfloat16 [8, 4096, 8192], P('dp', 'sp')
- key_gradient: bfloat16 [8, 4096, 1024], P('dp', 'sp')
- value_gradient: bfloat16 [8, 4096, 1024], P('dp', 'sp')
- kproj_grad: float32 [4096, 1024], P(('sp', 'dp'))
Inputs may be any that keep to these rules, and one draw needn't show every extreme that they name: `group_first`: each half of a row's devices holds either one group of 16 neighbouring devices or two aligned groups of 8; every device of a group holds the same first device, length and offset; in every draw the first group of row 0 has 16 devices. `seq_length`: A group of g devices holds a sequence of at least g * 64 and at most g * 128 tokens; the group starting at device 0 of row 0 is full. `pos_offset`: the group starting at device 0 of row 0 has offset 4095.
All inputs are finite; a program needn't handle non-finite values.
Results may differ from a plain program's by a relative error of at most 0.019.
Values may be sent and summed in bfloat16 or wider, within the bound.
No kernel may reach another device: no remote copies, remote signals or barrier semaphores. Data moves between devices by JAX's collectives and lax.ppermute only.
A program may use at most 128 MiB of HBM per device.

v0:
```python
import math

import jax
import jax.numpy as jnp
from jax import lax
from jax.sharding import PartitionSpec as P

QUERY_HEADS = 64
KEY_VALUE_HEADS = 8
HEAD_SIZE = 128


def angles(positions):
    half_dim = HEAD_SIZE // 2
    rates = jnp.exp(
        jnp.arange(half_dim, dtype=jnp.float32) * (-2.0 * math.log(10000.0) / HEAD_SIZE)
    )
    phase = positions.astype(jnp.float32)[:, None] * rates[None, :]
    return (jnp.cos(phase)[:, None, :], jnp.sin(phase)[:, None, :])


def apply_rotary(field, cosine_table, sine_line):
    half_dim = field.shape[-1] // 2
    first_half = field[..., :half_dim]
    second_half = field[..., half_dim:]
    return jnp.concatenate(
        [
            first_half * cosine_table - second_half * sine_line,
            second_half * cosine_table + first_half * sine_line,
        ],
        -1,
    )


def inverse_rotary(field, cosine_table, sine_line):
    half_dim = field.shape[-1] // 2
    first_half = field[..., :half_dim]
    second_half = field[..., half_dim:]
    return jnp.concatenate(
        [
            first_half * cosine_table + second_half * sine_line,
            second_half * cosine_table - first_half * sine_line,
        ],
        -1,
    )


def attend(
    query_block,
    grad_block,
    key_block,
    value_block,
    query_index,
    key_index,
    query_seq,
    key_seq,
    key_valid,
):
    scaling = HEAD_SIZE ** (-0.5)
    scores = (
        jnp.einsum("ihd,jd->hij", query_block, key_block, preferred_element_type=jnp.float32)
        * scaling
    )
    allowed = (
        (query_seq[:, None] == key_seq[None, :])
        & (key_index[None, :] <= query_index[:, None])
        & key_valid[None, :]
    )
    scores = jnp.where(allowed[None], scores, -1e30)
    row_peak = jnp.max(scores, axis=-1, keepdims=True)
    weights = jnp.exp(scores - row_peak)
    weights = weights / jnp.sum(weights, axis=-1, keepdims=True)
    rounded = weights.astype(jnp.bfloat16)
    prob_grad = jnp.einsum(
        "ihd,jd->hij", grad_block, value_block, preferred_element_type=jnp.float32
    )
    value_part = jnp.einsum("hij,ihd->jd", rounded, grad_block, preferred_element_type=jnp.float32)
    row_dot = jnp.sum(weights * prob_grad, axis=-1, keepdims=True)
    score_grad = (weights * (prob_grad - row_dot) * scaling).astype(jnp.bfloat16)
    query_part = jnp.einsum(
        "hij,jd->ihd", score_grad, key_block, preferred_element_type=jnp.float32
    )
    key_part = jnp.einsum(
        "hij,ihd->jd", score_grad, query_block, preferred_element_type=jnp.float32
    )
    return (query_part, key_part, value_part)


def add_rows(accum, part, start_row):
    current = lax.dynamic_slice_in_dim(accum, start_row, part.shape[0], 0)
    return lax.dynamic_update_slice_in_dim(accum, current + part, start_row, 0)


def local(
    queries,
    key_before_rotary,
    value_inputs,
    out_grad,
    layer_input,
    group_first,
    seq_length,
    pos_offset,
):
    device_local_tokens = queries.shape[1]
    sequence_parallel_width = lax.axis_size("sp")
    my_index = lax.axis_index("sp")
    tokens_per_row = sequence_parallel_width * device_local_tokens
    heads_dev = QUERY_HEADS // sequence_parallel_width
    key_value_repeat = sequence_parallel_width // KEY_VALUE_HEADS
    device_of = jnp.arange(tokens_per_row, dtype=jnp.int32) // device_local_tokens
    inner_pos = jnp.arange(tokens_per_row, dtype=jnp.int32) % device_local_tokens
    seq_ids = jnp.repeat(group_first[0], device_local_tokens)
    local_pos = (device_of - seq_ids) * device_local_tokens + inner_pos
    row_valid_mask = local_pos < jnp.repeat(seq_length[0], device_local_tokens)
    cosine_table, sine_line = angles(jnp.repeat(pos_offset[0], device_local_tokens) + local_pos)
    local_cosine = lax.dynamic_slice_in_dim(
        cosine_table, my_index * device_local_tokens, device_local_tokens, 0
    )
    local_sine = lax.dynamic_slice_in_dim(
        sine_line, my_index * device_local_tokens, device_local_tokens, 0
    )
    own_valid = lax.dynamic_slice_in_dim(
        row_valid_mask, my_index * device_local_tokens, device_local_tokens, 0
    )
    rotated_queries = apply_rotary(
        queries[0].reshape(device_local_tokens, QUERY_HEADS, HEAD_SIZE).astype(jnp.float32),
        local_cosine,
        local_sine,
    )
    rotated_queries = rotated_queries.astype(jnp.bfloat16).reshape(
        device_local_tokens, QUERY_HEADS * HEAD_SIZE
    )
    rotated_keys = apply_rotary(
        key_before_rotary[0]
        .reshape(device_local_tokens, KEY_VALUE_HEADS, HEAD_SIZE)
        .astype(jnp.float32),
        local_cosine,
        local_sine,
    ).astype(jnp.bfloat16)
    incoming_gradient = jnp.where(own_valid[:, None], out_grad[0], jnp.zeros_like(out_grad[0]))
    q_all, grad_all = (
        lax.all_to_all(rotated_queries, "sp", split_axis=1, concat_axis=0, tiled=True),
        lax.all_to_all(incoming_gradient, "sp", split_axis=1, concat_axis=0, tiled=True),
    )
    q_all = q_all.reshape(tokens_per_row, heads_dev, HEAD_SIZE)
    grad_all = grad_all.reshape(tokens_per_row, heads_dev, HEAD_SIZE)
    key_wide = jnp.repeat(rotated_keys, key_value_repeat, axis=1).reshape(
        device_local_tokens, sequence_parallel_width * HEAD_SIZE
    )
    value_wide = jnp.repeat(
        value_inputs[0].reshape(device_local_tokens, KEY_VALUE_HEADS, HEAD_SIZE),
        key_value_repeat,
        axis=1,
    ).reshape(device_local_tokens, sequence_parallel_width * HEAD_SIZE)
    kv_all = lax.all_to_all(
        jnp.stack([key_wide, value_wide]), "sp", split_axis=2, concat_axis=1, tiled=True
    )
    key_all = kv_all[0]
    value_all = kv_all[1]
    block_rows = 4 * device_local_tokens
    block_count = tokens_per_row // block_rows
    halved_rows = tokens_per_row // 2
    per_half = halved_rows // block_rows
    positions = jnp.arange(tokens_per_row, dtype=jnp.int32)

    def block_step(block_id, carry):
        query_acc, key_running_sum, value_running_sum = carry
        start_row = block_id * block_rows
        half_start = block_id // per_half * halved_rows
        inner_block = block_id % per_half
        query_block = lax.dynamic_slice_in_dim(q_all, start_row, block_rows, 0)
        grad_block = lax.dynamic_slice_in_dim(grad_all, start_row, block_rows, 0)
        query_index = lax.dynamic_slice_in_dim(positions, start_row, block_rows, 0)
        query_seq = lax.dynamic_slice_in_dim(seq_ids, start_row, block_rows, 0)

        def make_branch(count):
            key_length = count * block_rows

            def branch(operand):

                def keyed(array):
                    return lax.dynamic_slice_in_dim(array, half_start, key_length, 0)

                query_part, key_part, value_part = attend(
                    query_block,
                    grad_block,
                    keyed(key_all),
                    keyed(value_all),
                    query_index,
                    keyed(positions),
                    query_seq,
                    keyed(seq_ids),
                    keyed(row_valid_mask),
                )
                padding_amount = jnp.zeros((halved_rows - key_length, HEAD_SIZE), jnp.float32)
                return (
                    query_part,
                    jnp.concatenate([key_part, padding_amount], 0),
                    jnp.concatenate([value_part, padding_amount], 0),
                )

            return branch

        branches = [make_branch(count) for count in range(1, per_half + 1)]
        query_part, key_part, value_part = lax.switch(inner_block, branches, 0)
        query_acc = lax.dynamic_update_slice_in_dim(query_acc, query_part, start_row, 0)
        key_running_sum = add_rows(key_running_sum, key_part, half_start)
        value_running_sum = add_rows(value_running_sum, value_part, half_start)
        return (query_acc, key_running_sum, value_running_sum)

    start_state = (
        jnp.zeros((tokens_per_row, heads_dev, HEAD_SIZE), jnp.float32),
        jnp.zeros((tokens_per_row, HEAD_SIZE), jnp.float32),
        jnp.zeros((tokens_per_row, HEAD_SIZE), jnp.float32),
    )
    query_acc, key_running_sum, value_running_sum = lax.fori_loop(
        0, block_count, block_step, start_state
    )
    query_rows = (
        inverse_rotary(query_acc, cosine_table, sine_line)
        .astype(jnp.bfloat16)
        .reshape(tokens_per_row, heads_dev * HEAD_SIZE)
    )
    query_grad = lax.all_to_all(query_rows, "sp", split_axis=0, concat_axis=1, tiled=True)
    key_rows = inverse_rotary(key_running_sum[:, None, :], cosine_table, sine_line)[:, 0, :]
    partial_sums = jnp.stack([key_rows, value_running_sum])
    returned_result = lax.all_to_all(
        partial_sums.astype(jnp.bfloat16), "sp", split_axis=1, concat_axis=2, tiled=True
    ).astype(partial_sums.dtype)
    summed = (
        returned_result.reshape(
            2, device_local_tokens, KEY_VALUE_HEADS, key_value_repeat, HEAD_SIZE
        )
        .sum(3)
        .reshape(2, device_local_tokens, KEY_VALUE_HEADS * HEAD_SIZE)
    )
    key_gradient = summed[0].astype(jnp.bfloat16)
    value_gradient = summed[1].astype(jnp.bfloat16)
    own_input = layer_input[0]
    kproj_grad = lax.psum_scatter(
        lax.dot_general(
            own_input, key_gradient, (((0,), (0,)), ((), ())), preferred_element_type=jnp.float32
        ),
        ("sp", "dp"),
        scatter_dimension=0,
        tiled=True,
    )
    return (query_grad[None], key_gradient[None], value_gradient[None], kproj_grad)


def solution(mesh):
    placed = (
        P("dp", "sp", None),
        P("dp", "sp", None),
        P("dp", "sp", None),
        P("dp", "sp", None),
        P("dp", "sp", None),
        P("dp", None),
        P("dp", None),
        P("dp", None),
    )
    return jax.shard_map(
        local,
        mesh=mesh,
        in_specs=placed,
        out_specs=(
            P("dp", "sp", None),
            P("dp", "sp", None),
            P("dp", "sp", None),
            P(("sp", "dp"), None),
        ),
        check_vma=False,
    )
```

profile of v0, /device:TPU:1, one launch (start us, length us, event | category | flops | bytes accessed | tf_op | source)
XLA Modules:
  0.0 2274.5 jit_solution(11390319846453047708)
XLA Ops:
  7.2 4.4 copy.130
  21.1 10.2 all-to-all-start
  38.6 42.4 %all-to-all-done = bf16[128,32,256]{0,2,1:T(8,128)(2,1)S(1)} async-done(((bf16[128,32,256]{0,2,1:T(8,128)(2,1)}), bf16[128,32,256]{0,2,1:T(8,128)(2,1)S(1)}, u32[]{:S(2)}, u32[]{:S(2)}) %all-to-all-start) | async-done | bytes 2097184 | tf_op jit(solution)/shard_map/all_to_all | solution.py:142
  81.0 5.8 all-to-all-start.1
  91.7 18.1 copy.137
  109.8 26.8 %all-to-all-done.1 = bf16[128,32,256]{0,2,1:T(8,128)(2,1)} async-done(((bf16[128,32,256]{0,2,1:T(8,128)(2,1)}), bf16[128,32,256]{0,2,1:T(8,128)(2,1)}, u32[]{:S(2)}, u32[]{:S(2)}) %all-to-all-start.1) | async-done | bytes 2097184 | tf_op jit(solution)/shard_map/all_to_all | solution.py:143
  136.6 5.3 all-to-all-start.2
  154.1 37.7 %all-to-all-done.2 = bf16[2,128,4096]{1,0,2:T(2,128)(2,1)} async-done(((bf16[2,128,4096]{1,0,2:T(2,128)(2,1)}), bf16[2,128,4096]{1,0,2:T(2,128)(2,1)}, u32[]{:S(2)}, u32[]{:S(2)}) %all-to-all-start.2) | async-done | bytes 2097184 | tf_op jit(solution)/shard_map/all_to_all | solution.py:155
  202.0 415.2 %while.21 = (s32[]{:T(128)}, f32[4096,2,128]{0,2,1:T(8,128)}, f32[4096,128]{0,1:T(8,128)}, f32[4096,128]{1,0:T(8,128)}, bf16[4096,2,128]{0,2,1:T(8,128)(2,1)}, /...) while((s32[]{:T(128)}, f32[4096,2,128]{0,2,1:T(8,128)}, ...), condition=%wide.region_17.18_spmd.clone.clone, body=%wide.region_0.17_spmd.clone.clone.sunk | while | flops 2731089920 | bytes 110193584 | solution.py:216
  226.4 19.0 conditional.4
  260.1 27.6 %conditional.4 = (f32[512,2,128]{0,2,1:T(8,128)}, f32[2048,128]{1,0:T(8,128)S(1)}, f32[2048,128]{1,0:T(8,128)S(1)}) conditional(s32[]{:T(128)} %clamp.13, (s32[]{:T(128)}, bf16[4096,128]{1,0:T(8,128)(2,1)}, s32[512]{0:T(512)S(1)}, s32[4096]{0:T(1024)S(1)}, s32[4096]{0:T(1024)S(1)}, /*index=5*/s32[512]{0:T(512)S(1)}, ...), branch_computations={%region_1.4_spmd, %region_5.8_spmd, %region_9.12_spmd, %region_13.... | conditional | flops 2730500096 | bytes 83966064 | solution.py:205
  268.7 8.4 fusion.58
  277.1 7.5 fusion.59
  302.3 40.6 %conditional.4 = (f32[512,2,128]{0,2,1:T(8,128)}, f32[2048,128]{1,0:T(8,128)S(1)}, f32[2048,128]{1,0:T(8,128)S(1)}) conditional(s32[]{:T(128)} %clamp.13, (s32[]{:T(128)}, bf16[4096,128]{1,0:T(8,128)(2,1)}, s32[512]{0:T(512)S(1)}, s32[4096]{0:T(1024)S(1)}, s32[4096]{0:T(1024)S(1)}, /*index=5*/s32[512]{0:T(512)S(1)}, ...), branch_computations={%region_1.4_spmd, %region_5.8_spmd, %region_9.12_spmd, %region_13.... | conditional | flops 2730500096 | bytes 83966064 | solution.py:205
  302.4 4.7 fusion.114
  308.9 5.2 fusion.231
  314.0 11.3 fusion.111
  325.3 10.1 fusion.107
  336.7 5.0 fusion.108
  357.5 46.5 %conditional.4 = (f32[512,2,128]{0,2,1:T(8,128)}, f32[2048,128]{1,0:T(8,128)S(1)}, f32[2048,128]{1,0:T(8,128)S(1)}) conditional(s32[]{:T(128)} %clamp.13, (s32[]{:T(128)}, bf16[4096,128]{1,0:T(8,128)(2,1)}, s32[512]{0:T(512)S(1)}, s32[4096]{0:T(1024)S(1)}, s32[4096]{0:T(1024)S(1)}, /*index=5*/s32[512]{0:T(512)S(1)}, ...), branch_computations={%region_1.4_spmd, %region_5.8_spmd, %region_9.12_spmd, %region_13.... | conditional | flops 2730500096 | bytes 83966064 | solution.py:205
  357.5 5.6 fusion.164
  365.2 7.7 fusion.234
  372.8 14.5 fusion.161
  387.3 11.9 fusion.157
  399.3 4.6 fusion.158
  418.5 19.0 conditional.4
  452.2 27.6 %conditional.4 = (f32[512,2,128]{0,2,1:T(8,128)}, f32[2048,128]{1,0:T(8,128)S(1)}, f32[2048,128]{1,0:T(8,128)S(1)}) conditional(s32[]{:T(128)} %clamp.13, (s32[]{:T(128)}, bf16[4096,128]{1,0:T(8,128)(2,1)}, s32[512]{0:T(512)S(1)}, s32[4096]{0:T(1024)S(1)}, s32[4096]{0:T(1024)S(1)}, /*index=5*/s32[512]{0:T(512)S(1)}, ...), branch_computations={%region_1.4_spmd, %region_5.8_spmd, %region_9.12_spmd, %region_13.... | conditional | flops 2730500096 | bytes 83966064 | solution.py:205
  460.8 8.4 fusion.58
  469.1 7.5 fusion.59
  494.4 40.6 %conditional.4 = (f32[512,2,128]{0,2,1:T(8,128)}, f32[2048,128]{1,0:T(8,128)S(1)}, f32[2048,128]{1,0:T(8,128)S(1)}) conditional(s32[]{:T(128)} %clamp.13, (s32[]{:T(128)}, bf16[4096,128]{1,0:T(8,128)(2,1)}, s32[512]{0:T(512)S(1)}, s32[4096]{0:T(1024)S(1)}, s32[4096]{0:T(1024)S(1)}, /*index=5*/s32[512]{0:T(512)S(1)}, ...), branch_computations={%region_1.4_spmd, %region_5.8_spmd, %region_9.12_spmd, %region_13.... | conditional | flops 2730500096 | bytes 83966064 | solution.py:205
  494.5 4.7 fusion.114
  501.0 5.2 fusion.231
  506.1 11.3 fusion.111
  517.4 10.1 fusion.107
  528.8 5.0 fusion.108
  549.6 46.5 %conditional.4 = (f32[512,2,128]{0,2,1:T(8,128)}, f32[2048,128]{1,0:T(8,128)S(1)}, f32[2048,128]{1,0:T(8,128)S(1)}) conditional(s32[]{:T(128)} %clamp.13, (s32[]{:T(128)}, bf16[4096,128]{1,0:T(8,128)(2,1)}, s32[512]{0:T(512)S(1)}, s32[4096]{0:T(1024)S(1)}, s32[4096]{0:T(1024)S(1)}, /*index=5*/s32[512]{0:T(512)S(1)}, ...), branch_computations={%region_1.4_spmd, %region_5.8_spmd, %region_9.12_spmd, %region_13.... | conditional | flops 2730500096 | bytes 83966064 | solution.py:205
  549.7 5.6 fusion.164
  557.3 7.7 fusion.234
  565.0 14.5 fusion.161
  579.5 11.9 fusion.157
  591.4 4.6 fusion.158
  619.5 4.2 fusion.208
  626.5 17.8 copy.147
  644.3 54.6 %all_to_all.63 = bf16[2,4096,128]{2,0,1:T(2,128)(2,1)S(1)} all-to-all(bf16[2,4096,128]{2,0,1:T(2,128)(2,1)S(1)} %copy.147), channel_id=1, replica_groups=mesh['sp'=32,'dp'=8] {'sp'}, dimensions={1} | all-to-all | bytes 4194304 | tf_op jit(solution)/shard_map/all_to_all | solution.py:227
  704.1 8.0 convolution_bitcast_fusion.3
  712.1 17.5 copy.171
  737.4 84.2 %all_to_all.64 = bf16[32,128,256]{2,1,0:T(8,128)(2,1)S(1)} all-to-all(bf16[32,128,256]{2,1,0:T(8,128)(2,1)} %copy.169), channel_id=1, replica_groups=mesh['sp'=32,'dp'=8] {'sp'}, dimensions={0} | all-to-all | bytes 4194304 | tf_op jit(solution)/shard_map/all_to_all | solution.py:224
  830.6 1436.8 %reduce-scatter.4.cloned.1.call-done = f32[16,1024]{1,0:T(8,128)} async-done(((f32[4096,1024]{1,0:T(8,128)}), f32[16,1024]{1,0:T(8,128)}) %reduce-scatter.4.cloned.1.call-update) | async-done | bytes 65552
  (295 shorter events, 261.1 us)
Async XLA Ops:
  7.2 696.9 %copy-start = (bf16[1,128,4096]{2,1,0:T(8,128)(2,1)S(1)}, bf16[1,128,4096]{2,1,0:T(8,128)(2,1)}, u32[]{:S(2)}) copy-start(bf16[1,128,4096]{2,1,0:T(8,128)(2,1)} %param.18) | copy-start | bytes 3145732
  7.2 4.4 copy-start.16
  7.2 4.4 copy-start.20
  7.2 8.8 copy-start.18
  11.7 0.6 copy-start.14
  16.0 5.1 copy-start.7
  16.0 5.1 copy-start.9
  21.1 14.3 copy-start.17
  21.1 59.9 %all-to-all-start = ((bf16[128,32,256]{0,2,1:T(8,128)(2,1)}), bf16[128,32,256]{0,2,1:T(8,128)(2,1)S(1)}, u32[]{:S(2)}, u32[]{:S(2)}) async-start(bf16[128,32,256]{0,2,1:T(8,128)(2,1)} %bitcast.343), calls=%async_computation | async-start | bytes 4194304 | tf_op jit(solution)/shard_map/all_to_all | solution.py:142
  81.0 55.5 %all-to-all-start.1 = ((bf16[128,32,256]{0,2,1:T(8,128)(2,1)}), bf16[128,32,256]{0,2,1:T(8,128)(2,1)}, u32[]{:S(2)}, u32[]{:S(2)}) async-start(bf16[128,32,256]{0,2,1:T(8,128)(2,1)} %broadcast_select_fusion), calls=%async_computation.1 | async-start | bytes 4194304 | tf_op jit(solution)/shard_map/all_to_all | solution.py:143
  136.6 55.2 %all-to-all-start.2 = ((bf16[2,128,4096]{1,0,2:T(2,128)(2,1)}), bf16[2,128,4096]{1,0,2:T(2,128)(2,1)}, u32[]{:S(2)}, u32[]{:S(2)}) async-start(bf16[2,128,4096]{1,0,2:T(2,128)(2,1)} %copy.137), calls=%async_computation.2 | async-start | bytes 4194304 | tf_op jit(solution)/shard_map/all_to_all | solution.py:155
  141.9 2125.6 %reduce-scatter.4.cloned.1.call-start = ((), (), s32[]{:S(2)}) async-start(), calls=%async_computation.6 | async-start | bytes 16842752
  202.0 417.1 %copy-start.15 = (f32[4096]{0:T(1024)S(1)}, f32[4096]{0:T(1024)}, u32[]{:S(2)}) copy-start(f32[4096]{0:T(1024)} %copy-done.14) | copy-start | bytes 49156
  202.0 417.1 %copy-start.19 = (f32[64]{0:T(128)S(1)}, f32[64]{0:T(128)}, u32[]{:S(2)}) copy-start(f32[64]{0:T(128)} %copy-done.18) | copy-start | bytes 772
  245.5 2.3 copy-start.1
  252.8 2.7 copy-start.2
  260.1 4.9 copy-start.4
  260.2 4.9 copy-start.12
  287.7 2.3 copy-start.1
  295.0 2.7 copy-start.2
  302.3 6.5 copy-start.5
  302.3 6.5 copy-start.13
  342.9 2.3 copy-start.1
  350.1 2.7 copy-start.2
  357.5 7.7 copy-start.6
  403.9 2.3 copy-start.1
  411.2 2.7 copy-start.2
  437.5 2.3 copy-start.1
  444.8 2.7 copy-start.2
  452.2 4.9 copy-start.4
  452.2 4.9 copy-start.12
  479.8 2.3 copy-start.1
  487.0 2.7 copy-start.2
  494.4 6.5 copy-start.5
  494.4 6.5 copy-start.13
  535.0 2.3 copy-start.1
  542.2 2.7 copy-start.2
  549.6 7.7 copy-start.6
  596.1 2.3 copy-start.1
  603.3 2.7 copy-start.2
  617.3 2.2 copy-start.3
  729.6 1.2 copy-start.8
  729.6 1.5 copy-start.10
  824.5 5.0 copy-start.11
Sparse Core Ops, SparseCore 0:
  729.8 1537.6 reduce-scatter.3
where the time goes:
time: 2280 us; the launch traced here: 2270 us
  waiting for transfers between devices  1540 us (68%)
  matrix products  253 us (11%)
  local copies, waits for them, and re-layouts  205 us (9%)
  blocking collectives  139 us (6%)
  other arithmetic  65.6 us (3%)
  loops' own time  32 us (1%)
    unnamed x2, waiting for transfers between devices  1440 us
    all_to_all x1, blocking collectives, local(): lax.all_to_all(query_rows, 'sp', split_axis=0, concat_axis=1, tiled=True)  84.2 us
    dot_general x8, matrix products, attend(): jnp.einsum('hij,jd->ihd', score_grad, key_block, preferred_element_type=j...  76.5 us
    dot_general x8, matrix products, attend(): jnp.einsum('hij,ihd->jd', score_grad, query_block, preferred_element_type...  66.9 us
    all_to_all x1, blocking collectives, local(): lax.all_to_all(partial_sums.astype(jnp.bfloat16), 'sp', split_axis=1, con...  54.6 us
  transfers between devices with their start and end apart: 4, of which 4 were waited for; matrix products, arithmetic and copies ran while one was open for 3% of the time, Pallas kernels for 0%

commit v1 on v0

v1 whole, which is shorter than its diff:
```python
import math

import jax
import jax.numpy as jnp
from jax import lax
from jax.experimental import pallas as pl
from jax.experimental.pallas import tpu as pltpu
from jax.sharding import PartitionSpec as P

HEADS = 64
KV_HEADS = 8
D = 128
HALF = D // 2
TOK = 128
SP = 32
PARTS = 2
REP = HEADS // KV_HEADS
CHUNK = 2 * TOK
CHUNKS = 8
STACK = 2
ROWS = STACK * CHUNK
SCALE = D ** (-0.5)
LOG2E = 1.4426950408889634
MIB = 1 << 20

HALF_GROUPS = [list(range(16)), list(range(16, 32))]
QUAD_GROUPS = [
    [h * 16 + xl * 8 + z * 2 + c for xl in range(2) for c in range(2)]
    for h in range(2)
    for z in range(4)
]
Y_GROUPS = [
    [(x * 8 + z * 2 + c) * 8 + y * 2 + zh for c in range(2) for y in range(4)]
    for x in range(4)
    for z in range(4)
    for zh in range(2)
]
PLANE_GROUPS = [
    [s * 8 + y * 2 + zh for s in range(SP) for zh in range(2)] for y in range(4)
]


def swap(array, axes, groups):
    return lax.all_to_all(
        array, axes, split_axis=0, concat_axis=0, axis_index_groups=groups, tiled=True
    )


def params(limit=48):
    return pltpu.CompilerParams(vmem_limit_bytes=limit * MIB)


def cost(flops, nbytes):
    return pl.CostEstimate(flops=flops, bytes_accessed=nbytes, transcendentals=0)


def dot(a, b, dims):
    return lax.dot_general(a, b, (dims, ((), ())), preferred_element_type=jnp.float32)


def turn(x, cos, sin):
    return x * cos + pltpu.roll(x, HALF, 1) * sin


def key_prep_kernel(k_ref, v_ref, cos_ref, sin_ref, *outs):
    cos, sin = cos_ref[...], sin_ref[...]
    for part in range(PARTS):
        cols = slice(part * D, (part + 1) * D)
        k = turn(k_ref[:, cols].astype(jnp.float32), cos, sin).astype(jnp.bfloat16)
        v = v_ref[:, cols]
        for z in range(4):
            outs[part][0, z, 0, 0] = k
            outs[part][0, z, 0, 1] = v


def key_prep(k, v, cos, sin):
    table = pl.BlockSpec((TOK, D), lambda j: (0, 0))
    column = pl.BlockSpec((TOK, PARTS * D), lambda j: (0, j))
    shape = jax.ShapeDtypeStruct((2, 4, 2, 2, TOK, D), jnp.bfloat16)
    return pl.pallas_call(
        key_prep_kernel,
        grid=(4,),
        in_specs=[column, column, table, table],
        out_specs=[
            pl.BlockSpec((1, 4, 1, 2, TOK, D), lambda j: (j // 2, 0, j % 2, 0, 0, 0))
        ]
        * PARTS,
        out_shape=[shape] * PARTS,
        compiler_params=params(),
        cost_estimate=cost(1 << 20, 3 * MIB),
        name="key_prep",
    )(k, v, cos, sin)


def query_prep_kernel(q_ref, g_ref, cos_ref, sin_ref, valid_ref, *outs):
    cos, sin = cos_ref[...], sin_ref[...]
    keep = valid_ref[...] > 0.0
    for part in range(PARTS):
        for h in range(REP):
            cols = slice((part * REP + h) * D, (part * REP + h + 1) * D)
            q = turn(q_ref[:, cols].astype(jnp.float32), cos, sin)
            outs[part][0, 0, :, h * D : (h + 1) * D] = q.astype(jnp.bfloat16)
            g = jnp.where(keep, g_ref[:, cols].astype(jnp.float32), 0.0)
            outs[part][0, 1, :, h * D : (h + 1) * D] = g.astype(jnp.bfloat16)


def query_prep(q, g, cos, sin, valid):
    table = pl.BlockSpec((TOK, D), lambda j: (0, 0))
    column = pl.BlockSpec((TOK, PARTS * REP * D), lambda j: (0, j))
    shape = jax.ShapeDtypeStruct((4, 2, TOK, REP * D), jnp.bfloat16)
    return pl.pallas_call(
        query_prep_kernel,
        grid=(4,),
        in_specs=[column, column, table, table, table],
        out_specs=[pl.BlockSpec((1, 2, TOK, REP * D), lambda j: (j, 0, 0, 0))] * PARTS,
        out_shape=[shape] * PARTS,
        compiler_params=params(),
        cost_estimate=cost(8 << 20, 8 * MIB),
        name="query_prep",
    )(q, g, cos, sin, valid)


def input_prep_kernel(x_ref, out_ref):
    for s in range(4):
        xt = x_ref[:, s * TOK : (s + 1) * TOK].T
        for y in range(4):
            piece = xt[y * 32 : (y + 1) * 32]
            out_ref[0, y, s] = piece
            out_ref[1, y, s] = piece


def input_prep(x):
    return pl.pallas_call(
        input_prep_kernel,
        grid=(8,),
        in_specs=[pl.BlockSpec((TOK, 512), lambda i: (0, i))],
        out_specs=pl.BlockSpec((2, 4, 4, 32, TOK), lambda i: (0, 0, i, 0, 0)),
        out_shape=jax.ShapeDtypeStruct((2, 4, SP, 32, TOK), jnp.bfloat16),
        compiler_params=params(),
        cost_estimate=cost(1 << 20, 3 * MIB),
        name="input_prep",
    )(x)


def attention_kernel(
    meta_ref,
    qg_ref,
    kv_ref,
    cos_ref,
    sin_ref,
    dq_ref,
    dkv_ref,
    kt_ref,
    s_ref,
    dp_ref,
    dk_ref,
    dv_ref,
    dqt_ref,
):
    block, heads = pl.program_id(0), pl.program_id(1)
    low, diagonal, count = meta_ref[block, 0], meta_ref[block, 1], meta_ref[block, 2]

    def keys(p, which):
        return kv_ref[pl.ds(2 * p, 2), which].reshape(CHUNK, D)

    @pl.when((block == 0) & (heads == 0))
    def _():
        dk_ref[...] = jnp.zeros_like(dk_ref)
        dv_ref[...] = jnp.zeros_like(dv_ref)
        for p in range(CHUNKS):
            kt_ref[p] = keys(p, 0).T

    def stacked(which):
        return jnp.concatenate(
            [
                qg_ref[0, :, which, :, h * D : (h + 1) * D].reshape(CHUNK, D)
                for h in range(STACK)
            ],
            axis=0,
        )

    @pl.when(count <= 0)
    def _():
        dq_ref[...] = jnp.zeros_like(dq_ref)

    @pl.when(count > 0)
    def _():
        q, g = stacked(0), stacked(1)
        nt = ((1,), (1,))
        nn = ((1,), (0,))

        def score(p, peak):
            s = dot(keys(p, 0), q, nt)
            s_ref[p] = s
            dp_ref[p] = dot(keys(p, 1), g, nt)
            return jnp.maximum(peak, jnp.max(s, axis=0, keepdims=True))

        peak = lax.fori_loop(low, diagonal, score, jnp.full((1, ROWS), -1e30, jnp.float32))
        key_at = lax.broadcasted_iota(jnp.int32, (CHUNK, ROWS), 0)
        row_at = lax.broadcasted_iota(jnp.int32, (CHUNK, ROWS), 1) & (CHUNK - 1)
        allowed = (key_at <= row_at) & (key_at < count)
        s = jnp.where(allowed, dot(keys(diagonal, 0), q, nt), -1e30)
        s_ref[diagonal] = s
        dp_ref[diagonal] = dot(keys(diagonal, 1), g, nt)
        peak = jnp.maximum(peak, jnp.max(s, axis=0, keepdims=True))

        def weigh(p, sums):
            total, mixed = sums
            e = jnp.exp2((s_ref[p] - peak) * (SCALE * LOG2E))
            s_ref[p] = e
            return (
                total + jnp.sum(e, axis=0, keepdims=True),
                mixed + jnp.sum(e * dp_ref[p], axis=0, keepdims=True),
            )

        zero = jnp.zeros((1, ROWS), jnp.float32)
        total, mixed = lax.fori_loop(low, diagonal + 1, weigh, (zero, zero))
        inverse = 1.0 / total
        row_dot = mixed * inverse
        dqt_ref[...] = jnp.zeros_like(dqt_ref)

        def spread(p, carry):
            weights = s_ref[p] * inverse
            ds = (weights * (dp_ref[p] - row_dot)).astype(jnp.bfloat16)
            dv_ref[p] += dot(weights.astype(jnp.bfloat16), g, nn)
            dk_ref[p] += dot(ds, q, nn)
            dqt_ref[...] += dot(kt_ref[p], ds, nn)
            return carry

        lax.fori_loop(low, diagonal + 1, spread, 0)
        cos, sin = cos_ref[0], sin_ref[0]
        for h in range(STACK):
            cols = slice(h * CHUNK, (h + 1) * CHUNK)
            x1 = dqt_ref[:HALF, cols] * SCALE
            x2 = dqt_ref[HALF:, cols] * SCALE
            y = jnp.concatenate([x1 * cos + x2 * sin, x2 * cos - x1 * sin], axis=0)
            dq_ref[0, :, :, h * D : (h + 1) * D] = y.T.astype(jnp.bfloat16).reshape(2, TOK, D)

    @pl.when((block == 1) & (heads == REP // STACK - 1))
    def _():
        for p in range(CHUNKS):
            dk = (dk_ref[p] * SCALE).astype(jnp.bfloat16)
            dkv_ref[2 * p : 2 * p + 2, 0] = dk.reshape(2, TOK, D)
            dkv_ref[2 * p : 2 * p + 2, 1] = dv_ref[p].astype(jnp.bfloat16).reshape(2, TOK, D)


def attention(meta, qg, kv, cos, sin):
    width = STACK * D
    table = pl.BlockSpec((1, HALF, CHUNK), lambda b, h: (b, 0, 0))
    whole = pl.BlockSpec((16, 2, TOK, D), lambda b, h: (0, 0, 0, 0))
    return pl.pallas_call(
        attention_kernel,
        grid=(2, REP // STACK),
        in_specs=[
            pl.BlockSpec(memory_space=pltpu.SMEM),
            pl.BlockSpec((1, 2, 2, TOK, width), lambda b, h: (b, 0, 0, 0, h)),
            whole,
            table,
            table,
        ],
        out_specs=[
            pl.BlockSpec((1, 2, TOK, width), lambda b, h: (b, 0, 0, h)),
            whole,
        ],
        out_shape=[
            jax.ShapeDtypeStruct((2, 2, TOK, REP * D), jnp.bfloat16),
            jax.ShapeDtypeStruct((16, 2, TOK, D), jnp.bfloat16),
        ],
        scratch_shapes=[
            pltpu.VMEM((CHUNKS, D, CHUNK), jnp.bfloat16),
            pltpu.VMEM((CHUNKS, CHUNK, ROWS), jnp.float32),
            pltpu.VMEM((CHUNKS, CHUNK, ROWS), jnp.float32),
            pltpu.VMEM((CHUNKS, CHUNK, D), jnp.float32),
            pltpu.VMEM((CHUNKS, CHUNK, D), jnp.float32),
            pltpu.VMEM((D, ROWS), jnp.float32),
        ],
        compiler_params=params(),
        cost_estimate=cost(25 * 10**9, 6 * MIB),
        name="attention",
    )(meta, qg.reshape(2, 2, 2, TOK, REP * D), kv, cos, sin)


def key_post_kernel(a_ref, b_ref, cos_ref, sin_ref, dk_ref, dv_ref, kg_ref):
    cos, sin = cos_ref[...], sin_ref[...]
    for part, ref in enumerate((a_ref, b_ref)):
        cols = slice(part * D, (part + 1) * D)
        dk = ref[0, 0, 0, 0].astype(jnp.float32)
        dv = ref[0, 0, 0, 1].astype(jnp.float32)
        for z in range(1, 4):
            dk += ref[0, z, 0, 0].astype(jnp.float32)
            dv += ref[0, z, 0, 1].astype(jnp.float32)
        dk = turn(dk, cos, -sin).astype(jnp.bfloat16)
        dk_ref[:, cols] = dk
        dv_ref[:, cols] = dv.astype(jnp.bfloat16)
        for y in range(4):
            kg_ref[0, y, :, cols] = dk


def key_post(a, b, cos, sin):
    shape = (2, 4, 2, 2, TOK, D)
    table = pl.BlockSpec((TOK, D), lambda j: (0, 0))
    column = pl.BlockSpec((TOK, PARTS * D), lambda j: (0, j))
    source = pl.BlockSpec((1, 4, 1, 2, TOK, D), lambda j: (j // 2, 0, j % 2, 0, 0, 0))
    full = jax.ShapeDtypeStruct((TOK, KV_HEADS * D), jnp.bfloat16)
    return pl.pallas_call(
        key_post_kernel,
        grid=(4,),
        in_specs=[source, source, table, table],
        out_specs=[
            column,
            column,
            pl.BlockSpec((1, 4, TOK, PARTS * D), lambda j: (j // 2, 0, 0, j % 2)),
        ],
        out_shape=[full, full, jax.ShapeDtypeStruct((2, 4, TOK, 512), jnp.bfloat16)],
        compiler_params=params(),
        cost_estimate=cost(2 << 20, 4 * MIB),
        name="key_post",
    )(a.reshape(shape), b.reshape(shape), cos, sin)


def query_post_kernel(a_ref, b_ref, out_ref):
    out_ref[:, : REP * D] = a_ref[0]
    out_ref[:, REP * D :] = b_ref[0]


def query_post(a, b):
    source = pl.BlockSpec((1, TOK, REP * D), lambda j: (j, 0, 0))
    return pl.pallas_call(
        query_post_kernel,
        grid=(4,),
        in_specs=[source, source],
        out_specs=pl.BlockSpec((TOK, PARTS * REP * D), lambda j: (0, j)),
        out_shape=jax.ShapeDtypeStruct((TOK, HEADS * D), jnp.bfloat16),
        compiler_params=params(),
        cost_estimate=cost(1 << 20, 4 * MIB),
        name="query_post",
    )(a, b)


def project_kernel(x_ref, kg_ref, out_ref):
    nn = ((1,), (0,))
    total = dot(x_ref[0], kg_ref[0], nn)
    for i in range(1, 8):
        total += dot(x_ref[i], kg_ref[i], nn)
    out_ref[...] = total.astype(jnp.bfloat16)


def project(xt, kg):
    return pl.pallas_call(
        project_kernel,
        grid=(4,),
        in_specs=[
            pl.BlockSpec((8, 256, TOK), lambda i: (0, i, 0)),
            pl.BlockSpec((8, TOK, 512), lambda i: (0, 0, 0)),
        ],
        out_specs=pl.BlockSpec((256, 512), lambda i: (i, 0)),
        out_shape=jax.ShapeDtypeStruct((1024, 512), jnp.bfloat16),
        compiler_params=params(),
        cost_estimate=cost(10**9, 4 * MIB),
        name="project",
    )(xt, kg)


def final_sum_kernel(x_ref, out_ref):
    for c in range(2):
        total = jnp.zeros((16, 512), jnp.float32)
        for s in range(16):
            for zh in range(2):
                total += x_ref[s, c, zh].astype(jnp.float32)
        out_ref[:, c * 512 : (c + 1) * 512] = total


def final_sum(x):
    return pl.pallas_call(
        final_sum_kernel,
        in_specs=[pl.BlockSpec(memory_space=pltpu.VMEM)],
        out_specs=pl.BlockSpec(memory_space=pltpu.VMEM),
        out_shape=jax.ShapeDtypeStruct((16, 1024), jnp.float32),
        compiler_params=params(),
        cost_estimate=cost(1 << 20, MIB),
        name="final_sum",
    )(x)


def local(q, k, v, g, x, group_first, seq_length, pos_offset):
    me = lax.axis_index("sp")
    first, length, offset = group_first[0], seq_length[0], pos_offset[0]
    rates = jnp.exp(jnp.arange(HALF, dtype=jnp.float32) * (-2.0 * math.log(10000.0) / D))
    token = jnp.arange(TOK, dtype=jnp.int32)

    own = (me - first[me]) * TOK + token
    phase = (offset[me] + own).astype(jnp.float32)[:, None] * rates[None, :]
    cos, sin = jnp.cos(phase), jnp.sin(phase)
    cos = jnp.concatenate([cos, cos], -1)
    sin = jnp.concatenate([-sin, sin], -1)
    valid = jnp.broadcast_to((own < length[me]).astype(jnp.float32)[:, None], (TOK, D))

    half = me // 16
    z = me % 8 // 2
    device = half * 16 + jnp.arange(2, dtype=jnp.int32) * 8 + z * 2
    start = first[device]
    before = (device - start) * TOK
    meta = jnp.stack(
        [
            (start - half * 16) // 2,
            (device - half * 16) // 2,
            jnp.clip(length[device] - before, 0, CHUNK),
        ],
        axis=1,
    )
    place = (offset[device] + before)[:, None] + jnp.arange(CHUNK, dtype=jnp.int32)[None, :]
    turned = place.astype(jnp.float32)[:, None, :] * rates[None, :, None]
    cos_t, sin_t = jnp.cos(turned), jnp.sin(turned)

    kv_out = key_prep(k[0], v[0], cos, sin)
    qg_out = query_prep(q[0], g[0], cos, sin, valid)
    xt_out = input_prep(x[0]).reshape(8, 1024, TOK)

    dq_back, dkv_back = [], []
    arrived = []
    for part in range(PARTS):
        kv = swap(kv_out[part].reshape(16, 2, TOK, D), "sp", HALF_GROUPS)
        qg = swap(qg_out[part], "sp", QUAD_GROUPS)
        arrived.append((qg, kv))
    xt = swap(xt_out, ("sp", "dp"), Y_GROUPS)
    for qg, kv in arrived:
        dq, dkv = attention(meta, qg, kv, cos_t, sin_t)
        dkv_back.append(swap(dkv, "sp", HALF_GROUPS))
        dq_back.append(swap(dq.reshape(4, TOK, REP * D), "sp", QUAD_GROUPS))

    key_gradient, value_gradient, kg = key_post(*dkv_back, cos, sin)
    kg = swap(kg.reshape(8, TOK, 512), ("sp", "dp"), Y_GROUPS)
    partial = project(xt, kg)
    pieces = swap(partial.reshape(64, 16, 512), ("sp", "dp"), PLANE_GROUPS)
    kproj_grad = final_sum(pieces.reshape(16, 2, 2, 16, 512))
    query_grad = query_post(*dq_back)
    return (query_grad[None], key_gradient[None], value_gradient[None], kproj_grad)


def solution(mesh):
    tokens = P("dp", "sp", None)
    table = P("dp", None)
    return jax.shard_map(
        local,
        mesh=mesh,
        in_specs=(tokens,) * 5 + (table,) * 3,
        out_specs=(tokens, tokens, tokens, P(("sp", "dp"), None)),
        check_vma=False,
    )
```

time: 2280 us -> 353 us (0.15)
  waiting for transfers between devices: 1540 us -> 113 us
  matrix products: 253 us -> 0 us
  local copies, waits for them, and re-layouts: 205 us -> 17.3 us
  other arithmetic: 65.6 us -> 2.63 us
  Pallas kernels: 0 us -> 59.7 us
  blocking collectives: 139 us -> 99.6 us
  starting transfers between devices: 21.3 us -> 57.9 us
  loops' own time: 32 us -> 0 us
    unnamed x2 -> x0, waiting for transfers between devices: 1440 us -> none
    dot_general x33 -> x0, matrix products: 213 us -> none  [the longest x8 76.5 us: attend(): jnp.einsum('hij,jd->ihd', score_grad, key_block, preferred_element_type=j...]
    pallas_call x0 -> x9, Pallas kernels: none -> 59.7 us  [the longest x2 42.7 us: attention(): pl.pallas_call(attention_kernel, grid=(2, REP // STACK), in_specs=[pl.Blo...]
    dynamic_slice x80 -> x2, local copies, waits for them, and re-layouts: 50.5 us -> 1.85 us  [the longest x1 1.26 us: local(): length[me]]
    another operation x5 -> x0, local copies, waits for them, and re-layouts: 40.1 us -> none  [the longest x1 18.1 us: local(): jnp.stack([key_wide, value_wide])]
    dynamic_update_slice x24 -> x0, local copies, waits for them, and re-layouts: 40 us -> none  [the longest x16 21.5 us: add_rows(): return lax.dynamic_update_slice_in_dim(accum, current + part, start_row, 0)]
    sub x8 -> x0, matrix products: 39.9 us -> none  [attend(): weights = jnp.exp(scores - row_peak)]
    all_to_all x2 -> x3, blocking collectives: 139 us -> 99.6 us  [swap(): lax.all_to_all(array, axes, split_axis=0, concat_axis=0, axis_index_group...]
  transfers between devices with their start and end apart: 4 -> 8, of which waited for: 4 -> 8; matrix products, arithmetic and copies ran while one was open for 3% -> 1% of each run, Pallas kernels for 0% -> 15%
where the time goes in v1:
time: 353 us; the launch traced here: 351 us
  waiting for transfers between devices  113 us (32%)
  blocking collectives  99.6 us (28%)
  Pallas kernels  59.7 us (17%)
  starting transfers between devices  57.9 us (16%)
  local copies, waits for them, and re-layouts  17.3 us (5%)
    all_to_all x8, waiting for transfers between devices, swap(): lax.all_to_all(array, axes, split_axis=0, concat_axis=0, axis_index_group...  113 us
    all_to_all x3, blocking collectives, swap(): lax.all_to_all(array, axes, split_axis=0, concat_axis=0, axis_index_group...  99.6 us
    all_to_all x8, starting transfers between devices, swap(): lax.all_to_all(array, axes, split_axis=0, concat_axis=0, axis_index_group...  57.9 us
    pallas_call x2, Pallas kernels, attention(): pl.pallas_call(attention_kernel, grid=(2, REP // STACK), in_specs=[pl.Blo...  42.7 us
    unnamed x38, local copies, waits for them, and re-layouts  13.2 us
  transfers between devices with their start and end apart: 8, of which 8 were waited for; matrix products, arithmetic and copies ran while one was open for 1% of the time, Pallas kernels for 15%

profile of v1, /device:TPU:1, one launch (start us, length us, event | category | flops | bytes accessed | tf_op | source)
XLA Modules:
  0.0 351.1 jit_solution(13503498458045382490)
XLA Ops:
  0.7 1.3 constant_dynamic-slice_fusion
  2.6 0.6 constant_dynamic-slice_fusion.2
  3.2 0.6 add_convert_fusion.1
  4.2 0.7 compare_convert_fusion
  5.1 4.8 %query_prep.1 = (bf16[4,2,128,1024]{3,2,1,0:T(8,128)(2,1)}, bf16[4,2,128,1024]{3,2,1,0:T(8,128)(2,1)S(1)}) custom-call(bf16[128,8192]{1,0:T(8,128)(2,1)} %bitcast.44, bf16[128,8192]{1,0:T(8,128)(2,1)} %bitcast.45, f32[128,128]{1,0:T(8,128)S(1)} %pad_maximum_fusion.cos_ref, f32[128,128]{1,0:T(8,128)S(1)} %pad_maximum_fusion.1.sin_ref, ...), custom_call_target="tpu_custom_call" | custom-call | flops 8388608 | bytes 8388608 | tf_op jit(solution)/shard_map/query_prep/pallas_call | solution.py:111
  9.9 31.1 %all_to_all.55 = bf16[4,2,128,1024]{3,2,1,0:T(8,128)(2,1)} all-to-all(bf16[4,2,128,1024]{3,2,1,0:T(8,128)(2,1)S(1)} %get-tuple-element.18), channel_id=1, replica_groups={{0,8,64,72},{16,24,80,88},{32,40,96,104},{48,56,112,120},{128,136,192,2..., dimensions={0} | all-to-all | bytes 4194304 | tf_op jit(solution)/shard_map/all_to_all | solution.py:44
  41.0 5.6 %all-to-all-start = ((bf16[4,2,128,1024]{3,2,1,0:T(8,128)(2,1)}), bf16[4,2,128,1024]{3,2,1,0:T(8,128)(2,1)}, u32[]{:S(2)}, u32[]{:S(2)}) async-start(bf16[4,2,128,1024]{3,2,1,0:T(8,128)(2,1)} %get-tuple-element.15), calls=%async_computation | async-start | bytes 4194304 | tf_op jit(solution)/shard_map/all_to_all | solution.py:44
  46.6 1.1 input_prep.1
  47.7 1.4 copy-done.1
  49.0 22.5 %all-to-all-done = bf16[4,2,128,1024]{3,2,1,0:T(8,128)(2,1)} async-done(((bf16[4,2,128,1024]{3,2,1,0:T(8,128)(2,1)}), bf16[4,2,128,1024]{3,2,1,0:T(8,128)(2,1)}, u32[]{:S(2)}, u32[]{:S(2)}) %all-to-all-start) | async-done | bytes 2097184 | tf_op jit(solution)/shard_map/all_to_all | solution.py:44
  71.5 4.5 %all-to-all-start.8 = ((bf16[8,1024,128]{2,1,0:T(8,128)(2,1)}), bf16[8,1024,128]{2,1,0:T(8,128)(2,1)S(1)}, u32[]{:S(2)}, u32[]{:S(2)}) async-start(bf16[8,1024,128]{2,1,0:T(8,128)(2,1)} %bitcast.29), calls=%async_computation.8 | async-start | bytes 4194304 | tf_op jit(solution)/shard_map/all_to_all | solution.py:44
  76.1 1.9 key_prep.1
  78.0 1.0 copy-done.9
  79.0 23.3 %all-to-all-done.8.x_ref = bf16[8,1024,128]{2,1,0:T(8,128)(2,1)S(1)} async-done(((bf16[8,1024,128]{2,1,0:T(8,128)(2,1)}), bf16[8,1024,128]{2,1,0:T(8,128)(2,1)S(1)}, u32[]{:S(2)}, u32[]{:S(2)}) %all-to-all-start.8) | async-done | bytes 2097184 | tf_op jit(solution)/shard_map/all_to_all | solution.py:44
  102.3 5.5 %all-to-all-start.4 = ((bf16[16,2,128,128]{3,2,1,0:T(8,128)(2,1)}), bf16[16,2,128,128]{3,2,1,0:T(8,128)(2,1)S(1)}, u32[]{:S(2)}, u32[]{:S(2)}) async-start(bf16[16,2,128,128]{3,2,1,0:T(8,128)(2,1)} %bitcast.36), calls=%async_computation.4 | async-start | bytes 2097152 | tf_op jit(solution)/shard_map/all_to_all | solution.py:44
  107.9 0.6 gather_fusion
  108.5 0.6 gather_fusion.2
  109.2 0.6 gather_fusion.1
  110.2 0.5 multiply_sine_fusion
  110.7 22.0 %all-to-all-done.4.kv_ref = bf16[16,2,128,128]{3,2,1,0:T(8,128)(2,1)S(1)} async-done(((bf16[16,2,128,128]{3,2,1,0:T(8,128)(2,1)}), bf16[16,2,128,128]{3,2,1,0:T(8,128)(2,1)S(1)}, u32[]{:S(2)}, u32[]{:S(2)}) %all-to-all-start.4) | async-done | bytes 1048608 | tf_op jit(solution)/shard_map/all_to_all | solution.py:44
  132.7 4.4 %all-to-all-start.1 = ((bf16[16,2,128,128]{3,2,1,0:T(8,128)(2,1)}), bf16[16,2,128,128]{3,2,1,0:T(8,128)(2,1)}, u32[]{:S(2)}, u32[]{:S(2)}) async-start(bf16[16,2,128,128]{3,2,1,0:T(8,128)(2,1)} %bitcast.12), calls=%async_computation.1 | async-start | bytes 2097152 | tf_op jit(solution)/shard_map/all_to_all | solution.py:44
  137.1 1.6 copy-done.7
  138.7 21.1 %attention.3 = (bf16[2,2,128,1024]{3,2,1,0:T(8,128)(2,1)S(1)}, bf16[16,2,128,128]{3,2,1,0:T(8,128)(2,1)S(1)}) custom-call(s32[2,3]{1,0:T(2,128)S(1)} %pad_add_fusion.meta_ref, bf16[2,2,2,128,1024]{4,3,2,1,0:T(8,128)(2,1)S(1)} %bitcast.34, bf16[16,2,128,128]{3,2,1,0:T(8,128)(2,1)S(1)} %all-to-all-done.4.kv_ref, f32[2,64,256]{2,1,0:T(8,128)S(1)} %get-tuple-element.27.cos_ref, ...), custom_call_target="tpu_custom_call" | custom-call | flops 24999999488 | bytes 6291456 | tf_op jit(solution)/shard_map/attention/pallas_call | solution.py:251
  159.8 1.0 copy-done.11
  160.8 1.0 copy-done.12
  161.8 0.4 all-to-all-done.1.kv_ref
  162.2 23.6 %all-to-all-start.7 = ((bf16[16,2,128,128]{3,2,1,0:T(8,128)(2,1)}), bf16[16,2,128,128]{3,2,1,0:T(8,128)(2,1)S(1)}, u32[]{:S(2)}, u32[]{:S(2)}) async-start(bf16[16,2,128,128]{3,2,1,0:T(8,128)(2,1)} %copy-done.12), calls=%async_computation.7 | async-start | bytes 2097152 | tf_op jit(solution)/shard_map/all_to_all | solution.py:44
  185.8 21.7 %attention.2 = (bf16[2,2,128,1024]{3,2,1,0:T(8,128)(2,1)S(1)}, bf16[16,2,128,128]{3,2,1,0:T(8,128)(2,1)S(1)}) custom-call(s32[2,3]{1,0:T(2,128)S(1)} %pad_add_fusion.meta_ref, bf16[2,2,2,128,1024]{4,3,2,1,0:T(8,128)(2,1)} %bitcast.9.qg_ref, bf16[16,2,128,128]{3,2,1,0:T(8,128)(2,1)} %all-to-all-done.1.kv_ref, f32[2,64,256]{2,1,0:T(8,128)S(1)} %get-tuple-element.27.cos_ref, ...), custom_call_target="tpu_custom_call" | custom-call | flops 24999999488 | bytes 6291456 | tf_op jit(solution)/shard_map/attention/pallas_call | solution.py:251
  207.5 1.0 copy-done.10
  208.5 1.0 copy-done.13
  209.5 1.3 all-to-all-done.7
  210.8 48.4 %all_to_all.56 = bf16[16,2,128,128]{3,2,1,0:T(8,128)(2,1)} all-to-all(bf16[16,2,128,128]{3,2,1,0:T(8,128)(2,1)} %copy-done.13), channel_id=1, replica_groups={{0,8,16,24,32,40,48,56,64,72,80,88,96,104,112,120},{128,136,144,152,160..., dimensions={0} | all-to-all | bytes 2097152 | tf_op jit(solution)/shard_map/all_to_all | solution.py:44
  259.2 4.2 %all-to-all-start.5 = ((bf16[4,128,1024]{2,1,0:T(8,128)(2,1)}), bf16[4,128,1024]{2,1,0:T(8,128)(2,1)}, u32[]{:S(2)}, u32[]{:S(2)}) async-start(bf16[4,128,1024]{2,1,0:T(8,128)(2,1)} %bitcast.38), calls=%async_computation.5 | async-start | bytes 2097152 | tf_op jit(solution)/shard_map/all_to_all | solution.py:44
  263.5 1.2 copy-done.2
  264.7 1.9 key_post.1
  266.5 1.0 copy-done.14
  267.5 9.5 %all-to-all-done.5.b_ref = bf16[4,128,1024]{2,1,0:T(8,128)(2,1)} async-done(((bf16[4,128,1024]{2,1,0:T(8,128)(2,1)}), bf16[4,128,1024]{2,1,0:T(8,128)(2,1)}, u32[]{:S(2)}, u32[]{:S(2)}) %all-to-all-start.5) | async-done | bytes 1048608 | tf_op jit(solution)/shard_map/all_to_all | solution.py:44
  277.0 20.1 %all_to_all.57.kg_ref = bf16[8,128,512]{2,1,0:T(8,128)(2,1)} all-to-all(bf16[8,128,512]{2,1,0:T(8,128)(2,1)} %bitcast.39), channel_id=1, replica_groups={{0,2,4,6,8,10,12,14},{1,3,5,7,9,11,13,15},{16,18,20,22,24,26,28,30},{17..., dimensions={0} | all-to-all | bytes 2097152 | tf_op jit(solution)/shard_map/all_to_all | solution.py:44
  297.1 3.9 %all-to-all-start.2 = ((bf16[4,128,1024]{2,1,0:T(8,128)(2,1)}), bf16[4,128,1024]{2,1,0:T(8,128)(2,1)S(1)}, u32[]{:S(2)}, u32[]{:S(2)}) async-start(bf16[4,128,1024]{2,1,0:T(8,128)(2,1)} %bitcast.37), calls=%async_computation.2 | async-start | bytes 2097152 | tf_op jit(solution)/shard_map/all_to_all | solution.py:44
  300.9 1.2 copy-done.6
  302.1 2.9 project.1
  305.1 1.0 copy-done.5
  306.0 8.5 %all-to-all-done.2.a_ref = bf16[4,128,1024]{2,1,0:T(8,128)(2,1)S(1)} async-done(((bf16[4,128,1024]{2,1,0:T(8,128)(2,1)}), bf16[4,128,1024]{2,1,0:T(8,128)(2,1)S(1)}, u32[]{:S(2)}, u32[]{:S(2)}) %all-to-all-start.2) | async-done | bytes 1048608 | tf_op jit(solution)/shard_map/all_to_all | solution.py:44
  314.5 1.0 copy-done.3
  315.5 6.2 %all-to-all-start.10 = ((bf16[64,16,512]{2,1,0:T(8,128)(2,1)}), bf16[64,16,512]{2,1,0:T(8,128)(2,1)S(1)}, u32[]{:S(2)}, u32[]{:S(2)}) async-start(bf16[64,16,512]{2,1,0:T(8,128)(2,1)} %bitcast.33), calls=%async_computation.10 | async-start | bytes 2097152 | tf_op jit(solution)/shard_map/all_to_all | solution.py:44
  321.7 3.6 %query_post.1 = bf16[128,8192]{1,0:T(8,128)(2,1)} custom-call(bf16[4,128,1024]{2,1,0:T(8,128)(2,1)S(1)} %copy-done.4, bf16[4,128,1024]{2,1,0:T(8,128)(2,1)} %all-to-all-done.5.b_ref), custom_call_target="tpu_custom_call" | custom-call | flops 1048576 | bytes 4194304 | tf_op jit(solution)/shard_map/query_post/pallas_call | solution.py:328
  325.3 25.0 %all-to-all-done.10 = bf16[64,16,512]{2,1,0:T(8,128)(2,1)S(1)} async-done(((bf16[64,16,512]{2,1,0:T(8,128)(2,1)}), bf16[64,16,512]{2,1,0:T(8,128)(2,1)S(1)}, u32[]{:S(2)}, u32[]{:S(2)}) %all-to-all-start.10) | async-done | bytes 1048608 | tf_op jit(solution)/shard_map/all_to_all | solution.py:44
  350.4 0.8 final_sum.1
  (40 shorter events, 1.1 us)
Async XLA Ops:
  0.6 2.0 copy-start
  41.0 5.6 %copy-start.8 = (bf16[1,128,4096]{2,1,0:T(8,128)(2,1)S(1)}, bf16[1,128,4096]{2,1,0:T(8,128)(2,1)}, u32[]{:S(2)}) copy-start(bf16[1,128,4096]{2,1,0:T(8,128)(2,1)} %param.12) | copy-start | bytes 3145732
  41.0 30.5 %all-to-all-start = ((bf16[4,2,128,1024]{3,2,1,0:T(8,128)(2,1)}), bf16[4,2,128,1024]{3,2,1,0:T(8,128)(2,1)}, u32[]{:S(2)}, u32[]{:S(2)}) async-start(bf16[4,2,128,1024]{3,2,1,0:T(8,128)(2,1)} %get-tuple-element.15), calls=%async_computation | async-start | bytes 4194304 | tf_op jit(solution)/shard_map/all_to_all | solution.py:44
  47.7 1.4 copy-start.1
  71.5 4.5 %copy-start.15 = (bf16[1,128,1024]{2,1,0:T(8,128)(2,1)S(1)}, bf16[1,128,1024]{2,1,0:T(8,128)(2,1)}, u32[]{:S(2)}) copy-start(bf16[1,128,1024]{2,1,0:T(8,128)(2,1)} %param.9) | copy-start | bytes 786436
  71.5 4.5 %copy-start.16 = (bf16[1,128,1024]{2,1,0:T(8,128)(2,1)S(1)}, bf16[1,128,1024]{2,1,0:T(8,128)(2,1)}, u32[]{:S(2)}) copy-start(bf16[1,128,1024]{2,1,0:T(8,128)(2,1)} %param.10) | copy-start | bytes 786436
  71.5 30.8 %all-to-all-start.8 = ((bf16[8,1024,128]{2,1,0:T(8,128)(2,1)}), bf16[8,1024,128]{2,1,0:T(8,128)(2,1)S(1)}, u32[]{:S(2)}, u32[]{:S(2)}) async-start(bf16[8,1024,128]{2,1,0:T(8,128)(2,1)} %bitcast.29), calls=%async_computation.8 | async-start | bytes 4194304 | tf_op jit(solution)/shard_map/all_to_all | solution.py:44
  76.0 31.8 %copy-start.17 = (s32[1,32]{1,0:T(1,128)S(1)}, s32[1,32]{1,0:T(1,128)}, u32[]{:S(2)}) copy-start(s32[1,32]{1,0:T(1,128)} %param.13) | copy-start | bytes 388
  76.0 33.2 %copy-start.18 = (s32[1,32]{1,0:T(1,128)S(1)}, s32[1,32]{1,0:T(1,128)}, u32[]{:S(2)}) copy-start(s32[1,32]{1,0:T(1,128)} %param.14) | copy-start | bytes 388
  78.0 1.0 copy-start.9
  102.3 30.5 %all-to-all-start.4 = ((bf16[16,2,128,128]{3,2,1,0:T(8,128)(2,1)}), bf16[16,2,128,128]{3,2,1,0:T(8,128)(2,1)S(1)}, u32[]{:S(2)}, u32[]{:S(2)}) async-start(bf16[16,2,128,128]{3,2,1,0:T(8,128)(2,1)} %bitcast.36), calls=%async_computation.4 | async-start | bytes 2097152 | tf_op jit(solution)/shard_map/all_to_all | solution.py:44
  132.7 29.5 %all-to-all-start.1 = ((bf16[16,2,128,128]{3,2,1,0:T(8,128)(2,1)}), bf16[16,2,128,128]{3,2,1,0:T(8,128)(2,1)}, u32[]{:S(2)}, u32[]{:S(2)}) async-start(bf16[16,2,128,128]{3,2,1,0:T(8,128)(2,1)} %bitcast.12), calls=%async_computation.1 | async-start | bytes 2097152 | tf_op jit(solution)/shard_map/all_to_all | solution.py:44
  137.1 1.6 copy-start.7
  159.8 1.0 copy-start.11
  160.8 1.0 copy-start.12
  162.2 48.6 %all-to-all-start.7 = ((bf16[16,2,128,128]{3,2,1,0:T(8,128)(2,1)}), bf16[16,2,128,128]{3,2,1,0:T(8,128)(2,1)S(1)}, u32[]{:S(2)}, u32[]{:S(2)}) async-start(bf16[16,2,128,128]{3,2,1,0:T(8,128)(2,1)} %copy-done.12), calls=%async_computation.7 | async-start | bytes 2097152 | tf_op jit(solution)/shard_map/all_to_all | solution.py:44
  207.5 1.0 copy-start.10
  208.5 1.0 copy-start.13
  259.2 17.8 %all-to-all-start.5 = ((bf16[4,128,1024]{2,1,0:T(8,128)(2,1)}), bf16[4,128,1024]{2,1,0:T(8,128)(2,1)}, u32[]{:S(2)}, u32[]{:S(2)}) async-start(bf16[4,128,1024]{2,1,0:T(8,128)(2,1)} %bitcast.38), calls=%async_computation.5 | async-start | bytes 2097152 | tf_op jit(solution)/shard_map/all_to_all | solution.py:44
  263.4 1.2 copy-start.2
  266.5 1.0 copy-start.14
  297.1 17.4 %all-to-all-start.2 = ((bf16[4,128,1024]{2,1,0:T(8,128)(2,1)}), bf16[4,128,1024]{2,1,0:T(8,128)(2,1)S(1)}, u32[]{:S(2)}, u32[]{:S(2)}) async-start(bf16[4,128,1024]{2,1,0:T(8,128)(2,1)} %bitcast.37), calls=%async_computation.2 | async-start | bytes 2097152 | tf_op jit(solution)/shard_map/all_to_all | solution.py:44
  300.9 1.2 copy-start.6
  305.1 1.0 copy-start.5
  314.5 1.0 copy-start.3
  315.5 6.2 %copy-start.4 = (bf16[4,128,1024]{2,1,0:T(8,128)(2,1)S(1)}, bf16[4,128,1024]{2,1,0:T(8,128)(2,1)}, u32[]{:S(2)}) copy-start(bf16[4,128,1024]{2,1,0:T(8,128)(2,1)} %copy-done.3) | copy-start | bytes 3145732
  315.5 34.9 %all-to-all-start.10 = ((bf16[64,16,512]{2,1,0:T(8,128)(2,1)}), bf16[64,16,512]{2,1,0:T(8,128)(2,1)S(1)}, u32[]{:S(2)}, u32[]{:S(2)}) async-start(bf16[64,16,512]{2,1,0:T(8,128)(2,1)} %bitcast.33), calls=%async_computation.10 | async-start | bytes 2097152 | tf_op jit(solution)/shard_map/all_to_all | solution.py:44

commit v2 on v1

v2 whole, which is shorter than its diff:
```python
import math

import jax
import jax.numpy as jnp
from jax import lax
from jax.experimental import pallas as pl
from jax.experimental.pallas import tpu as pltpu
from jax.sharding import PartitionSpec as P

HEADS = 64
KV_HEADS = 8
D = 128
HALF = D // 2
TOK = 128
SP = 32
PARTS = 2
REP = HEADS // KV_HEADS
CHUNK = 2 * TOK
CHUNKS = 8
STACK = 4
ROWS = STACK * CHUNK
SCALE = D ** (-0.5)
LOG2E = 1.4426950408889634
MIB = 1 << 20

HALF_GROUPS = [list(range(16)), list(range(16, 32))]
PLANE_GROUPS = [
    [s * 8 + y * 2 + zh for s in range(SP) for zh in range(2)] for y in range(4)
]


def swap(array, axes, groups):
    return lax.all_to_all(
        array, axes, split_axis=0, concat_axis=0, axis_index_groups=groups, tiled=True
    )


def quad_send(array, delta):
    flip = (delta & 1) | (delta >> 1) << 3
    return lax.ppermute(array, "sp", [(s, s ^ flip) for s in range(SP)])


def y_send(array, step, core=0):
    pairs = []
    for s in range(SP):
        for d in range(8):
            to = ((d // 2 + step) % 4) * 2 + d % 2
            pairs.append((s * 8 + d, (s ^ core) * 8 + to))
    return lax.ppermute(array, ("sp", "dp"), pairs)


def after(array, *earlier):
    return lax.optimization_barrier((array, *earlier))[0]


def params(limit=48):
    return pltpu.CompilerParams(vmem_limit_bytes=limit * MIB)


def cost(flops, nbytes):
    return pl.CostEstimate(flops=flops, bytes_accessed=nbytes, transcendentals=0)


def dot(a, b, dims):
    return lax.dot_general(a, b, (dims, ((), ())), preferred_element_type=jnp.float32)


def turn(x, cos, sin):
    return x * cos + pltpu.roll(x, HALF, 1) * sin


def key_prep_kernel(k_ref, v_ref, cos_ref, sin_ref, *outs):
    cos, sin = cos_ref[...], sin_ref[...]
    for part in range(PARTS):
        cols = slice(part * D, (part + 1) * D)
        k = turn(k_ref[:, cols].astype(jnp.float32), cos, sin).astype(jnp.bfloat16)
        v = v_ref[:, cols]
        for z in range(4):
            outs[part][0, z, 0, 0] = k
            outs[part][0, z, 0, 1] = v


def key_prep(k, v, cos, sin):
    table = pl.BlockSpec((TOK, D), lambda j: (0, 0))
    column = pl.BlockSpec((TOK, PARTS * D), lambda j: (0, j))
    shape = jax.ShapeDtypeStruct((2, 4, 2, 2, TOK, D), jnp.bfloat16)
    return pl.pallas_call(
        key_prep_kernel,
        grid=(4,),
        in_specs=[column, column, table, table],
        out_specs=[
            pl.BlockSpec((1, 4, 1, 2, TOK, D), lambda j: (j // 2, 0, j % 2, 0, 0, 0))
        ]
        * PARTS,
        out_shape=[shape] * PARTS,
        compiler_params=params(),
        cost_estimate=cost(1 << 20, 3 * MIB),
        name="key_prep",
    )(k, v, cos, sin)


def query_prep_kernel(me_ref, q_ref, g_ref, cos_ref, sin_ref, valid_ref, *outs):
    cos, sin = cos_ref[...], sin_ref[...]
    keep = valid_ref[...] > 0.0
    for delta in range(4):

        @pl.when(pl.program_id(0) == delta)
        def _():
            for h in range(REP):
                cols = slice(h * D, (h + 1) * D)
                q = turn(q_ref[:, cols].astype(jnp.float32), cos, sin)
                outs[delta][0, :, cols] = q.astype(jnp.bfloat16)
                g = jnp.where(keep, g_ref[:, cols].astype(jnp.float32), 0.0)
                outs[delta][1, :, cols] = g.astype(jnp.bfloat16)


def query_prep(part, quad, q, g, cos, sin, valid):
    table = pl.BlockSpec((TOK, D), lambda i, me: (0, 0))
    column = pl.BlockSpec((TOK, REP * D), lambda i, me: (0, (me[0] ^ i) * PARTS + part))
    shape = jax.ShapeDtypeStruct((2, TOK, REP * D), jnp.bfloat16)
    return pl.pallas_call(
        query_prep_kernel,
        grid_spec=pltpu.PrefetchScalarGridSpec(
            num_scalar_prefetch=1,
            grid=(4,),
            in_specs=[column, column, table, table, table],
            out_specs=[pl.BlockSpec((2, TOK, REP * D), lambda i, me: (0, 0, 0))] * 4,
        ),
        out_shape=[shape] * 4,
        compiler_params=params(),
        cost_estimate=cost(4 << 20, 4 * MIB),
        name="query_prep",
    )(quad, q, g, cos, sin, valid)


def input_prep_kernel(me_ref, x_ref, *refs):
    outs, flipped = refs[:4], refs[4]
    for s in range(4):
        flipped[...] = x_ref[:, s * TOK : (s + 1) * TOK].T
        for step in range(4):
            at = pl.multiple_of((me_ref[0] + step) % 4 * 32, 32)
            outs[step][s] = flipped[pl.ds(at, 32)]


def input_prep(y, x):
    return pl.pallas_call(
        input_prep_kernel,
        grid_spec=pltpu.PrefetchScalarGridSpec(
            num_scalar_prefetch=1,
            grid=(8,),
            in_specs=[pl.BlockSpec((TOK, 512), lambda i, me: (0, i))],
            out_specs=[pl.BlockSpec((4, 32, TOK), lambda i, me: (i, 0, 0))] * 4,
            scratch_shapes=[pltpu.VMEM((TOK, TOK), jnp.bfloat16)],
        ),
        out_shape=[jax.ShapeDtypeStruct((SP, 32, TOK), jnp.bfloat16)] * 4,
        compiler_params=params(),
        cost_estimate=cost(1 << 20, 2 * MIB),
        name="input_prep",
    )(y, x)


def attention_kernel(meta_ref, *refs):
    qg_refs, (kv_ref, cos_ref, sin_ref) = refs[:4], refs[4:7]
    dq_refs, dkv_ref = refs[7:11], refs[11]
    kt_ref, e_ref, dp_ref, peak_ref, dk_ref, dv_ref, dqt_ref = refs[12:]
    heads = pl.program_id(0)
    nt, nn = ((1,), (1,)), ((1,), (0,))

    def keys(p, which):
        return kv_ref[pl.ds(2 * p, 2), which].reshape(CHUNK, D)

    @pl.when(heads == 0)
    def _():
        dk_ref[...] = jnp.zeros_like(dk_ref)
        dv_ref[...] = jnp.zeros_like(dv_ref)
        for p in range(CHUNKS):
            kt_ref[p] = keys(p, 0).T

    def attend(block):
        low, diagonal = meta_ref[block, 0], meta_ref[block, 1]
        count, core = meta_ref[block, 2], meta_ref[block, 3]

        def stacked(which):
            return jnp.concatenate(
                [
                    qg_refs[2 * block + other][which, :, h * D : (h + 1) * D]
                    for h in range(STACK)
                    for other in range(2)
                ],
                axis=0,
            )

        @pl.when(count <= 0)
        def _():
            for other in range(2):
                ref = dq_refs[2 * block + other]
                ref[...] = jnp.zeros_like(ref)

        @pl.when(count > 0)
        def _():
            q, g = stacked(0), stacked(1)

            def score(p, state, allowed=None):
                peak, total, mixed = state
                s = dot(keys(p, 0), q, nt)
                if allowed is not None:
                    s = jnp.where(allowed, s, -1e30)
                dp = dot(keys(p, 1), g, nt)
                dp_ref[p] = dp
                higher = jnp.maximum(peak, jnp.max(s, axis=0, keepdims=True))
                shrink = jnp.exp2((peak - higher) * (SCALE * LOG2E))
                e = jnp.exp2((s - higher) * (SCALE * LOG2E))
                e_ref[p] = e
                peak_ref[p] = higher
                return (
                    higher,
                    total * shrink + jnp.sum(e, axis=0, keepdims=True),
                    mixed * shrink + jnp.sum(e * dp, axis=0, keepdims=True),
                )

            zero = jnp.zeros((1, ROWS), jnp.float32)
            state = (jnp.full((1, ROWS), -1e30, jnp.float32), zero, zero)
            state = lax.fori_loop(low, diagonal, score, state)
            key_at = lax.broadcasted_iota(jnp.int32, (CHUNK, ROWS), 0)
            row_at = lax.broadcasted_iota(jnp.int32, (CHUNK, ROWS), 1) & (CHUNK - 1)
            row_at = row_at ^ (core * TOK)
            allowed = (key_at <= row_at) & (key_at < count)
            peak, total, mixed = score(diagonal, state, allowed)
            inverse = 1.0 / total
            row_dot = mixed * inverse
            dqt_ref[...] = jnp.zeros_like(dqt_ref)

            def spread(p, carry):
                factor = jnp.exp2((peak_ref[p] - peak) * (SCALE * LOG2E)) * inverse
                weights = e_ref[p] * factor
                ds = (weights * (dp_ref[p] - row_dot)).astype(jnp.bfloat16)
                dv_ref[p] += dot(weights.astype(jnp.bfloat16), g, nn)
                dk_ref[p] += dot(ds, q, nn)
                dqt_ref[...] += dot(kt_ref[p], ds, nn)
                return carry

            lax.fori_loop(low, diagonal + 1, spread, 0)
            cos, sin = cos_ref[block], sin_ref[block]
            for h in range(STACK):
                cols = slice(h * CHUNK, (h + 1) * CHUNK)
                x1 = dqt_ref[:HALF, cols] * SCALE
                x2 = dqt_ref[HALF:, cols] * SCALE
                y = jnp.concatenate([x1 * cos + x2 * sin, x2 * cos - x1 * sin], axis=0)
                y = y.T.astype(jnp.bfloat16)
                for other in range(2):
                    dq_refs[2 * block + other][:, h * D : (h + 1) * D] = y[
                        other * TOK : (other + 1) * TOK
                    ]

    attend(0)
    attend(1)

    @pl.when(heads == REP // STACK - 1)
    def _():
        for p in range(CHUNKS):
            dk = (dk_ref[p] * SCALE).astype(jnp.bfloat16)
            dkv_ref[2 * p : 2 * p + 2, 0] = dk.reshape(2, TOK, D)
            dkv_ref[2 * p : 2 * p + 2, 1] = dv_ref[p].astype(jnp.bfloat16).reshape(2, TOK, D)


def attention(meta, qg, kv, cos, sin):
    width = STACK * D
    table = pl.BlockSpec((2, HALF, CHUNK), lambda h: (0, 0, 0))
    whole = pl.BlockSpec((16, 2, TOK, D), lambda h: (0, 0, 0, 0))
    return pl.pallas_call(
        attention_kernel,
        grid=(REP // STACK,),
        in_specs=[pl.BlockSpec(memory_space=pltpu.SMEM)]
        + [pl.BlockSpec((2, TOK, width), lambda h: (0, 0, h))] * 4
        + [whole, table, table],
        out_specs=[pl.BlockSpec((TOK, width), lambda h: (0, h))] * 4 + [whole],
        out_shape=[jax.ShapeDtypeStruct((TOK, REP * D), jnp.bfloat16)] * 4
        + [jax.ShapeDtypeStruct((16, 2, TOK, D), jnp.bfloat16)],
        scratch_shapes=[
            pltpu.VMEM((CHUNKS, D, CHUNK), jnp.bfloat16),
            pltpu.VMEM((CHUNKS, CHUNK, ROWS), jnp.float32),
            pltpu.VMEM((CHUNKS, CHUNK, ROWS), jnp.float32),
            pltpu.VMEM((CHUNKS, 1, ROWS), jnp.float32),
            pltpu.VMEM((CHUNKS, CHUNK, D), jnp.float32),
            pltpu.VMEM((CHUNKS, CHUNK, D), jnp.float32),
            pltpu.VMEM((D, ROWS), jnp.float32),
        ],
        compiler_params=params(),
        cost_estimate=cost(25 * 10**9, 6 * MIB),
        name="attention",
    )(meta, *qg, kv, cos, sin)


def key_post_kernel(core_ref, in_ref, cos_ref, sin_ref, dk_ref, dv_ref, same_ref, other_ref):
    cos, sin = cos_ref[...], sin_ref[...]
    dk = in_ref[0, 0, 0, 0].astype(jnp.float32)
    dv = in_ref[0, 0, 0, 1].astype(jnp.float32)
    for z in range(1, 4):
        dk += in_ref[0, z, 0, 0].astype(jnp.float32)
        dv += in_ref[0, z, 0, 1].astype(jnp.float32)
    dk = turn(dk, cos, -sin).astype(jnp.bfloat16)
    dk_ref[0] = dk
    dv_ref[0] = dv.astype(jnp.bfloat16)
    quad = pl.program_id(0)
    for side in range(2):
        cols = slice(side * D, (side + 1) * D)

        @pl.when((quad % 2 == side) & (quad // 2 == core_ref[0]))
        def _():
            same_ref[:, cols] = dk

        @pl.when((quad % 2 == side) & (quad // 2 != core_ref[0]))
        def _():
            other_ref[:, cols] = dk


def key_post(core, back, cos, sin):
    table = pl.BlockSpec((TOK, D), lambda j, me: (0, 0))
    piece = pl.BlockSpec((TOK, 2 * D), lambda j, me: (0, 0))
    lane = pl.BlockSpec((1, TOK, D), lambda j, me: (j, 0, 0))
    full = jax.ShapeDtypeStruct((4, TOK, D), jnp.bfloat16)
    sent = jax.ShapeDtypeStruct((TOK, 2 * D), jnp.bfloat16)
    return pl.pallas_call(
        key_post_kernel,
        grid_spec=pltpu.PrefetchScalarGridSpec(
            num_scalar_prefetch=1,
            grid=(4,),
            in_specs=[
                pl.BlockSpec(
                    (1, 4, 1, 2, TOK, D), lambda j, me: (j // 2, 0, j % 2, 0, 0, 0)
                ),
                table,
                table,
            ],
            out_specs=[lane, lane, piece, piece],
        ),
        out_shape=[full, full, sent, sent],
        compiler_params=params(),
        cost_estimate=cost(1 << 20, 2 * MIB),
        name="key_post",
    )(core, back.reshape(2, 4, 2, 2, TOK, D), cos, sin)


def join_kernel(ka_ref, kb_ref, va_ref, vb_ref, dk_ref, dv_ref):
    for j in range(4):
        for part, (k_ref, v_ref) in enumerate(((ka_ref, va_ref), (kb_ref, vb_ref))):
            cols = slice((PARTS * j + part) * D, (PARTS * j + part + 1) * D)
            dk_ref[:, cols] = k_ref[j]
            dv_ref[:, cols] = v_ref[j]


def join(ka, kb, va, vb):
    vmem = pl.BlockSpec(memory_space=pltpu.VMEM)
    full = jax.ShapeDtypeStruct((TOK, KV_HEADS * D), jnp.bfloat16)
    return pl.pallas_call(
        join_kernel,
        in_specs=[vmem] * 4,
        out_specs=[vmem] * 2,
        out_shape=[full] * 2,
        compiler_params=params(),
        cost_estimate=cost(1 << 20, MIB),
        name="join",
    )(ka, kb, va, vb)


def query_post_kernel(me_ref, *refs):
    out_ref = refs[8]
    for delta in range(4):

        @pl.when(pl.program_id(0) == delta)
        def _():
            out_ref[:, : REP * D] = refs[delta][...]
            out_ref[:, REP * D :] = refs[4 + delta][...]


def query_post(quad, a, b):
    source = pl.BlockSpec((TOK, REP * D), lambda i, me: (0, 0))
    return pl.pallas_call(
        query_post_kernel,
        grid_spec=pltpu.PrefetchScalarGridSpec(
            num_scalar_prefetch=1,
            grid=(4,),
            in_specs=[source] * 8,
            out_specs=pl.BlockSpec((TOK, PARTS * REP * D), lambda i, me: (0, me[0] ^ i)),
        ),
        out_shape=jax.ShapeDtypeStruct((TOK, HEADS * D), jnp.bfloat16),
        compiler_params=params(),
        cost_estimate=cost(1 << 20, 4 * MIB),
        name="query_post",
    )(quad, *a, *b)


def project_kernel(*refs):
    nn = ((1,), (0,))
    total = dot(refs[0][...], refs[8][...], nn)
    for i in range(1, 8):
        total += dot(refs[i][...], refs[8 + i][...], nn)
    refs[16][...] = total.astype(jnp.bfloat16)


def project(xt, kg):
    return pl.pallas_call(
        project_kernel,
        grid=(2,),
        in_specs=[pl.BlockSpec((512, TOK), lambda i: (i, 0))] * 8
        + [pl.BlockSpec((TOK, 2 * D), lambda i: (0, 0))] * 8,
        out_specs=pl.BlockSpec((512, 2 * D), lambda i: (i, 0)),
        out_shape=jax.ShapeDtypeStruct((1024, 2 * D), jnp.bfloat16),
        compiler_params=params(),
        cost_estimate=cost(10**9, 3 * MIB),
        name="project",
    )(*xt, *kg)


def final_sum_kernel(a_ref, b_ref, out_ref):
    for c in range(2):
        for part, ref in enumerate((a_ref, b_ref)):
            total = jnp.zeros((16, 2 * D), jnp.float32)
            for s in range(16):
                for zh in range(2):
                    total += ref[s, c, zh].astype(jnp.float32)
            for side in range(2):
                head = (2 * c + side) * PARTS + part
                out_ref[:, head * D : (head + 1) * D] = total[:, side * D : (side + 1) * D]


def final_sum(a, b):
    vmem = pl.BlockSpec(memory_space=pltpu.VMEM)
    return pl.pallas_call(
        final_sum_kernel,
        in_specs=[vmem] * 2,
        out_specs=vmem,
        out_shape=jax.ShapeDtypeStruct((16, 1024), jnp.float32),
        compiler_params=params(),
        cost_estimate=cost(1 << 20, MIB),
        name="final_sum",
    )(a.reshape(16, 2, 2, 16, 2 * D), b.reshape(16, 2, 2, 16, 2 * D))


def local(q, k, v, g, x, group_first, seq_length, pos_offset):
    me = lax.axis_index("sp")
    first, length, offset = group_first[0], seq_length[0], pos_offset[0]
    rates = jnp.exp(jnp.arange(HALF, dtype=jnp.float32) * (-2.0 * math.log(10000.0) / D))
    token = jnp.arange(TOK, dtype=jnp.int32)

    own = (me - first[me]) * TOK + token
    phase = (offset[me] + own).astype(jnp.float32)[:, None] * rates[None, :]
    cos, sin = jnp.cos(phase), jnp.sin(phase)
    cos = jnp.concatenate([cos, cos], -1)
    sin = jnp.concatenate([-sin, sin], -1)
    valid = jnp.broadcast_to((own < length[me]).astype(jnp.float32)[:, None], (TOK, D))

    half = me // 16
    z = me % 8 // 2
    core = me % 2
    quad = me // 8 % 2 * 2 + core
    y = lax.axis_index("dp") // 2
    beside = (me // 8 % 2) ^ jnp.arange(2, dtype=jnp.int32)
    device = half * 16 + beside * 8 + z * 2
    start = first[device]
    before = (device - start) * TOK
    meta = jnp.stack(
        [
            (start - half * 16) // 2,
            (device - half * 16) // 2,
            jnp.clip(length[device] - before, 0, CHUNK),
            jnp.broadcast_to(core, (2,)),
        ],
        axis=1,
    )
    inside = jnp.arange(CHUNK, dtype=jnp.int32) ^ (core * TOK)
    place = (offset[device] + before)[:, None] + inside[None, :]
    turned = place.astype(jnp.float32)[:, None, :] * rates[None, :, None]
    cos_t, sin_t = jnp.cos(turned), jnp.sin(turned)
    quad_at, y_at, core_at = (i.astype(jnp.int32).reshape(1) for i in (quad, y, core))

    def quad_swap(pieces):
        return [pieces[0]] + [quad_send(pieces[d], d) for d in range(1, 4)]

    kv_out = [a.reshape(16, 2, TOK, D) for a in key_prep(k[0], v[0], cos, sin)]
    qg_out = [
        query_prep(part, quad_at, q[0], g[0], cos, sin, valid) for part in range(PARTS)
    ]
    qg_in = [quad_swap(qg_out[0])]
    kv_in = [swap(kv_out[0], "sp", HALF_GROUPS)]
    qg_in.append(quad_swap([after(piece, *qg_in[0]) for piece in qg_out[1]]))
    kv_in.append(swap(after(kv_out[1], kv_in[0]), "sp", HALF_GROUPS))

    xt = [a.reshape(1024, TOK) for a in input_prep(y_at, x[0])]
    xt = [xt[0]] + [y_send(xt[step], step) for step in range(1, 4)]
    xt = xt + [y_send(a, 0, 1) for a in xt]

    dq_back, dkv_back = [], []
    for part in range(PARTS):
        *dq, dkv = attention(meta, qg_in[part], kv_in[part], cos_t, sin_t)
        dkv_back.append(swap(dkv, "sp", HALF_GROUPS))
        dq_back.append(quad_swap(dq))

    dk, dv, pieces = [], [], []
    for part in range(PARTS):
        dk_part, dv_part, same, other = key_post(core_at, dkv_back[part], cos, sin)
        dk.append(dk_part)
        dv.append(dv_part)
        kg = [same] + [y_send(same, step) for step in range(1, 4)]
        kg += [y_send(other, step, 1) for step in range(4)]
        partial = project(xt, kg).reshape(64, 16, 2 * D)
        pieces.append(swap(partial, ("sp", "dp"), PLANE_GROUPS))
    kproj_grad = final_sum(*pieces)
    key_gradient, value_gradient = join(*dk, *dv)
    query_grad = query_post(quad_at, *dq_back)
    return (query_grad[None], key_gradient[None], value_gradient[None], kproj_grad)


def solution(mesh):
    tokens = P("dp", "sp", None)
    table = P("dp", None)
    return jax.shard_map(
        local,
        mesh=mesh,
        in_specs=(tokens,) * 5 + (table,) * 3,
        out_specs=(tokens, tokens, tokens, P(("sp", "dp"), None)),
        check_vma=False,
    )
```

time: 353 us -> 265 us (0.75); the launches traced: 351 us -> 260 us
  blocking collectives: 99.6 us -> 0 us
  starting transfers between devices: 57.9 us -> 98.3 us
  waiting for transfers between devices: 113 us -> 75.2 us
  local copies, waits for them, and re-layouts: 17.3 us -> 28.9 us
  Pallas kernels: 59.7 us -> 51.9 us
    all_to_all x8 -> x6, waiting for transfers between devices: 113 us -> 11.4 us  [swap(): lax.all_to_all(array, axes, split_axis=0, concat_axis=0, axis_index_group...]
    all_to_all x3 -> x0, blocking collectives: 99.6 us -> none  [swap(): lax.all_to_all(array, axes, split_axis=0, concat_axis=0, axis_index_group...]
    ppermute x0 -> x33, waiting for transfers between devices: none -> 63.8 us  [the longest x12 46.1 us: quad_send(): return lax.ppermute(array, 'sp', [(s, s ^ flip) for s in range(SP)])]
    ppermute x0 -> x33, starting transfers between devices: none -> 40.6 us  [the longest x21 31.9 us: y_send(): return lax.ppermute(array, ('sp', 'dp'), pairs)]
    unnamed x38 -> x92, local copies, waits for them, and re-layouts: 13.2 us -> 24.6 us
    pallas_call x8 -> x12, Pallas kernels: 57.8 us -> 50 us  [the longest x2 31.8 us: attention(): pl.pallas_call(attention_kernel, grid=(REP // STACK,), in_specs=[pl.Block...]
    all_to_all x8 -> x6, starting transfers between devices: 57.9 us -> 57.7 us  [swap(): lax.all_to_all(array, axes, split_axis=0, concat_axis=0, axis_index_group...]
  transfers between devices with their start and end apart: 8 -> 39, of which waited for: 8 -> 14; matrix products, arithmetic and copies ran while one was open for 1% -> 2% of each run, Pallas kernels for 15% -> 19%
where the time goes in v2:
time: 265 us; the launch traced here: 260 us
  starting transfers between devices  98.3 us (37%)
  waiting for transfers between devices  75.2 us (28%)
  Pallas kernels  51.9 us (20%)
  local copies, waits for them, and re-layouts  28.9 us (11%)
  other arithmetic  3.37 us (1%)
    all_to_all x6, starting transfers between devices, swap(): lax.all_to_all(array, axes, split_axis=0, concat_axis=0, axis_index_group...  57.7 us
    ppermute x12, waiting for transfers between devices, quad_send(): return lax.ppermute(array, 'sp', [(s, s ^ flip) for s in range(SP)])  46.1 us
    ppermute x21, starting transfers between devices, y_send(): return lax.ppermute(array, ('sp', 'dp'), pairs)  31.9 us
    pallas_call x2, Pallas kernels, attention(): pl.pallas_call(attention_kernel, grid=(REP // STACK,), in_specs=[pl.Block...  31.8 us
    unnamed x92, local copies, waits for them, and re-layouts  24.6 us
    ppermute x21, waiting for transfers between devices, y_send(): return lax.ppermute(array, ('sp', 'dp'), pairs)  17.7 us
    all_to_all x6, waiting for transfers between devices, swap(): lax.all_to_all(array, axes, split_axis=0, concat_axis=0, axis_index_group...  11.4 us
    ppermute x12, starting transfers between devices, quad_send(): return lax.ppermute(array, 'sp', [(s, s ^ flip) for s in range(SP)])  8.7 us
  transfers between devices with their start and end apart: 39, of which 14 were waited for; matrix products, arithmetic and copies ran while one was open for 2% of the time, Pallas kernels for 19%

profile of v2, /device:TPU:1, one launch (start us, length us, event | category | flops | bytes accessed | tf_op | source)
XLA Modules:
  0.0 259.5 jit_solution(1106799957303380148)
XLA Ops:
  0.7 1.4 constant_dynamic-slice_fusion
  6.4 1.9 key_prep.1
  8.3 1.0 copy-done.3
  9.3 8.3 %all-to-all-start = ((bf16[16,2,128,128]{3,2,1,0:T(8,128)(2,1)}), bf16[16,2,128,128]{3,2,1,0:T(8,128)(2,1)S(1)}, u32[]{:S(2)}, u32[]{:S(2)}) async-start(bf16[16,2,128,128]{3,2,1,0:T(8,128)(2,1)} %bitcast.40), calls=%async_computation | async-start | bytes 2097152 | tf_op jit(solution)/shard_map/all_to_all | solution.py:33
  18.4 4.0 %query_prep.2 = (bf16[2,128,1024]{2,1,0:T(8,128)(2,1)S(1)}, bf16[2,128,1024]{2,1,0:T(8,128)(2,1)}, bf16[2,128,1024]{2,1,0:T(8,128)(2,1)}, bf16[2,128,1024]{2,1,0:T(8,128)(2,1)}) custom-call(s32[1]{0:T(128)} %bitcast.me_ref, bf16[128,8192]{1,0:T(8,128)(2,1)S(1)} %bitcast.33, bf16[128,8192]{1,0:T(8,128)(2,1)} %bitcast.51, ...), custom_call_target="tpu_custom_call" | custom-call | flops 4194304 | bytes 4194304 | tf_op jit(solution)/shard_map/query_prep/pallas_call | solution.py:121
  23.4 1.6 collective-permute-start.1
  27.7 4.0 %query_prep.3 = (bf16[2,128,1024]{2,1,0:T(8,128)(2,1)S(1)}, bf16[2,128,1024]{2,1,0:T(8,128)(2,1)}, bf16[2,128,1024]{2,1,0:T(8,128)(2,1)}, bf16[2,128,1024]{2,1,0:T(8,128)(2,1)}) custom-call(s32[1]{0:T(128)} %bitcast.me_ref, bf16[128,8192]{1,0:T(8,128)(2,1)S(1)} %bitcast.34, bf16[128,8192]{1,0:T(8,128)(2,1)} %bitcast.52, ...), custom_call_target="tpu_custom_call" | custom-call | flops 4194304 | bytes 4194304 | tf_op jit(solution)/shard_map/query_prep/pallas_call | solution.py:121
  32.7 1.3 multiply_sine_fusion
  34.0 8.6 %collective-permute-done.1.refs_2_ = bf16[2,128,1024]{2,1,0:T(8,128)(2,1)} collective-permute-done((bf16[2,128,1024]{2,1,0:T(8,128)(2,1)}, bf16[2,128,1024]{2,1,0:T(8,128)(2,1)}, u32[]{:S(2)}, u32[]{:S(2)}) %collective-permute-start.1) | collective-permute-done | bytes 524320 | tf_op jit(solution)/shard_map/ppermute | solution.py:40
  42.6 11.4 %collective-permute-done.2.refs_3_ = bf16[2,128,1024]{2,1,0:T(8,128)(2,1)} collective-permute-done((bf16[2,128,1024]{2,1,0:T(8,128)(2,1)}, bf16[2,128,1024]{2,1,0:T(8,128)(2,1)}, u32[]{:S(2)}, u32[]{:S(2)}) %collective-permute-start.2) | collective-permute-done | bytes 524320 | tf_op jit(solution)/shard_map/ppermute | solution.py:40
  54.2 1.2 collective-permute-start.7
  56.1 6.3 %all-to-all-start.1 = ((bf16[16,2,128,128]{3,2,1,0:T(8,128)(2,1)}), bf16[16,2,128,128]{3,2,1,0:T(8,128)(2,1)S(1)}, u32[]{:S(2)}, u32[]{:S(2)}) async-start(bf16[16,2,128,128]{3,2,1,0:T(8,128)(2,1)} %bitcast.14), calls=%async_computation.1 | async-start | bytes 2097152 | tf_op jit(solution)/shard_map/all_to_all | solution.py:33
  64.2 1.0 copy-done.15
  65.3 15.9 %attention.2 = (bf16[128,1024]{1,0:T(8,128)(2,1)S(1)}, bf16[128,1024]{1,0:T(8,128)(2,1)S(1)}, bf16[128,1024]{1,0:T(8,128)(2,1)S(1)}, bf16[128,1024]{1,0:T(8,128)(2,1)S(1)}, bf16[16,2,128,128]{3,2,1,0:T(8,128)(2,1)S(1)}) custom-call(s32[2,4]{1,0:T(2,128)S(1)} %add_add_fusion.meta_ref, bf16[2,128,1024]{2,1,0:T(8,128)(2,1)S(1)} %copy-done.15, ...), custom_call_target="tpu_custom_call" | custom-call | flops 24999999488 | bytes 6291456 | tf_op jit(solution)/shard_map/attention/pallas_call | solution.py:270
  81.2 1.0 copy-done.5
  84.2 6.3 %all-to-all-done.1.refs_4_ = bf16[16,2,128,128]{3,2,1,0:T(8,128)(2,1)S(1)} async-done(((bf16[16,2,128,128]{3,2,1,0:T(8,128)(2,1)}), bf16[16,2,128,128]{3,2,1,0:T(8,128)(2,1)S(1)}, u32[]{:S(2)}, u32[]{:S(2)}) %all-to-all-start.1) | async-done | bytes 1048608 | tf_op jit(solution)/shard_map/all_to_all | solution.py:33
  90.5 13.0 %all-to-all-start.2 = ((bf16[16,2,128,128]{3,2,1,0:T(8,128)(2,1)}), bf16[16,2,128,128]{3,2,1,0:T(8,128)(2,1)S(1)}, u32[]{:S(2)}, u32[]{:S(2)}) async-start(bf16[16,2,128,128]{3,2,1,0:T(8,128)(2,1)} %copy-done.5), calls=%async_computation.2 | async-start | bytes 2097152 | tf_op jit(solution)/shard_map/all_to_all | solution.py:33
  103.6 15.9 %attention.3 = (bf16[128,1024]{1,0:T(8,128)(2,1)S(1)}, bf16[128,1024]{1,0:T(8,128)(2,1)S(1)}, bf16[128,1024]{1,0:T(8,128)(2,1)S(1)}, bf16[128,1024]{1,0:T(8,128)(2,1)S(1)}, bf16[16,2,128,128]{3,2,1,0:T(8,128)(2,1)S(1)}) custom-call(s32[2,4]{1,0:T(2,128)S(1)} %add_add_fusion.meta_ref, bf16[2,128,1024]{2,1,0:T(8,128)(2,1)S(1)} %copy-done.17, ...), custom_call_target="tpu_custom_call" | custom-call | flops 24999999488 | bytes 6291456 | tf_op jit(solution)/shard_map/attention/pallas_call | solution.py:270
  119.5 1.0 copy-done.4
  123.3 5.1 %all-to-all-done.2 = bf16[16,2,128,128]{3,2,1,0:T(8,128)(2,1)S(1)} async-done(((bf16[16,2,128,128]{3,2,1,0:T(8,128)(2,1)}), bf16[16,2,128,128]{3,2,1,0:T(8,128)(2,1)S(1)}, u32[]{:S(2)}, u32[]{:S(2)}) %all-to-all-start.2) | async-done | bytes 1048608 | tf_op jit(solution)/shard_map/all_to_all | solution.py:33
  128.4 13.8 %all-to-all-start.3 = ((bf16[16,2,128,128]{3,2,1,0:T(8,128)(2,1)}), bf16[16,2,128,128]{3,2,1,0:T(8,128)(2,1)S(1)}, u32[]{:S(2)}, u32[]{:S(2)}) async-start(bf16[16,2,128,128]{3,2,1,0:T(8,128)(2,1)} %copy-done.4), calls=%async_computation.3 | async-start | bytes 2097152 | tf_op jit(solution)/shard_map/all_to_all | solution.py:33
  142.2 1.1 input_prep.1
  143.5 2.6 collective-permute-start.14
  146.7 11.3 %collective-permute-done.12.refs_1_ = bf16[1024,128]{1,0:T(8,128)(2,1)S(1)} collective-permute-done((bf16[1024,128]{1,0:T(8,128)(2,1)S(1)}, bf16[1024,128]{1,0:T(8,128)(2,1)S(1)}, u32[]{:S(2)}, u32[]{:S(2)}) %collective-permute-start.12) | collective-permute-done | bytes 262176 | tf_op jit(solution)/shard_map/ppermute | solution.py:49
  160.3 3.2 %collective-permute-start.20 = (bf16[128,256]{1,0:T(8,128)(2,1)S(1)}, bf16[128,256]{1,0:T(8,128)(2,1)S(1)}, u32[]{:S(2)}, u32[]{:S(2)}) collective-permute-start(bf16[128,256]{1,0:T(8,128)(2,1)S(1)} %get-tuple-element.78.refs_8_), channel_id=1, source_target_pairs={{0,4},{1,5},{2,6},{3,7},{4,0},{5,1},{6,2},{7,3},{8,12},{9,13},{10,... | collective-permute-start | bytes 196616 | tf_op jit(solution)/shard_map/ppermute | solution.py:49
  164.2 10.7 %collective-permute-start.23 = (bf16[128,256]{1,0:T(8,128)(2,1)S(1)}, bf16[128,256]{1,0:T(8,128)(2,1)S(1)}, u32[]{:S(2)}, u32[]{:S(2)}) collective-permute-start(bf16[128,256]{1,0:T(8,128)(2,1)S(1)} %get-tuple-element.79), channel_id=1, source_target_pairs={{0,10},{1,11},{2,12},{3,13},{4,14},{5,15},{6,8},{7,9},{8,2},{9,3},... | collective-permute-start | bytes 196616 | tf_op jit(solution)/shard_map/ppermute | solution.py:49
  175.3 2.2 collective-permute-start.25
  178.2 2.0 collective-permute-done.24.refs_14_
  180.3 2.1 project.2
  185.2 6.4 %all-to-all-start.4 = ((bf16[64,16,256]{2,1,0:T(8,128)(2,1)}), bf16[64,16,256]{2,1,0:T(8,128)(2,1)S(1)}, u32[]{:S(2)}, u32[]{:S(2)}) async-start(bf16[64,16,256]{2,1,0:T(8,128)(2,1)} %bitcast.27), calls=%async_computation.4 | async-start | bytes 1048576 | tf_op jit(solution)/shard_map/all_to_all | solution.py:33
  192.3 1.9 collective-permute-start.26
  194.3 2.2 collective-permute-start.27
  196.8 1.2 collective-permute-start.29
  198.0 1.3 collective-permute-start.30
  199.3 1.1 collective-permute-start.31
  200.4 1.6 collective-permute-start.32
  202.0 1.3 collective-permute-done.30.refs_13_
  203.3 1.9 collective-permute-done.31.refs_14_
  205.6 0.9 copy-done.29
  213.2 2.1 project.3
  215.3 10.0 %all-to-all-start.5 = ((bf16[64,16,256]{2,1,0:T(8,128)(2,1)}), bf16[64,16,256]{2,1,0:T(8,128)(2,1)S(1)}, u32[]{:S(2)}, u32[]{:S(2)}) async-start(bf16[64,16,256]{2,1,0:T(8,128)(2,1)} %bitcast.29), calls=%async_computation.5 | async-start | bytes 1048576 | tf_op jit(solution)/shard_map/all_to_all | solution.py:33
  225.9 1.3 collective-permute-start.4
  227.7 1.3 collective-permute-start.10
  229.7 7.7 %collective-permute-done.4.refs_2_ = bf16[128,1024]{1,0:T(8,128)(2,1)S(1)} collective-permute-done((bf16[128,1024]{1,0:T(8,128)(2,1)S(1)}, bf16[128,1024]{1,0:T(8,128)(2,1)S(1)}, u32[]{:S(2)}, u32[]{:S(2)}) %collective-permute-start.4) | collective-permute-done | bytes 262176 | tf_op jit(solution)/shard_map/ppermute | solution.py:40
  237.4 7.5 %collective-permute-done.5.refs_3_ = bf16[128,1024]{1,0:T(8,128)(2,1)S(1)} collective-permute-done((bf16[128,1024]{1,0:T(8,128)(2,1)S(1)}, bf16[128,1024]{1,0:T(8,128)(2,1)S(1)}, u32[]{:S(2)}, u32[]{:S(2)}) %collective-permute-start.5) | collective-permute-done | bytes 262176 | tf_op jit(solution)/shard_map/ppermute | solution.py:40
  244.9 5.1 %collective-permute-done.10.refs_6_ = bf16[128,1024]{1,0:T(8,128)(2,1)S(1)} collective-permute-done((bf16[128,1024]{1,0:T(8,128)(2,1)}, bf16[128,1024]{1,0:T(8,128)(2,1)S(1)}, u32[]{:S(2)}, u32[]{:S(2)}) %collective-permute-start.10) | collective-permute-done | bytes 262176 | tf_op jit(solution)/shard_map/ppermute | solution.py:40
  250.1 5.7 %collective-permute-done.11.refs_7_ = bf16[128,1024]{1,0:T(8,128)(2,1)S(1)} collective-permute-done((bf16[128,1024]{1,0:T(8,128)(2,1)S(1)}, bf16[128,1024]{1,0:T(8,128)(2,1)S(1)}, u32[]{:S(2)}, u32[]{:S(2)}) %collective-permute-start.11) | collective-permute-done | bytes 262176 | tf_op jit(solution)/shard_map/ppermute | solution.py:40
  255.8 1.8 query_post.1
  (159 shorter events, 36.1 us)
Async XLA Ops:
  9.3 46.8 %all-to-all-start = ((bf16[16,2,128,128]{3,2,1,0:T(8,128)(2,1)}), bf16[16,2,128,128]{3,2,1,0:T(8,128)(2,1)S(1)}, u32[]{:S(2)}, u32[]{:S(2)}) async-start(bf16[16,2,128,128]{3,2,1,0:T(8,128)(2,1)} %bitcast.40), calls=%async_computation | async-start | bytes 2097152 | tf_op jit(solution)/shard_map/all_to_all | solution.py:33
  23.2 10.7 %collective-permute-start = (bf16[2,128,1024]{2,1,0:T(8,128)(2,1)}, bf16[2,128,1024]{2,1,0:T(8,128)(2,1)}, u32[]{:S(2)}, u32[]{:S(2)}) collective-permute-start(bf16[2,128,1024]{2,1,0:T(8,128)(2,1)} %get-tuple-element.44), channel_id=1, source_target_pairs={{0,8},{8,0},{16,24},{24,16},{32,40},{40,32},{48,56},{56,48},{64,72... | collective-permute-start | bytes 1572872 | tf_op jit(solution)/shard_map/ppermute | solution.py:40
  23.4 19.2 %collective-permute-start.1 = (bf16[2,128,1024]{2,1,0:T(8,128)(2,1)}, bf16[2,128,1024]{2,1,0:T(8,128)(2,1)}, u32[]{:S(2)}, u32[]{:S(2)}) collective-permute-start(bf16[2,128,1024]{2,1,0:T(8,128)(2,1)} %get-tuple-element.45), channel_id=1, source_target_pairs={{0,64},{8,72},{16,80},{24,88},{32,96},{40,104},{48,112},{56,120},{... | collective-permute-start | bytes 1572872 | tf_op jit(solution)/shard_map/ppermute | solution.py:40
  25.0 29.0 %collective-permute-start.2 = (bf16[2,128,1024]{2,1,0:T(8,128)(2,1)}, bf16[2,128,1024]{2,1,0:T(8,128)(2,1)}, u32[]{:S(2)}, u32[]{:S(2)}) collective-permute-start(bf16[2,128,1024]{2,1,0:T(8,128)(2,1)} %get-tuple-element.46), channel_id=1, source_target_pairs={{0,72},{8,64},{16,88},{24,80},{32,104},{40,96},{48,120},{56,112},{... | collective-permute-start | bytes 1572872 | tf_op jit(solution)/shard_map/ppermute | solution.py:40
  54.0 49.5 %collective-permute-start.6 = (bf16[2,128,1024]{2,1,0:T(8,128)(2,1)}, bf16[2,128,1024]{2,1,0:T(8,128)(2,1)}, u32[]{:S(2)}, u32[]{:S(2)}) collective-permute-start(bf16[2,128,1024]{2,1,0:T(8,128)(2,1)} %get-tuple-element.55), channel_id=1, source_target_pairs={{0,8},{8,0},{16,24},{24,16},{32,40},{40,32},{48,56},{56,48},{64,72... | collective-permute-start | bytes 1572872 | tf_op jit(solution)/shard_map/ppermute | solution.py:40
  54.2 49.3 %collective-permute-start.7 = (bf16[2,128,1024]{2,1,0:T(8,128)(2,1)}, bf16[2,128,1024]{2,1,0:T(8,128)(2,1)}, u32[]{:S(2)}, u32[]{:S(2)}) collective-permute-start(bf16[2,128,1024]{2,1,0:T(8,128)(2,1)} %get-tuple-element.57), channel_id=1, source_target_pairs={{0,64},{8,72},{16,80},{24,88},{32,96},{40,104},{48,112},{56,120},{... | collective-permute-start | bytes 1572872 | tf_op jit(solution)/shard_map/ppermute | solution.py:40
  55.4 48.1 %collective-permute-start.8 = (bf16[2,128,1024]{2,1,0:T(8,128)(2,1)}, bf16[2,128,1024]{2,1,0:T(8,128)(2,1)}, u32[]{:S(2)}, u32[]{:S(2)}) collective-permute-start(bf16[2,128,1024]{2,1,0:T(8,128)(2,1)} %get-tuple-element.59), channel_id=1, source_target_pairs={{0,72},{8,64},{16,88},{24,80},{32,104},{40,96},{48,120},{56,112},{... | collective-permute-start | bytes 1572872 | tf_op jit(solution)/shard_map/ppermute | solution.py:40
  56.1 34.4 %all-to-all-start.1 = ((bf16[16,2,128,128]{3,2,1,0:T(8,128)(2,1)}), bf16[16,2,128,128]{3,2,1,0:T(8,128)(2,1)S(1)}, u32[]{:S(2)}, u32[]{:S(2)}) async-start(bf16[16,2,128,128]{3,2,1,0:T(8,128)(2,1)} %bitcast.14), calls=%async_computation.1 | async-start | bytes 2097152 | tf_op jit(solution)/shard_map/all_to_all | solution.py:33
  90.5 37.9 %all-to-all-start.2 = ((bf16[16,2,128,128]{3,2,1,0:T(8,128)(2,1)}), bf16[16,2,128,128]{3,2,1,0:T(8,128)(2,1)S(1)}, u32[]{:S(2)}, u32[]{:S(2)}) async-start(bf16[16,2,128,128]{3,2,1,0:T(8,128)(2,1)} %copy-done.5), calls=%async_computation.2 | async-start | bytes 2097152 | tf_op jit(solution)/shard_map/all_to_all | solution.py:33
  128.4 56.8 %all-to-all-start.3 = ((bf16[16,2,128,128]{3,2,1,0:T(8,128)(2,1)}), bf16[16,2,128,128]{3,2,1,0:T(8,128)(2,1)S(1)}, u32[]{:S(2)}, u32[]{:S(2)}) async-start(bf16[16,2,128,128]{3,2,1,0:T(8,128)(2,1)} %copy-done.4), calls=%async_computation.3 | async-start | bytes 2097152 | tf_op jit(solution)/shard_map/all_to_all | solution.py:33
  143.2 37.0 %copy-start.28 = (bf16[32,32,128]{2,1,0:T(8,128)(2,1)}, bf16[32,32,128]{2,1,0:T(8,128)(2,1)S(1)}, u32[]{:S(2)}) copy-start(bf16[32,32,128]{2,1,0:T(8,128)(2,1)S(1)} %get-tuple-element.74) | copy-start | bytes 786436
  143.3 14.8 %collective-permute-start.12 = (bf16[1024,128]{1,0:T(8,128)(2,1)S(1)}, bf16[1024,128]{1,0:T(8,128)(2,1)S(1)}, u32[]{:S(2)}, u32[]{:S(2)}) collective-permute-start(bf16[1024,128]{1,0:T(8,128)(2,1)S(1)} %bitcast.48), channel_id=1, source_target_pairs={{0,2},{1,3},{2,4},{3,5},{4,6},{5,7},{6,0},{7,1},{8,10},{9,11},{10,... | collective-permute-start | bytes 786440 | tf_op jit(solution)/shard_map/ppermute | solution.py:49
  143.4 15.5 %collective-permute-start.13 = (bf16[1024,128]{1,0:T(8,128)(2,1)S(1)}, bf16[1024,128]{1,0:T(8,128)(2,1)S(1)}, u32[]{:S(2)}, u32[]{:S(2)}) collective-permute-start(bf16[1024,128]{1,0:T(8,128)(2,1)S(1)} %bitcast.47), channel_id=1, source_target_pairs={{0,4},{1,5},{2,6},{3,7},{4,0},{5,1},{6,2},{7,3},{8,12},{9,13},{10,... | collective-permute-start | bytes 786440 | tf_op jit(solution)/shard_map/ppermute | solution.py:49
  143.5 15.5 %collective-permute-start.14 = (bf16[1024,128]{1,0:T(8,128)(2,1)S(1)}, bf16[1024,128]{1,0:T(8,128)(2,1)S(1)}, u32[]{:S(2)}, u32[]{:S(2)}) collective-permute-start(bf16[1024,128]{1,0:T(8,128)(2,1)S(1)} %bitcast.46), channel_id=1, source_target_pairs={{0,6},{1,7},{2,0},{3,1},{4,2},{5,3},{6,4},{7,5},{8,14},{9,15},{10,... | collective-permute-start | bytes 786440 | tf_op jit(solution)/shard_map/ppermute | solution.py:49
  146.0 14.3 %collective-permute-start.15 = (bf16[1024,128]{1,0:T(8,128)(2,1)S(1)}, bf16[1024,128]{1,0:T(8,128)(2,1)S(1)}, u32[]{:S(2)}, u32[]{:S(2)}) collective-permute-start(bf16[1024,128]{1,0:T(8,128)(2,1)S(1)} %bitcast.43), channel_id=1, source_target_pairs={{0,8},{1,9},{2,10},{3,11},{4,12},{5,13},{6,14},{7,15},{8,0},{9,1},... | collective-permute-start | bytes 786440 | tf_op jit(solution)/shard_map/ppermute | solution.py:49
  158.1 22.2 %copy-start.30 = (bf16[1024,128]{1,0:T(8,128)(2,1)}, bf16[1024,128]{1,0:T(8,128)(2,1)S(1)}, u32[]{:S(2)}) copy-start(bf16[1024,128]{1,0:T(8,128)(2,1)S(1)} %collective-permute-done.12.refs_1_) | copy-start | bytes 786436
  158.1 5.4 %collective-permute-start.16 = (bf16[1024,128]{1,0:T(8,128)(2,1)S(1)}, bf16[1024,128]{1,0:T(8,128)(2,1)S(1)}, u32[]{:S(2)}, u32[]{:S(2)}) collective-permute-start(bf16[1024,128]{1,0:T(8,128)(2,1)S(1)} %collective-permute-done.12.refs_1_), channel_id=1, source_target_pairs={{0,8},{1,9},{2,10},{3,11},{4,12},{5,13},{6,14},{7,15},{8,0},{9,1},... | collective-permute-start | bytes 786440 | tf_op jit(solution)/shard_map/ppermute | solution.py:49
  158.9 21.4 %copy-start.32 = (bf16[1024,128]{1,0:T(8,128)(2,1)}, bf16[1024,128]{1,0:T(8,128)(2,1)S(1)}, u32[]{:S(2)}) copy-start(bf16[1024,128]{1,0:T(8,128)(2,1)S(1)} %collective-permute-done.13.refs_2_) | copy-start | bytes 786436
  158.9 4.6 %collective-permute-start.17 = (bf16[1024,128]{1,0:T(8,128)(2,1)S(1)}, bf16[1024,128]{1,0:T(8,128)(2,1)S(1)}, u32[]{:S(2)}, u32[]{:S(2)}) collective-permute-start(bf16[1024,128]{1,0:T(8,128)(2,1)S(1)} %collective-permute-done.13.refs_2_), channel_id=1, source_target_pairs={{0,8},{1,9},{2,10},{3,11},{4,12},{5,13},{6,14},{7,15},{8,0},{9,1},... | collective-permute-start | bytes 786440 | tf_op jit(solution)/shard_map/ppermute | solution.py:49
  159.0 21.3 %copy-start.34 = (bf16[1024,128]{1,0:T(8,128)(2,1)}, bf16[1024,128]{1,0:T(8,128)(2,1)S(1)}, u32[]{:S(2)}) copy-start(bf16[1024,128]{1,0:T(8,128)(2,1)S(1)} %collective-permute-done.14.refs_3_) | copy-start | bytes 786436
  159.0 5.2 %collective-permute-start.18 = (bf16[1024,128]{1,0:T(8,128)(2,1)S(1)}, bf16[1024,128]{1,0:T(8,128)(2,1)S(1)}, u32[]{:S(2)}, u32[]{:S(2)}) collective-permute-start(bf16[1024,128]{1,0:T(8,128)(2,1)S(1)} %collective-permute-done.14.refs_3_), channel_id=1, source_target_pairs={{0,8},{1,9},{2,10},{3,11},{4,12},{5,13},{6,14},{7,15},{8,0},{9,1},... | collective-permute-start | bytes 786440 | tf_op jit(solution)/shard_map/ppermute | solution.py:49
  160.2 14.7 %collective-permute-start.19 = (bf16[128,256]{1,0:T(8,128)(2,1)S(1)}, bf16[128,256]{1,0:T(8,128)(2,1)S(1)}, u32[]{:S(2)}, u32[]{:S(2)}) collective-permute-start(bf16[128,256]{1,0:T(8,128)(2,1)S(1)} %get-tuple-element.78.refs_8_), channel_id=1, source_target_pairs={{0,2},{1,3},{2,4},{3,5},{4,6},{5,7},{6,0},{7,1},{8,10},{9,11},{10,... | collective-permute-start | bytes 196616 | tf_op jit(solution)/shard_map/ppermute | solution.py:49
  160.3 15.0 %collective-permute-start.20 = (bf16[128,256]{1,0:T(8,128)(2,1)S(1)}, bf16[128,256]{1,0:T(8,128)(2,1)S(1)}, u32[]{:S(2)}, u32[]{:S(2)}) collective-permute-start(bf16[128,256]{1,0:T(8,128)(2,1)S(1)} %get-tuple-element.78.refs_8_), channel_id=1, source_target_pairs={{0,4},{1,5},{2,6},{3,7},{4,0},{5,1},{6,2},{7,3},{8,12},{9,13},{10,... | collective-permute-start | bytes 196616 | tf_op jit(solution)/shard_map/ppermute | solution.py:49
  163.5 14.0 %collective-permute-start.21 = (bf16[128,256]{1,0:T(8,128)(2,1)S(1)}, bf16[128,256]{1,0:T(8,128)(2,1)S(1)}, u32[]{:S(2)}, u32[]{:S(2)}) collective-permute-start(bf16[128,256]{1,0:T(8,128)(2,1)S(1)} %get-tuple-element.78.refs_8_), channel_id=1, source_target_pairs={{0,6},{1,7},{2,0},{3,1},{4,2},{5,3},{6,4},{7,5},{8,14},{9,15},{10,... | collective-permute-start | bytes 196616 | tf_op jit(solution)/shard_map/ppermute | solution.py:49
  163.5 14.0 %collective-permute-start.22 = (bf16[128,256]{1,0:T(8,128)(2,1)S(1)}, bf16[128,256]{1,0:T(8,128)(2,1)S(1)}, u32[]{:S(2)}, u32[]{:S(2)}) collective-permute-start(bf16[128,256]{1,0:T(8,128)(2,1)S(1)} %get-tuple-element.79), channel_id=1, source_target_pairs={{0,8},{1,9},{2,10},{3,11},{4,12},{5,13},{6,14},{7,15},{8,0},{9,1},... | collective-permute-start | bytes 196616 | tf_op jit(solution)/shard_map/ppermute | solution.py:49
  164.2 14.1 %collective-permute-start.23 = (bf16[128,256]{1,0:T(8,128)(2,1)S(1)}, bf16[128,256]{1,0:T(8,128)(2,1)S(1)}, u32[]{:S(2)}, u32[]{:S(2)}) collective-permute-start(bf16[128,256]{1,0:T(8,128)(2,1)S(1)} %get-tuple-element.79), channel_id=1, source_target_pairs={{0,10},{1,11},{2,12},{3,13},{4,14},{5,15},{6,8},{7,9},{8,2},{9,3},... | collective-permute-start | bytes 196616 | tf_op jit(solution)/shard_map/ppermute | solution.py:49
  174.8 5.4 %collective-permute-start.24 = (bf16[128,256]{1,0:T(8,128)(2,1)S(1)}, bf16[128,256]{1,0:T(8,128)(2,1)S(1)}, u32[]{:S(2)}, u32[]{:S(2)}) collective-permute-start(bf16[128,256]{1,0:T(8,128)(2,1)S(1)} %get-tuple-element.79), channel_id=1, source_target_pairs={{0,12},{1,13},{2,14},{3,15},{4,8},{5,9},{6,10},{7,11},{8,4},{9,5},... | collective-permute-start | bytes 196616 | tf_op jit(solution)/shard_map/ppermute | solution.py:49
  175.3 5.0 %collective-permute-start.25 = (bf16[128,256]{1,0:T(8,128)(2,1)S(1)}, bf16[128,256]{1,0:T(8,128)(2,1)S(1)}, u32[]{:S(2)}, u32[]{:S(2)}) collective-permute-start(bf16[128,256]{1,0:T(8,128)(2,1)S(1)} %get-tuple-element.79), channel_id=1, source_target_pairs={{0,14},{1,15},{2,8},{3,9},{4,10},{5,11},{6,12},{7,13},{8,6},{9,7},... | collective-permute-start | bytes 196616 | tf_op jit(solution)/shard_map/ppermute | solution.py:49
  185.2 30.1 %all-to-all-start.4 = ((bf16[64,16,256]{2,1,0:T(8,128)(2,1)}), bf16[64,16,256]{2,1,0:T(8,128)(2,1)S(1)}, u32[]{:S(2)}, u32[]{:S(2)}) async-start(bf16[64,16,256]{2,1,0:T(8,128)(2,1)} %bitcast.27), calls=%async_computation.4 | async-start | bytes 1048576 | tf_op jit(solution)/shard_map/all_to_all | solution.py:33
  192.3 7.0 %collective-permute-start.26 = (bf16[128,256]{1,0:T(8,128)(2,1)S(1)}, bf16[128,256]{1,0:T(8,128)(2,1)S(1)}, u32[]{:S(2)}, u32[]{:S(2)}) collective-permute-start(bf16[128,256]{1,0:T(8,128)(2,1)S(1)} %get-tuple-element.80.refs_8_), channel_id=1, source_target_pairs={{0,2},{1,3},{2,4},{3,5},{4,6},{5,7},{6,0},{7,1},{8,10},{9,11},{10,... | collective-permute-start | bytes 196616 | tf_op jit(solution)/shard_map/ppermute | solution.py:49
  194.3 6.1 %collective-permute-start.27 = (bf16[128,256]{1,0:T(8,128)(2,1)S(1)}, bf16[128,256]{1,0:T(8,128)(2,1)S(1)}, u32[]{:S(2)}, u32[]{:S(2)}) collective-permute-start(bf16[128,256]{1,0:T(8,128)(2,1)S(1)} %get-tuple-element.80.refs_8_), channel_id=1, source_target_pairs={{0,4},{1,5},{2,6},{3,7},{4,0},{5,1},{6,2},{7,3},{8,12},{9,13},{10,... | collective-permute-start | bytes 196616 | tf_op jit(solution)/shard_map/ppermute | solution.py:49
  196.5 5.6 %collective-permute-start.28 = (bf16[128,256]{1,0:T(8,128)(2,1)S(1)}, bf16[128,256]{1,0:T(8,128)(2,1)S(1)}, u32[]{:S(2)}, u32[]{:S(2)}) collective-permute-start(bf16[128,256]{1,0:T(8,128)(2,1)S(1)} %get-tuple-element.80.refs_8_), channel_id=1, source_target_pairs={{0,6},{1,7},{2,0},{3,1},{4,2},{5,3},{6,4},{7,5},{8,14},{9,15},{10,... | collective-permute-start | bytes 196616 | tf_op jit(solution)/shard_map/ppermute | solution.py:49
  196.8 28.5 %copy-start.23 = (bf16[128,1024]{1,0:T(8,128)(2,1)S(1)}, bf16[128,1024]{1,0:T(8,128)(2,1)}, u32[]{:S(2)}) copy-start(bf16[128,1024]{1,0:T(8,128)(2,1)} %copy-done.22) | copy-start | bytes 786436
  196.8 29.1 %copy-start.21 = (bf16[128,1024]{1,0:T(8,128)(2,1)S(1)}, bf16[128,1024]{1,0:T(8,128)(2,1)}, u32[]{:S(2)}) copy-start(bf16[128,1024]{1,0:T(8,128)(2,1)} %copy-done.20) | copy-start | bytes 786436
  196.8 30.4 %copy-start.19 = (bf16[128,1024]{1,0:T(8,128)(2,1)S(1)}, bf16[128,1024]{1,0:T(8,128)(2,1)}, u32[]{:S(2)}) copy-start(bf16[128,1024]{1,0:T(8,128)(2,1)} %copy-done.18) | copy-start | bytes 786436
  196.8 32.2 %copy-start.25 = (bf16[128,1024]{1,0:T(8,128)(2,1)S(1)}, bf16[128,1024]{1,0:T(8,128)(2,1)}, u32[]{:S(2)}) copy-start(bf16[128,1024]{1,0:T(8,128)(2,1)} %copy-done.24) | copy-start | bytes 786436
  196.8 59.0 %copy-start.7 = (bf16[128,1024]{1,0:T(8,128)(2,1)S(1)}, bf16[128,1024]{1,0:T(8,128)(2,1)}, u32[]{:S(2)}) copy-start(bf16[128,1024]{1,0:T(8,128)(2,1)} %copy-done.6) | copy-start | bytes 786436
  196.8 5.2 %collective-permute-start.29 = (bf16[128,256]{1,0:T(8,128)(2,1)S(1)}, bf16[128,256]{1,0:T(8,128)(2,1)S(1)}, u32[]{:S(2)}, u32[]{:S(2)}) collective-permute-start(bf16[128,256]{1,0:T(8,128)(2,1)S(1)} %get-tuple-element.81), channel_id=1, source_target_pairs={{0,8},{1,9},{2,10},{3,11},{4,12},{5,13},{6,14},{7,15},{8,0},{9,1},... | collective-permute-start | bytes 196616 | tf_op jit(solution)/shard_map/ppermute | solution.py:49
  198.0 5.3 %collective-permute-start.30 = (bf16[128,256]{1,0:T(8,128)(2,1)S(1)}, bf16[128,256]{1,0:T(8,128)(2,1)S(1)}, u32[]{:S(2)}, u32[]{:S(2)}) collective-permute-start(bf16[128,256]{1,0:T(8,128)(2,1)S(1)} %get-tuple-element.81), channel_id=1, source_target_pairs={{0,10},{1,11},{2,12},{3,13},{4,14},{5,15},{6,8},{7,9},{8,2},{9,3},... | collective-permute-start | bytes 196616 | tf_op jit(solution)/shard_map/ppermute | solution.py:49
  199.3 5.9 %collective-permute-start.31 = (bf16[128,256]{1,0:T(8,128)(2,1)S(1)}, bf16[128,256]{1,0:T(8,128)(2,1)S(1)}, u32[]{:S(2)}, u32[]{:S(2)}) collective-permute-start(bf16[128,256]{1,0:T(8,128)(2,1)S(1)} %get-tuple-element.81), channel_id=1, source_target_pairs={{0,12},{1,13},{2,14},{3,15},{4,8},{5,9},{6,10},{7,11},{8,4},{9,5},... | collective-permute-start | bytes 196616 | tf_op jit(solution)/shard_map/ppermute | solution.py:49
  200.4 5.2 %collective-permute-start.32 = (bf16[128,256]{1,0:T(8,128)(2,1)S(1)}, bf16[128,256]{1,0:T(8,128)(2,1)S(1)}, u32[]{:S(2)}, u32[]{:S(2)}) collective-permute-start(bf16[128,256]{1,0:T(8,128)(2,1)S(1)} %get-tuple-element.81), channel_id=1, source_target_pairs={{0,14},{1,15},{2,8},{3,9},{4,10},{5,11},{6,12},{7,13},{8,6},{9,7},... | collective-permute-start | bytes 196616 | tf_op jit(solution)/shard_map/ppermute | solution.py:49
  215.3 43.2 %all-to-all-start.5 = ((bf16[64,16,256]{2,1,0:T(8,128)(2,1)}), bf16[64,16,256]{2,1,0:T(8,128)(2,1)S(1)}, u32[]{:S(2)}, u32[]{:S(2)}) async-start(bf16[64,16,256]{2,1,0:T(8,128)(2,1)} %bitcast.29), calls=%async_computation.5 | async-start | bytes 1048576 | tf_op jit(solution)/shard_map/all_to_all | solution.py:33
  225.3 3.7 %collective-permute-start.3 = (bf16[128,1024]{1,0:T(8,128)(2,1)S(1)}, bf16[128,1024]{1,0:T(8,128)(2,1)S(1)}, u32[]{:S(2)}, u32[]{:S(2)}) collective-permute-start(bf16[128,1024]{1,0:T(8,128)(2,1)S(1)} %copy-done.23), channel_id=1, source_target_pairs={{0,8},{8,0},{16,24},{24,16},{32,40},{40,32},{48,56},{56,48},{64,72... | collective-permute-start | bytes 786440 | tf_op jit(solution)/shard_map/ppermute | solution.py:40
  225.9 11.6 %collective-permute-start.4 = (bf16[128,1024]{1,0:T(8,128)(2,1)S(1)}, bf16[128,1024]{1,0:T(8,128)(2,1)S(1)}, u32[]{:S(2)}, u32[]{:S(2)}) collective-permute-start(bf16[128,1024]{1,0:T(8,128)(2,1)S(1)} %copy-done.21), channel_id=1, source_target_pairs={{0,64},{8,72},{16,80},{24,88},{32,96},{40,104},{48,112},{56,120},{... | collective-permute-start | bytes 786440 | tf_op jit(solution)/shard_map/ppermute | solution.py:40
  227.2 17.8 %collective-permute-start.5 = (bf16[128,1024]{1,0:T(8,128)(2,1)S(1)}, bf16[128,1024]{1,0:T(8,128)(2,1)S(1)}, u32[]{:S(2)}, u32[]{:S(2)}) collective-permute-start(bf16[128,1024]{1,0:T(8,128)(2,1)S(1)} %copy-done.19), channel_id=1, source_target_pairs={{0,72},{8,64},{16,88},{24,80},{32,104},{40,96},{48,120},{56,112},{... | collective-permute-start | bytes 786440 | tf_op jit(solution)/shard_map/ppermute | solution.py:40
  227.6 17.3 %collective-permute-start.9 = (bf16[128,1024]{1,0:T(8,128)(2,1)}, bf16[128,1024]{1,0:T(8,128)(2,1)S(1)}, u32[]{:S(2)}, u32[]{:S(2)}) collective-permute-start(bf16[128,1024]{1,0:T(8,128)(2,1)} %copy-done.27), channel_id=1, source_target_pairs={{0,8},{8,0},{16,24},{24,16},{32,40},{40,32},{48,56},{56,48},{64,72... | collective-permute-start | bytes 786440 | tf_op jit(solution)/shard_map/ppermute | solution.py:40
  227.7 22.3 %collective-permute-start.10 = (bf16[128,1024]{1,0:T(8,128)(2,1)}, bf16[128,1024]{1,0:T(8,128)(2,1)S(1)}, u32[]{:S(2)}, u32[]{:S(2)}) collective-permute-start(bf16[128,1024]{1,0:T(8,128)(2,1)} %copy-done.26), channel_id=1, source_target_pairs={{0,64},{8,72},{16,80},{24,88},{32,96},{40,104},{48,112},{56,120},{... | collective-permute-start | bytes 786440 | tf_op jit(solution)/shard_map/ppermute | solution.py:40
  229.0 26.7 %collective-permute-start.11 = (bf16[128,1024]{1,0:T(8,128)(2,1)S(1)}, bf16[128,1024]{1,0:T(8,128)(2,1)S(1)}, u32[]{:S(2)}, u32[]{:S(2)}) collective-permute-start(bf16[128,1024]{1,0:T(8,128)(2,1)S(1)} %copy-done.25), channel_id=1, source_target_pairs={{0,72},{8,64},{16,88},{24,80},{32,104},{40,96},{48,120},{56,112},{... | collective-permute-start | bytes 786440 | tf_op jit(solution)/shard_map/ppermute | solution.py:40
  (37 other events, 136.3 us)

commit v3 on v2

--- a/solution.py
+++ b/solution.py
@@ -53,7 +53,7 @@
     return lax.optimization_barrier((array, *earlier))[0]
 
 
-def params(limit=48):
+def params(limit=12):
     return pltpu.CompilerParams(vmem_limit_bytes=limit * MIB)
 
 
@@ -102,33 +102,37 @@
 def query_prep_kernel(me_ref, q_ref, g_ref, cos_ref, sin_ref, valid_ref, *outs):
     cos, sin = cos_ref[...], sin_ref[...]
     keep = valid_ref[...] > 0.0
-    for delta in range(4):
-
-        @pl.when(pl.program_id(0) == delta)
+    for at, out in enumerate(outs):
+
+        @pl.when(pl.program_id(0) == at)
         def _():
             for h in range(REP):
                 cols = slice(h * D, (h + 1) * D)
                 q = turn(q_ref[:, cols].astype(jnp.float32), cos, sin)
-                outs[delta][0, :, cols] = q.astype(jnp.bfloat16)
+                out[0, :, cols] = q.astype(jnp.bfloat16)
                 g = jnp.where(keep, g_ref[:, cols].astype(jnp.float32), 0.0)
-                outs[delta][1, :, cols] = g.astype(jnp.bfloat16)
-
-
-def query_prep(part, quad, q, g, cos, sin, valid):
+                out[1, :, cols] = g.astype(jnp.bfloat16)
+
+
+def query_prep(part, deltas, quad, q, g, cos, sin, valid):
+    count, low = len(deltas), deltas[0]
+    first = part == 0 and low == 1
     table = pl.BlockSpec((TOK, D), lambda i, me: (0, 0))
-    column = pl.BlockSpec((TOK, REP * D), lambda i, me: (0, (me[0] ^ i) * PARTS + part))
+    column = pl.BlockSpec(
+        (TOK, REP * D), lambda i, me: (0, (me[0] ^ (i + low)) * PARTS + part)
+    )
     shape = jax.ShapeDtypeStruct((2, TOK, REP * D), jnp.bfloat16)
     return pl.pallas_call(
         query_prep_kernel,
         grid_spec=pltpu.PrefetchScalarGridSpec(
             num_scalar_prefetch=1,
-            grid=(4,),
+            grid=(count,),
             in_specs=[column, column, table, table, table],
-            out_specs=[pl.BlockSpec((2, TOK, REP * D), lambda i, me: (0, 0, 0))] * 4,
+            out_specs=[pl.BlockSpec((2, TOK, REP * D), lambda i, me: (0, 0, 0))] * count,
         ),
-        out_shape=[shape] * 4,
-        compiler_params=params(),
-        cost_estimate=cost(4 << 20, 4 * MIB),
+        out_shape=[shape] * count,
+        compiler_params=params(56 if first else 12),
+        cost_estimate=cost(count << 20, count * MIB),
         name="query_prep",
     )(quad, q, g, cos, sin, valid)
 
@@ -285,7 +289,7 @@
             pltpu.VMEM((CHUNKS, CHUNK, D), jnp.float32),
             pltpu.VMEM((D, ROWS), jnp.float32),
         ],
-        compiler_params=params(),
+        compiler_params=params(34),
         cost_estimate=cost(25 * 10**9, 6 * MIB),
         name="attention",
     )(meta, *qg, kv, cos, sin)
@@ -395,46 +399,54 @@
     total = dot(refs[0][...], refs[8][...], nn)
     for i in range(1, 8):
         total += dot(refs[i][...], refs[8 + i][...], nn)
-    refs[16][...] = total.astype(jnp.bfloat16)
-
-
-def project(xt, kg):
+    total = total.astype(jnp.bfloat16)
+    if len(refs) == 17:
+        refs[16][...] = total
+    else:
+        refs[17][:, : 2 * D] = refs[16][...]
+        refs[17][:, 2 * D :] = total
+
+
+def project(xt, kg, earlier=()):
+    width = 2 * D * (1 + len(earlier))
     return pl.pallas_call(
         project_kernel,
         grid=(2,),
         in_specs=[pl.BlockSpec((512, TOK), lambda i: (i, 0))] * 8
-        + [pl.BlockSpec((TOK, 2 * D), lambda i: (0, 0))] * 8,
-        out_specs=pl.BlockSpec((512, 2 * D), lambda i: (i, 0)),
-        out_shape=jax.ShapeDtypeStruct((1024, 2 * D), jnp.bfloat16),
+        + [pl.BlockSpec((TOK, 2 * D), lambda i: (0, 0))] * 8
+        + [pl.BlockSpec((512, 2 * D), lambda i: (i, 0))] * len(earlier),
+        out_specs=pl.BlockSpec((512, width), lambda i: (i, 0)),
+        out_shape=jax.ShapeDtypeStruct((1024, width), jnp.bfloat16),
         compiler_params=params(),
         cost_estimate=cost(10**9, 3 * MIB),
         name="project",
-    )(*xt, *kg)
-
-
-def final_sum_kernel(a_ref, b_ref, out_ref):
+    )(*xt, *kg, *earlier)
+
+
+def final_sum_kernel(in_ref, out_ref):
     for c in range(2):
-        for part, ref in enumerate((a_ref, b_ref)):
-            total = jnp.zeros((16, 2 * D), jnp.float32)
-            for s in range(16):
-                for zh in range(2):
-                    total += ref[s, c, zh].astype(jnp.float32)
+        total = jnp.zeros((16, PARTS * 2 * D), jnp.float32)
+        for s in range(16):
+            for zh in range(2):
+                total += in_ref[s, c, zh].astype(jnp.float32)
+        for part in range(PARTS):
             for side in range(2):
                 head = (2 * c + side) * PARTS + part
-                out_ref[:, head * D : (head + 1) * D] = total[:, side * D : (side + 1) * D]
-
-
-def final_sum(a, b):
+                at = (part * 2 + side) * D
+                out_ref[:, head * D : (head + 1) * D] = total[:, at : at + D]
+
+
+def final_sum(pieces):
     vmem = pl.BlockSpec(memory_space=pltpu.VMEM)
     return pl.pallas_call(
         final_sum_kernel,
-        in_specs=[vmem] * 2,
+        in_specs=[vmem],
         out_specs=vmem,
         out_shape=jax.ShapeDtypeStruct((16, 1024), jnp.float32),
         compiler_params=params(),
         cost_estimate=cost(1 << 20, MIB),
         name="final_sum",
-    )(a.reshape(16, 2, 2, 16, 2 * D), b.reshape(16, 2, 2, 16, 2 * D))
+    )(pieces.reshape(16, 2, 2, 16, PARTS * 2 * D))
 
 
 def local(q, k, v, g, x, group_first, seq_length, pos_offset):
@@ -477,35 +489,46 @@
     def quad_swap(pieces):
         return [pieces[0]] + [quad_send(pieces[d], d) for d in range(1, 4)]
 
-    kv_out = [a.reshape(16, 2, TOK, D) for a in key_prep(k[0], v[0], cos, sin)]
-    qg_out = [
-        query_prep(part, quad_at, q[0], g[0], cos, sin, valid) for part in range(PARTS)
-    ]
-    qg_in = [quad_swap(qg_out[0])]
+    def query_pieces(part, deltas):
+        return query_prep(part, deltas, quad_at, q[0], g[0], cos, sin, valid)
+
+    def quad_swap(pieces):
+        return [quad_send(piece, d + 1) for d, piece in enumerate(pieces)]
+
+    sent = query_pieces(0, (1, 2, 3))
+    qg_in = [quad_swap(sent)]
+    kv_out = key_prep(after(k[0], *sent), v[0], cos, sin)
+    kv_out = [a.reshape(16, 2, TOK, D) for a in kv_out]
     kv_in = [swap(kv_out[0], "sp", HALF_GROUPS)]
-    qg_in.append(quad_swap([after(piece, *qg_in[0]) for piece in qg_out[1]]))
+    xt = [a.reshape(1024, TOK) for a in input_prep(y_at, after(x[0], qg_in[0][0]))]
+    xt = [xt[0]] + [y_send(xt[step], step) for step in range(1, 4)]
+    qg_in[0] = list(query_pieces(0, (0,))) + qg_in[0]
+    kv_in[0] = after(kv_in[0], *xt)
+
+    own = query_pieces(1, (0,))
+    sent = query_pieces(1, (1, 2, 3))
+    qg_in.append(list(own) + quad_swap([after(piece, *qg_in[0]) for piece in sent]))
     kv_in.append(swap(after(kv_out[1], kv_in[0]), "sp", HALF_GROUPS))
-
-    xt = [a.reshape(1024, TOK) for a in input_prep(y_at, x[0])]
-    xt = [xt[0]] + [y_send(xt[step], step) for step in range(1, 4)]
     xt = xt + [y_send(a, 0, 1) for a in xt]
+    kv_in[1] = after(kv_in[1], *xt)
 
     dq_back, dkv_back = [], []
     for part in range(PARTS):
         *dq, dkv = attention(meta, qg_in[part], kv_in[part], cos_t, sin_t)
         dkv_back.append(swap(dkv, "sp", HALF_GROUPS))
-        dq_back.append(quad_swap(dq))
-
-    dk, dv, pieces = [], [], []
+        dq_back.append([dq[0]] + quad_swap(dq[1:]))
+
+    dk, dv, partial = [], [], ()
     for part in range(PARTS):
-        dk_part, dv_part, same, other = key_post(core_at, dkv_back[part], cos, sin)
+        back = after(dkv_back[part], *dq_back[part])
+        dk_part, dv_part, same, other = key_post(core_at, back, cos, sin)
         dk.append(dk_part)
         dv.append(dv_part)
         kg = [same] + [y_send(same, step) for step in range(1, 4)]
         kg += [y_send(other, step, 1) for step in range(4)]
-        partial = project(xt, kg).reshape(64, 16, 2 * D)
-        pieces.append(swap(partial, ("sp", "dp"), PLANE_GROUPS))
-    kproj_grad = final_sum(*pieces)
+        partial = (project(xt, kg, partial),)
+    pieces = swap(partial[0].reshape(64, 16, 4 * D), ("sp", "dp"), PLANE_GROUPS)
+    kproj_grad = final_sum(pieces)
     key_gradient, value_gradient = join(*dk, *dv)
     query_grad = query_post(quad_at, *dq_back)
     return (query_grad[None], key_gradient[None], value_gradient[None], kproj_grad)

time: 265 us -> 242 us (0.913); the launches traced: 260 us -> 240 us
  starting transfers between devices: 98.3 us -> 78.1 us
  local copies, waits for them, and re-layouts: 28.9 us -> 14.9 us
  waiting for transfers between devices: 75.2 us -> 83.9 us
  Pallas kernels: 51.9 us -> 57.5 us
    all_to_all x6 -> x5, waiting for transfers between devices: 11.4 us -> 41.5 us  [swap(): lax.all_to_all(array, axes, split_axis=0, concat_axis=0, axis_index_group...]
    ppermute x21, waiting for transfers between devices: 17.7 us -> 0.55 us  [y_send(): return lax.ppermute(array, ('sp', 'dp'), pairs)]
    unnamed x92 -> x64, local copies, waits for them, and re-layouts: 24.6 us -> 10.2 us
    all_to_all x6 -> x5, starting transfers between devices: 57.7 us -> 46 us  [swap(): lax.all_to_all(array, axes, split_axis=0, concat_axis=0, axis_index_group...]
    ppermute x21, starting transfers between devices: 31.9 us -> 23.8 us  [y_send(): return lax.ppermute(array, ('sp', 'dp'), pairs)]
    ppermute x12, waiting for transfers between devices: 46.1 us -> 41.9 us  [quad_send(): return lax.ppermute(array, 'sp', [(s, s ^ flip) for s in range(SP)])]
    pallas_call x2 -> x4, Pallas kernels: 7.99 us -> 6.59 us  [query_prep(): pl.pallas_call(query_prep_kernel, grid_spec=pltpu.PrefetchScalarGridSpec(...]
  transfers between devices with their start and end apart: 39 -> 38, of which waited for: 14 -> 9; matrix products, arithmetic and copies ran while one was open for 2% -> 1% of each run, Pallas kernels for 19% -> 20%
where the time goes in v3:
time: 242 us; the launch traced here: 240 us
  waiting for transfers between devices  83.9 us (35%)
  starting transfers between devices  78.1 us (32%)
  Pallas kernels  57.5 us (24%)
  local copies, waits for them, and re-layouts  14.9 us (6%)
  other arithmetic  3.9 us (2%)
    all_to_all x5, starting transfers between devices, swap(): lax.all_to_all(array, axes, split_axis=0, concat_axis=0, axis_index_group...  46 us
    ppermute x12, waiting for transfers between devices, quad_send(): return lax.ppermute(array, 'sp', [(s, s ^ flip) for s in range(SP)])  41.9 us
    all_to_all x5, waiting for transfers between devices, swap(): lax.all_to_all(array, axes, split_axis=0, concat_axis=0, axis_index_group...  41.5 us
    pallas_call x2, Pallas kernels, attention(): pl.pallas_call(attention_kernel, grid=(REP // STACK,), in_specs=[pl.Block...  34.1 us
    ppermute x21, starting transfers between devices, y_send(): return lax.ppermute(array, ('sp', 'dp'), pairs)  23.8 us
    unnamed x64, local copies, waits for them, and re-layouts  10.2 us
    ppermute x12, starting transfers between devices, quad_send(): return lax.ppermute(array, 'sp', [(s, s ^ flip) for s in range(SP)])  8.29 us
    pallas_call x4, Pallas kernels, query_prep(): pl.pallas_call(query_prep_kernel, grid_spec=pltpu.PrefetchScalarGridSpec(...  6.59 us
  transfers between devices with their start and end apart: 38, of which 9 were waited for; matrix products, arithmetic and copies ran while one was open for 1% of the time, Pallas kernels for 20%

profile of v3, /device:TPU:1, one launch (start us, length us, event | category | flops | bytes accessed | tf_op | source)
XLA Modules:
  0.0 240.1 jit_solution(5009002102571693967)
XLA Ops:
  0.7 1.3 constant_dynamic-slice_fusion
  4.2 0.7 pad_maximum_fusion.cos_ref
  5.6 0.7 pad_maximum_fusion.1.sin_ref
  6.3 0.7 broadcast_in_dim.8.valid_ref
  7.0 3.9 %query_prep.5 = (bf16[2,128,1024]{2,1,0:T(8,128)(2,1)}, bf16[2,128,1024]{2,1,0:T(8,128)(2,1)}, bf16[2,128,1024]{2,1,0:T(8,128)(2,1)}) custom-call(s32[1]{0:T(128)} %bitcast.me_ref, bf16[128,8192]{1,0:T(8,128)(2,1)} %bitcast.31, bf16[128,8192]{1,0:T(8,128)(2,1)} %bitcast.35, f32[128,128]{1,0:T(8,128)} %pad_maximum_fusion.cos_ref, ...), custom_call_target="tpu_custom_call" | custom-call | flops 3145728 | bytes 3145728 | tf_op jit(solution)/shard_map/query_prep/pallas_call | solution.py:125
  10.9 2.0 key_prep.1
  12.9 1.0 copy-done.7
  13.9 8.5 %all-to-all-start = ((bf16[16,2,128,128]{3,2,1,0:T(8,128)(2,1)}), bf16[16,2,128,128]{3,2,1,0:T(8,128)(2,1)}, u32[]{:S(2)}, u32[]{:S(2)}) async-start(bf16[16,2,128,128]{3,2,1,0:T(8,128)(2,1)} %bitcast.43), calls=%async_computation | async-start | bytes 2097152 | tf_op jit(solution)/shard_map/all_to_all | solution.py:33
  22.6 1.5 collective-permute-start.1
  26.9 3.1 %input_prep.1 = (bf16[32,32,128]{2,1,0:T(8,128)(2,1)}, bf16[32,32,128]{2,1,0:T(8,128)(2,1)S(1)}, bf16[32,32,128]{2,1,0:T(8,128)(2,1)S(1)}, bf16[32,32,128]{2,1,0:T(8,128)(2,1)S(1)}) custom-call(s32[1]{0:T(128)} %bitcast.13.me_ref, bf16[128,4096]{1,0:T(8,128)(2,1)S(1)} %bitcast.42), custom_call_target="tpu_custom_call" | custom-call | flops 1048576 | bytes 2097152 | tf_op jit(solution)/shard_map/input_prep/pallas_call | solution.py:150
  30.0 1.3 collective-permute-start.3
  31.4 2.7 %collective-permute-start.4 = (bf16[1024,128]{1,0:T(8,128)(2,1)S(1)}, bf16[1024,128]{1,0:T(8,128)(2,1)}, u32[]{:S(2)}, u32[]{:S(2)}) collective-permute-start(bf16[1024,128]{1,0:T(8,128)(2,1)S(1)} %bitcast.47), channel_id=1, source_target_pairs={{0,4},{1,5},{2,6},{3,7},{4,0},{5,1},{6,2},{7,3},{8,12},{9,13},{10,... | collective-permute-start | bytes 786440 | tf_op jit(solution)/shard_map/ppermute | solution.py:49
  34.1 1.1 collective-permute-start.5
  35.2 12.2 %collective-permute-done.1.refs_2_ = bf16[2,128,1024]{2,1,0:T(8,128)(2,1)} collective-permute-done((bf16[2,128,1024]{2,1,0:T(8,128)(2,1)}, bf16[2,128,1024]{2,1,0:T(8,128)(2,1)}, u32[]{:S(2)}, u32[]{:S(2)}) %collective-permute-start.1) | collective-permute-done | bytes 524320 | tf_op jit(solution)/shard_map/ppermute | solution.py:40
  47.3 1.3 collective-permute-start.12
  48.8 1.6 copy-done.2
  51.0 2.2 query_prep.7
  53.7 5.1 %collective-permute-done.2.refs_3_ = bf16[2,128,1024]{2,1,0:T(8,128)(2,1)} collective-permute-done((bf16[2,128,1024]{2,1,0:T(8,128)(2,1)}, bf16[2,128,1024]{2,1,0:T(8,128)(2,1)}, u32[]{:S(2)}, u32[]{:S(2)}) %collective-permute-start.2) | collective-permute-done | bytes 524320 | tf_op jit(solution)/shard_map/ppermute | solution.py:40
  58.9 1.7 collective-permute-start.11
  60.6 5.5 %all-to-all-start.1 = ((bf16[16,2,128,128]{3,2,1,0:T(8,128)(2,1)}), bf16[16,2,128,128]{3,2,1,0:T(8,128)(2,1)S(1)}, u32[]{:S(2)}, u32[]{:S(2)}) async-start(bf16[16,2,128,128]{3,2,1,0:T(8,128)(2,1)} %bitcast.20), calls=%async_computation.1 | async-start | bytes 2097152 | tf_op jit(solution)/shard_map/all_to_all | solution.py:33
  66.7 17.2 %attention.2 = (bf16[128,1024]{1,0:T(8,128)(2,1)S(1)}, bf16[128,1024]{1,0:T(8,128)(2,1)}, bf16[128,1024]{1,0:T(8,128)(2,1)}, bf16[128,1024]{1,0:T(8,128)(2,1)S(1)}, bf16[16,2,128,128]{3,2,1,0:T(8,128)(2,1)}) custom-call(s32[2,4]{1,0:T(2,128)S(1)} %add_add_fusion.meta_ref, bf16[2,128,1024]{2,1,0:T(8,128)(2,1)S(1)} %query_prep.4.refs_0_, ...), custom_call_target="tpu_custom_call" | custom-call | flops 24999999488 | bytes 6291456 | tf_op jit(solution)/shard_map/attention/pallas_call | solution.py:274
  85.4 9.7 %all-to-all-done.1.refs_4_ = bf16[16,2,128,128]{3,2,1,0:T(8,128)(2,1)S(1)} async-done(((bf16[16,2,128,128]{3,2,1,0:T(8,128)(2,1)}), bf16[16,2,128,128]{3,2,1,0:T(8,128)(2,1)S(1)}, u32[]{:S(2)}, u32[]{:S(2)}) %all-to-all-start.1) | async-done | bytes 1048608 | tf_op jit(solution)/shard_map/all_to_all | solution.py:33
  95.1 9.2 %all-to-all-start.2 = ((bf16[16,2,128,128]{3,2,1,0:T(8,128)(2,1)}), bf16[16,2,128,128]{3,2,1,0:T(8,128)(2,1)S(1)}, u32[]{:S(2)}, u32[]{:S(2)}) async-start(bf16[16,2,128,128]{3,2,1,0:T(8,128)(2,1)} %get-tuple-element.74), calls=%async_computation.2 | async-start | bytes 2097152 | tf_op jit(solution)/shard_map/all_to_all | solution.py:33
  104.3 16.8 %attention.3 = (bf16[128,1024]{1,0:T(8,128)(2,1)S(1)}, bf16[128,1024]{1,0:T(8,128)(2,1)S(1)}, bf16[128,1024]{1,0:T(8,128)(2,1)S(1)}, bf16[128,1024]{1,0:T(8,128)(2,1)S(1)}, bf16[16,2,128,128]{3,2,1,0:T(8,128)(2,1)}) custom-call(s32[2,4]{1,0:T(2,128)S(1)} %add_add_fusion.meta_ref, bf16[2,128,1024]{2,1,0:T(8,128)(2,1)S(1)} %query_prep.6.refs_0_, ...), custom_call_target="tpu_custom_call" | custom-call | flops 24999999488 | bytes 6291456 | tf_op jit(solution)/shard_map/attention/pallas_call | solution.py:274
  123.3 6.0 %all-to-all-done.2 = bf16[16,2,128,128]{3,2,1,0:T(8,128)(2,1)S(1)} async-done(((bf16[16,2,128,128]{3,2,1,0:T(8,128)(2,1)}), bf16[16,2,128,128]{3,2,1,0:T(8,128)(2,1)S(1)}, u32[]{:S(2)}, u32[]{:S(2)}) %all-to-all-start.2) | async-done | bytes 1048608 | tf_op jit(solution)/shard_map/all_to_all | solution.py:33
  129.3 12.8 %all-to-all-start.3 = ((bf16[16,2,128,128]{3,2,1,0:T(8,128)(2,1)}), bf16[16,2,128,128]{3,2,1,0:T(8,128)(2,1)S(1)}, u32[]{:S(2)}, u32[]{:S(2)}) async-start(bf16[16,2,128,128]{3,2,1,0:T(8,128)(2,1)} %get-tuple-element.77), calls=%async_computation.3 | async-start | bytes 2097152 | tf_op jit(solution)/shard_map/all_to_all | solution.py:33
  142.2 1.6 collective-permute-start.7
  144.3 1.4 collective-permute-start.17
  146.3 12.1 %collective-permute-done.7.refs_2_ = bf16[128,1024]{1,0:T(8,128)(2,1)S(1)} collective-permute-done((bf16[128,1024]{1,0:T(8,128)(2,1)}, bf16[128,1024]{1,0:T(8,128)(2,1)S(1)}, u32[]{:S(2)}, u32[]{:S(2)}) %collective-permute-start.7) | collective-permute-done | bytes 262176 | tf_op jit(solution)/shard_map/ppermute | solution.py:40
  158.5 9.1 %collective-permute-done.8.refs_3_ = bf16[128,1024]{1,0:T(8,128)(2,1)S(1)} collective-permute-done((bf16[128,1024]{1,0:T(8,128)(2,1)}, bf16[128,1024]{1,0:T(8,128)(2,1)S(1)}, u32[]{:S(2)}, u32[]{:S(2)}) %collective-permute-start.8) | collective-permute-done | bytes 262176 | tf_op jit(solution)/shard_map/ppermute | solution.py:40
  167.5 1.3 key_post.2
  169.5 1.3 collective-permute-start.26
  171.5 2.4 collective-permute-start.28
  174.9 3.4 %collective-permute-done.18.refs_7_ = bf16[128,1024]{1,0:T(8,128)(2,1)S(1)} collective-permute-done((bf16[128,1024]{1,0:T(8,128)(2,1)}, bf16[128,1024]{1,0:T(8,128)(2,1)S(1)}, u32[]{:S(2)}, u32[]{:S(2)}) %collective-permute-start.18) | collective-permute-done | bytes 262176 | tf_op jit(solution)/shard_map/ppermute | solution.py:40
  179.0 1.4 collective-permute-start.30
  182.4 2.6 %collective-permute-start.32 = (bf16[128,256]{1,0:T(8,128)(2,1)}, bf16[128,256]{1,0:T(8,128)(2,1)S(1)}, u32[]{:S(2)}, u32[]{:S(2)}) collective-permute-start(bf16[128,256]{1,0:T(8,128)(2,1)} %get-tuple-element.87), channel_id=1, source_target_pairs={{0,14},{1,15},{2,8},{3,9},{4,10},{5,11},{6,12},{7,13},{8,6},{9,7},... | collective-permute-start | bytes 196616 | tf_op jit(solution)/shard_map/ppermute | solution.py:49
  185.0 2.1 collective-permute-start.20
  187.1 1.4 collective-permute-start.21
  188.5 1.1 collective-permute-start.22
  190.3 2.3 collective-permute-start.24
  192.6 1.7 collective-permute-start.25
  194.3 2.7 %project.2.refs_16_ = bf16[1024,256]{1,0:T(8,128)(2,1)S(1)} custom-call(bf16[1024,128]{1,0:T(8,128)(2,1)} %bitcast.15.refs_0_, bf16[1024,128]{1,0:T(8,128)(2,1)} %collective-permute-done.3.refs_1_, bf16[1024,128]{1,0:T(8,128)(2,1)} %collective-permute-done.4.refs_2_, bf16[1024,128]{1,0:T(8,128)(2,1)} %collective-permute-done.5.refs_3_, ...), custom_call_target="tpu_custom_call" | custom-call | flops 1000000000 | bytes 3145728 | tf_op jit(solution)/shard_map/project/pallas_call | solution.py:412
  197.1 3.5 %project.3 = bf16[1024,512]{1,0:T(8,128)(2,1)} custom-call(bf16[1024,128]{1,0:T(8,128)(2,1)} %bitcast.15.refs_0_, bf16[1024,128]{1,0:T(8,128)(2,1)} %collective-permute-done.3.refs_1_, bf16[1024,128]{1,0:T(8,128)(2,1)} %collective-permute-done.4.refs_2_, bf16[1024,128]{1,0:T(8,128)(2,1)} %collective-permute-done.5.refs_3_, ...), custom_call_target="tpu_custom_call" | custom-call | flops 1000000000 | bytes 3145728 | tf_op jit(solution)/shard_map/project/pallas_call | solution.py:412
  200.6 10.0 %all-to-all-start.4 = ((bf16[64,16,512]{2,1,0:T(8,128)(2,1)}), bf16[64,16,512]{2,1,0:T(8,128)(2,1)S(1)}, u32[]{:S(2)}, u32[]{:S(2)}) async-start(bf16[64,16,512]{2,1,0:T(8,128)(2,1)} %bitcast.27), calls=%async_computation.4 | async-start | bytes 2097152 | tf_op jit(solution)/shard_map/all_to_all | solution.py:33
  210.8 1.9 query_post.1
  212.6 0.9 join.1
  213.6 25.7 %all-to-all-done.4 = bf16[64,16,512]{2,1,0:T(8,128)(2,1)S(1)} async-done(((bf16[64,16,512]{2,1,0:T(8,128)(2,1)}), bf16[64,16,512]{2,1,0:T(8,128)(2,1)S(1)}, u32[]{:S(2)}, u32[]{:S(2)}) %all-to-all-start.4) | async-done | bytes 1048608 | tf_op jit(solution)/shard_map/all_to_all | solution.py:33
  239.3 0.8 final_sum.1
  (131 shorter events, 17.9 us)
Async XLA Ops:
  10.9 13.8 %copy-start.30 = (s32[1,32]{1,0:T(1,128)S(1)}, s32[1,32]{1,0:T(1,128)}, u32[]{:S(2)}) copy-start(s32[1,32]{1,0:T(1,128)} %param.13) | copy-start | bytes 388
  10.9 15.2 %copy-start.31 = (s32[1,32]{1,0:T(1,128)S(1)}, s32[1,32]{1,0:T(1,128)}, u32[]{:S(2)}) copy-start(s32[1,32]{1,0:T(1,128)} %param.14) | copy-start | bytes 388
  10.9 16.0 %copy-start.6 = (bf16[1,128,4096]{2,1,0:T(8,128)(2,1)S(1)}, bf16[1,128,4096]{2,1,0:T(8,128)(2,1)}, u32[]{:S(2)}) copy-start(bf16[1,128,4096]{2,1,0:T(8,128)(2,1)} %param.12) | copy-start | bytes 3145732
  13.9 34.9 %copy-start.1 = (bf16[1,128,8192]{2,1,0:T(8,128)(2,1)S(1)}, bf16[1,128,8192]{2,1,0:T(8,128)(2,1)}, u32[]{:S(2)}) copy-start(bf16[1,128,8192]{2,1,0:T(8,128)(2,1)} %param.8) | copy-start | bytes 6291460
  13.9 34.9 %copy-start.5 = (f32[128,128]{1,0:T(8,128)S(1)}, f32[128,128]{1,0:T(8,128)}, u32[]{:S(2)}) copy-start(f32[128,128]{1,0:T(8,128)} %broadcast_in_dim.8.valid_ref) | copy-start | bytes 196612
  13.9 46.7 %all-to-all-start = ((bf16[16,2,128,128]{3,2,1,0:T(8,128)(2,1)}), bf16[16,2,128,128]{3,2,1,0:T(8,128)(2,1)}, u32[]{:S(2)}, u32[]{:S(2)}) async-start(bf16[16,2,128,128]{3,2,1,0:T(8,128)(2,1)} %bitcast.43), calls=%async_computation | async-start | bytes 2097152 | tf_op jit(solution)/shard_map/all_to_all | solution.py:33
  22.4 4.5 %collective-permute-start = (bf16[2,128,1024]{2,1,0:T(8,128)(2,1)}, bf16[2,128,1024]{2,1,0:T(8,128)(2,1)}, u32[]{:S(2)}, u32[]{:S(2)}) collective-permute-start(bf16[2,128,1024]{2,1,0:T(8,128)(2,1)} %get-tuple-element.46), channel_id=1, source_target_pairs={{0,8},{8,0},{16,24},{24,16},{32,40},{40,32},{48,56},{56,48},{64,72... | collective-permute-start | bytes 1572872 | tf_op jit(solution)/shard_map/ppermute | solution.py:40
  22.6 24.7 %collective-permute-start.1 = (bf16[2,128,1024]{2,1,0:T(8,128)(2,1)}, bf16[2,128,1024]{2,1,0:T(8,128)(2,1)}, u32[]{:S(2)}, u32[]{:S(2)}) collective-permute-start(bf16[2,128,1024]{2,1,0:T(8,128)(2,1)} %get-tuple-element.47), channel_id=1, source_target_pairs={{0,64},{8,72},{16,80},{24,88},{32,96},{40,104},{48,112},{56,120},{... | collective-permute-start | bytes 1572872 | tf_op jit(solution)/shard_map/ppermute | solution.py:40
  24.2 34.6 %collective-permute-start.2 = (bf16[2,128,1024]{2,1,0:T(8,128)(2,1)}, bf16[2,128,1024]{2,1,0:T(8,128)(2,1)}, u32[]{:S(2)}, u32[]{:S(2)}) collective-permute-start(bf16[2,128,1024]{2,1,0:T(8,128)(2,1)} %get-tuple-element.48), channel_id=1, source_target_pairs={{0,72},{8,64},{16,88},{24,80},{32,104},{40,96},{48,120},{56,112},{... | collective-permute-start | bytes 1572872 | tf_op jit(solution)/shard_map/ppermute | solution.py:40
  30.0 18.7 %collective-permute-start.3 = (bf16[1024,128]{1,0:T(8,128)(2,1)S(1)}, bf16[1024,128]{1,0:T(8,128)(2,1)}, u32[]{:S(2)}, u32[]{:S(2)}) collective-permute-start(bf16[1024,128]{1,0:T(8,128)(2,1)S(1)} %bitcast.48), channel_id=1, source_target_pairs={{0,2},{1,3},{2,4},{3,5},{4,6},{5,7},{6,0},{7,1},{8,10},{9,11},{10,... | collective-permute-start | bytes 786440 | tf_op jit(solution)/shard_map/ppermute | solution.py:49
  31.4 27.6 %collective-permute-start.4 = (bf16[1024,128]{1,0:T(8,128)(2,1)S(1)}, bf16[1024,128]{1,0:T(8,128)(2,1)}, u32[]{:S(2)}, u32[]{:S(2)}) collective-permute-start(bf16[1024,128]{1,0:T(8,128)(2,1)S(1)} %bitcast.47), channel_id=1, source_target_pairs={{0,4},{1,5},{2,6},{3,7},{4,0},{5,1},{6,2},{7,3},{8,12},{9,13},{10,... | collective-permute-start | bytes 786440 | tf_op jit(solution)/shard_map/ppermute | solution.py:49
  34.1 26.5 %collective-permute-start.5 = (bf16[1024,128]{1,0:T(8,128)(2,1)S(1)}, bf16[1024,128]{1,0:T(8,128)(2,1)}, u32[]{:S(2)}, u32[]{:S(2)}) collective-permute-start(bf16[1024,128]{1,0:T(8,128)(2,1)S(1)} %bitcast.46), channel_id=1, source_target_pairs={{0,6},{1,7},{2,0},{3,1},{4,2},{5,3},{6,4},{7,5},{8,14},{9,15},{10,... | collective-permute-start | bytes 786440 | tf_op jit(solution)/shard_map/ppermute | solution.py:49
  47.3 18.8 %collective-permute-start.12 = (bf16[1024,128]{1,0:T(8,128)(2,1)}, bf16[1024,128]{1,0:T(8,128)(2,1)}, u32[]{:S(2)}, u32[]{:S(2)}) collective-permute-start(bf16[1024,128]{1,0:T(8,128)(2,1)} %bitcast.15.refs_0_), channel_id=1, source_target_pairs={{0,8},{1,9},{2,10},{3,11},{4,12},{5,13},{6,14},{7,15},{8,0},{9,1},... | collective-permute-start | bytes 786440 | tf_op jit(solution)/shard_map/ppermute | solution.py:49
  48.7 17.6 %collective-permute-start.13 = (bf16[1024,128]{1,0:T(8,128)(2,1)}, bf16[1024,128]{1,0:T(8,128)(2,1)}, u32[]{:S(2)}, u32[]{:S(2)}) collective-permute-start(bf16[1024,128]{1,0:T(8,128)(2,1)} %collective-permute-done.3.refs_1_), channel_id=1, source_target_pairs={{0,8},{1,9},{2,10},{3,11},{4,12},{5,13},{6,14},{7,15},{8,0},{9,1},... | collective-permute-start | bytes 786440 | tf_op jit(solution)/shard_map/ppermute | solution.py:49
  53.6 30.3 %copy-start.18 = (f32[2,64,256]{2,1,0:T(8,128)}, f32[2,64,256]{2,1,0:T(8,128)S(1)}, u32[]{:S(2)}) copy-start(f32[2,64,256]{2,1,0:T(8,128)S(1)} %get-tuple-element.89.refs_5_) | copy-start | bytes 393220
  58.8 45.5 %collective-permute-start.10 = (bf16[2,128,1024]{2,1,0:T(8,128)(2,1)}, bf16[2,128,1024]{2,1,0:T(8,128)(2,1)}, u32[]{:S(2)}, u32[]{:S(2)}) collective-permute-start(bf16[2,128,1024]{2,1,0:T(8,128)(2,1)} %get-tuple-element.64), channel_id=1, source_target_pairs={{0,64},{8,72},{16,80},{24,88},{32,96},{40,104},{48,112},{56,120},{... | collective-permute-start | bytes 1572872 | tf_op jit(solution)/shard_map/ppermute | solution.py:40
  58.9 45.4 %collective-permute-start.11 = (bf16[2,128,1024]{2,1,0:T(8,128)(2,1)}, bf16[2,128,1024]{2,1,0:T(8,128)(2,1)}, u32[]{:S(2)}, u32[]{:S(2)}) collective-permute-start(bf16[2,128,1024]{2,1,0:T(8,128)(2,1)} %get-tuple-element.66), channel_id=1, source_target_pairs={{0,72},{8,64},{16,88},{24,80},{32,104},{40,96},{48,120},{56,112},{... | collective-permute-start | bytes 1572872 | tf_op jit(solution)/shard_map/ppermute | solution.py:40
  60.6 43.7 %collective-permute-start.9 = (bf16[2,128,1024]{2,1,0:T(8,128)(2,1)}, bf16[2,128,1024]{2,1,0:T(8,128)(2,1)}, u32[]{:S(2)}, u32[]{:S(2)}) collective-permute-start(bf16[2,128,1024]{2,1,0:T(8,128)(2,1)} %get-tuple-element.62), channel_id=1, source_target_pairs={{0,8},{8,0},{16,24},{24,16},{32,40},{40,32},{48,56},{56,48},{64,72... | collective-permute-start | bytes 1572872 | tf_op jit(solution)/shard_map/ppermute | solution.py:40
  60.6 34.5 %all-to-all-start.1 = ((bf16[16,2,128,128]{3,2,1,0:T(8,128)(2,1)}), bf16[16,2,128,128]{3,2,1,0:T(8,128)(2,1)S(1)}, u32[]{:S(2)}, u32[]{:S(2)}) async-start(bf16[16,2,128,128]{3,2,1,0:T(8,128)(2,1)} %bitcast.20), calls=%async_computation.1 | async-start | bytes 2097152 | tf_op jit(solution)/shard_map/all_to_all | solution.py:33
  66.1 38.2 %collective-permute-start.14 = (bf16[1024,128]{1,0:T(8,128)(2,1)}, bf16[1024,128]{1,0:T(8,128)(2,1)}, u32[]{:S(2)}, u32[]{:S(2)}) collective-permute-start(bf16[1024,128]{1,0:T(8,128)(2,1)} %collective-permute-done.4.refs_2_), channel_id=1, source_target_pairs={{0,8},{1,9},{2,10},{3,11},{4,12},{5,13},{6,14},{7,15},{8,0},{9,1},... | collective-permute-start | bytes 786440 | tf_op jit(solution)/shard_map/ppermute | solution.py:49
  66.3 38.0 %collective-permute-start.15 = (bf16[1024,128]{1,0:T(8,128)(2,1)}, bf16[1024,128]{1,0:T(8,128)(2,1)}, u32[]{:S(2)}, u32[]{:S(2)}) collective-permute-start(bf16[1024,128]{1,0:T(8,128)(2,1)} %collective-permute-done.5.refs_3_), channel_id=1, source_target_pairs={{0,8},{1,9},{2,10},{3,11},{4,12},{5,13},{6,14},{7,15},{8,0},{9,1},... | collective-permute-start | bytes 786440 | tf_op jit(solution)/shard_map/ppermute | solution.py:49
  95.1 34.2 %all-to-all-start.2 = ((bf16[16,2,128,128]{3,2,1,0:T(8,128)(2,1)}), bf16[16,2,128,128]{3,2,1,0:T(8,128)(2,1)S(1)}, u32[]{:S(2)}, u32[]{:S(2)}) async-start(bf16[16,2,128,128]{3,2,1,0:T(8,128)(2,1)} %get-tuple-element.74), calls=%async_computation.2 | async-start | bytes 2097152 | tf_op jit(solution)/shard_map/all_to_all | solution.py:33
  129.3 51.1 %all-to-all-start.3 = ((bf16[16,2,128,128]{3,2,1,0:T(8,128)(2,1)}), bf16[16,2,128,128]{3,2,1,0:T(8,128)(2,1)S(1)}, u32[]{:S(2)}, u32[]{:S(2)}) async-start(bf16[16,2,128,128]{3,2,1,0:T(8,128)(2,1)} %get-tuple-element.77), calls=%async_computation.3 | async-start | bytes 2097152 | tf_op jit(solution)/shard_map/all_to_all | solution.py:33
  142.1 3.6 %collective-permute-start.6 = (bf16[128,1024]{1,0:T(8,128)(2,1)}, bf16[128,1024]{1,0:T(8,128)(2,1)S(1)}, u32[]{:S(2)}, u32[]{:S(2)}) collective-permute-start(bf16[128,1024]{1,0:T(8,128)(2,1)} %get-tuple-element.58), channel_id=1, source_target_pairs={{0,8},{8,0},{16,24},{24,16},{32,40},{40,32},{48,56},{56,48},{64,72... | collective-permute-start | bytes 786440 | tf_op jit(solution)/shard_map/ppermute | solution.py:40
  142.2 16.2 %collective-permute-start.7 = (bf16[128,1024]{1,0:T(8,128)(2,1)}, bf16[128,1024]{1,0:T(8,128)(2,1)S(1)}, u32[]{:S(2)}, u32[]{:S(2)}) collective-permute-start(bf16[128,1024]{1,0:T(8,128)(2,1)} %get-tuple-element.59), channel_id=1, source_target_pairs={{0,64},{8,72},{16,80},{24,88},{32,96},{40,104},{48,112},{56,120},{... | collective-permute-start | bytes 786440 | tf_op jit(solution)/shard_map/ppermute | solution.py:40
  143.8 23.7 %collective-permute-start.8 = (bf16[128,1024]{1,0:T(8,128)(2,1)}, bf16[128,1024]{1,0:T(8,128)(2,1)S(1)}, u32[]{:S(2)}, u32[]{:S(2)}) collective-permute-start(bf16[128,1024]{1,0:T(8,128)(2,1)} %copy-done.26), channel_id=1, source_target_pairs={{0,72},{8,64},{16,88},{24,80},{32,104},{40,96},{48,120},{56,112},{... | collective-permute-start | bytes 786440 | tf_op jit(solution)/shard_map/ppermute | solution.py:40
  144.2 26.6 %collective-permute-start.16 = (bf16[128,1024]{1,0:T(8,128)(2,1)}, bf16[128,1024]{1,0:T(8,128)(2,1)S(1)}, u32[]{:S(2)}, u32[]{:S(2)}) collective-permute-start(bf16[128,1024]{1,0:T(8,128)(2,1)} %copy-done.29), channel_id=1, source_target_pairs={{0,8},{8,0},{16,24},{24,16},{32,40},{40,32},{48,56},{56,48},{64,72... | collective-permute-start | bytes 786440 | tf_op jit(solution)/shard_map/ppermute | solution.py:40
  144.3 29.6 %collective-permute-start.17 = (bf16[128,1024]{1,0:T(8,128)(2,1)}, bf16[128,1024]{1,0:T(8,128)(2,1)S(1)}, u32[]{:S(2)}, u32[]{:S(2)}) collective-permute-start(bf16[128,1024]{1,0:T(8,128)(2,1)} %copy-done.28), channel_id=1, source_target_pairs={{0,64},{8,72},{16,80},{24,88},{32,96},{40,104},{48,112},{56,120},{... | collective-permute-start | bytes 786440 | tf_op jit(solution)/shard_map/ppermute | solution.py:40
  145.7 32.6 %collective-permute-start.18 = (bf16[128,1024]{1,0:T(8,128)(2,1)}, bf16[128,1024]{1,0:T(8,128)(2,1)S(1)}, u32[]{:S(2)}, u32[]{:S(2)}) collective-permute-start(bf16[128,1024]{1,0:T(8,128)(2,1)} %copy-done.27), channel_id=1, source_target_pairs={{0,72},{8,64},{16,88},{24,80},{32,104},{40,96},{48,120},{56,112},{... | collective-permute-start | bytes 786440 | tf_op jit(solution)/shard_map/ppermute | solution.py:40
  169.5 12.9 %collective-permute-start.26 = (bf16[128,256]{1,0:T(8,128)(2,1)S(1)}, bf16[128,256]{1,0:T(8,128)(2,1)S(1)}, u32[]{:S(2)}, u32[]{:S(2)}) collective-permute-start(bf16[128,256]{1,0:T(8,128)(2,1)S(1)} %get-tuple-element.86.refs_8_), channel_id=1, source_target_pairs={{0,2},{1,3},{2,4},{3,5},{4,6},{5,7},{6,0},{7,1},{8,10},{9,11},{10,... | collective-permute-start | bytes 196616 | tf_op jit(solution)/shard_map/ppermute | solution.py:49
  170.8 11.6 %collective-permute-start.27 = (bf16[128,256]{1,0:T(8,128)(2,1)S(1)}, bf16[128,256]{1,0:T(8,128)(2,1)S(1)}, u32[]{:S(2)}, u32[]{:S(2)}) collective-permute-start(bf16[128,256]{1,0:T(8,128)(2,1)S(1)} %get-tuple-element.86.refs_8_), channel_id=1, source_target_pairs={{0,4},{1,5},{2,6},{3,7},{4,0},{5,1},{6,2},{7,3},{8,12},{9,13},{10,... | collective-permute-start | bytes 196616 | tf_op jit(solution)/shard_map/ppermute | solution.py:49
  171.5 13.5 %collective-permute-start.28 = (bf16[128,256]{1,0:T(8,128)(2,1)S(1)}, bf16[128,256]{1,0:T(8,128)(2,1)S(1)}, u32[]{:S(2)}, u32[]{:S(2)}) collective-permute-start(bf16[128,256]{1,0:T(8,128)(2,1)S(1)} %get-tuple-element.86.refs_8_), channel_id=1, source_target_pairs={{0,6},{1,7},{2,0},{3,1},{4,2},{5,3},{6,4},{7,5},{8,14},{9,15},{10,... | collective-permute-start | bytes 196616 | tf_op jit(solution)/shard_map/ppermute | solution.py:49
  174.6 10.4 %collective-permute-start.29 = (bf16[128,256]{1,0:T(8,128)(2,1)}, bf16[128,256]{1,0:T(8,128)(2,1)S(1)}, u32[]{:S(2)}, u32[]{:S(2)}) collective-permute-start(bf16[128,256]{1,0:T(8,128)(2,1)} %get-tuple-element.87), channel_id=1, source_target_pairs={{0,8},{1,9},{2,10},{3,11},{4,12},{5,13},{6,14},{7,15},{8,0},{9,1},... | collective-permute-start | bytes 196616 | tf_op jit(solution)/shard_map/ppermute | solution.py:49
  179.0 8.1 %collective-permute-start.30 = (bf16[128,256]{1,0:T(8,128)(2,1)}, bf16[128,256]{1,0:T(8,128)(2,1)S(1)}, u32[]{:S(2)}, u32[]{:S(2)}) collective-permute-start(bf16[128,256]{1,0:T(8,128)(2,1)} %get-tuple-element.87), channel_id=1, source_target_pairs={{0,10},{1,11},{2,12},{3,13},{4,14},{5,15},{6,8},{7,9},{8,2},{9,3},... | collective-permute-start | bytes 196616 | tf_op jit(solution)/shard_map/ppermute | solution.py:49
  182.4 6.1 %collective-permute-start.31 = (bf16[128,256]{1,0:T(8,128)(2,1)}, bf16[128,256]{1,0:T(8,128)(2,1)S(1)}, u32[]{:S(2)}, u32[]{:S(2)}) collective-permute-start(bf16[128,256]{1,0:T(8,128)(2,1)} %get-tuple-element.87), channel_id=1, source_target_pairs={{0,12},{1,13},{2,14},{3,15},{4,8},{5,9},{6,10},{7,11},{8,4},{9,5},... | collective-permute-start | bytes 196616 | tf_op jit(solution)/shard_map/ppermute | solution.py:49
  182.4 7.2 %collective-permute-start.32 = (bf16[128,256]{1,0:T(8,128)(2,1)}, bf16[128,256]{1,0:T(8,128)(2,1)S(1)}, u32[]{:S(2)}, u32[]{:S(2)}) collective-permute-start(bf16[128,256]{1,0:T(8,128)(2,1)} %get-tuple-element.87), channel_id=1, source_target_pairs={{0,14},{1,15},{2,8},{3,9},{4,10},{5,11},{6,12},{7,13},{8,6},{9,7},... | collective-permute-start | bytes 196616 | tf_op jit(solution)/shard_map/ppermute | solution.py:49
  185.0 5.4 %collective-permute-start.19 = (bf16[128,256]{1,0:T(8,128)(2,1)S(1)}, bf16[128,256]{1,0:T(8,128)(2,1)S(1)}, u32[]{:S(2)}, u32[]{:S(2)}) collective-permute-start(bf16[128,256]{1,0:T(8,128)(2,1)S(1)} %get-tuple-element.84.refs_8_), channel_id=1, source_target_pairs={{0,2},{1,3},{2,4},{3,5},{4,6},{5,7},{6,0},{7,1},{8,10},{9,11},{10,... | collective-permute-start | bytes 196616 | tf_op jit(solution)/shard_map/ppermute | solution.py:49
  185.0 7.6 %collective-permute-start.20 = (bf16[128,256]{1,0:T(8,128)(2,1)S(1)}, bf16[128,256]{1,0:T(8,128)(2,1)S(1)}, u32[]{:S(2)}, u32[]{:S(2)}) collective-permute-start(bf16[128,256]{1,0:T(8,128)(2,1)S(1)} %get-tuple-element.84.refs_8_), channel_id=1, source_target_pairs={{0,4},{1,5},{2,6},{3,7},{4,0},{5,1},{6,2},{7,3},{8,12},{9,13},{10,... | collective-permute-start | bytes 196616 | tf_op jit(solution)/shard_map/ppermute | solution.py:49
  187.1 9.9 %collective-permute-start.21 = (bf16[128,256]{1,0:T(8,128)(2,1)S(1)}, bf16[128,256]{1,0:T(8,128)(2,1)S(1)}, u32[]{:S(2)}, u32[]{:S(2)}) collective-permute-start(bf16[128,256]{1,0:T(8,128)(2,1)S(1)} %get-tuple-element.84.refs_8_), channel_id=1, source_target_pairs={{0,6},{1,7},{2,0},{3,1},{4,2},{5,3},{6,4},{7,5},{8,14},{9,15},{10,... | collective-permute-start | bytes 196616 | tf_op jit(solution)/shard_map/ppermute | solution.py:49
  188.5 8.5 %collective-permute-start.22 = (bf16[128,256]{1,0:T(8,128)(2,1)S(1)}, bf16[128,256]{1,0:T(8,128)(2,1)S(1)}, u32[]{:S(2)}, u32[]{:S(2)}) collective-permute-start(bf16[128,256]{1,0:T(8,128)(2,1)S(1)} %get-tuple-element.85), channel_id=1, source_target_pairs={{0,8},{1,9},{2,10},{3,11},{4,12},{5,13},{6,14},{7,15},{8,0},{9,1},... | collective-permute-start | bytes 196616 | tf_op jit(solution)/shard_map/ppermute | solution.py:49
  189.6 7.4 %collective-permute-start.23 = (bf16[128,256]{1,0:T(8,128)(2,1)S(1)}, bf16[128,256]{1,0:T(8,128)(2,1)S(1)}, u32[]{:S(2)}, u32[]{:S(2)}) collective-permute-start(bf16[128,256]{1,0:T(8,128)(2,1)S(1)} %get-tuple-element.85), channel_id=1, source_target_pairs={{0,10},{1,11},{2,12},{3,13},{4,14},{5,15},{6,8},{7,9},{8,2},{9,3},... | collective-permute-start | bytes 196616 | tf_op jit(solution)/shard_map/ppermute | solution.py:49
  190.3 6.7 %collective-permute-start.24 = (bf16[128,256]{1,0:T(8,128)(2,1)S(1)}, bf16[128,256]{1,0:T(8,128)(2,1)S(1)}, u32[]{:S(2)}, u32[]{:S(2)}) collective-permute-start(bf16[128,256]{1,0:T(8,128)(2,1)S(1)} %get-tuple-element.85), channel_id=1, source_target_pairs={{0,12},{1,13},{2,14},{3,15},{4,8},{5,9},{6,10},{7,11},{8,4},{9,5},... | collective-permute-start | bytes 196616 | tf_op jit(solution)/shard_map/ppermute | solution.py:49
  192.6 4.4 %collective-permute-start.25 = (bf16[128,256]{1,0:T(8,128)(2,1)S(1)}, bf16[128,256]{1,0:T(8,128)(2,1)S(1)}, u32[]{:S(2)}, u32[]{:S(2)}) collective-permute-start(bf16[128,256]{1,0:T(8,128)(2,1)S(1)} %get-tuple-element.85), channel_id=1, source_target_pairs={{0,14},{1,15},{2,8},{3,9},{4,10},{5,11},{6,12},{7,13},{8,6},{9,7},... | collective-permute-start | bytes 196616 | tf_op jit(solution)/shard_map/ppermute | solution.py:49
  200.6 10.1 %copy-start.9 = (bf16[128,1024]{1,0:T(8,128)(2,1)S(1)}, bf16[128,1024]{1,0:T(8,128)(2,1)}, u32[]{:S(2)}) copy-start(bf16[128,1024]{1,0:T(8,128)(2,1)} %copy-done.8) | copy-start | bytes 786436
  200.6 10.1 %copy-start.11 = (bf16[128,1024]{1,0:T(8,128)(2,1)S(1)}, bf16[128,1024]{1,0:T(8,128)(2,1)}, u32[]{:S(2)}) copy-start(bf16[128,1024]{1,0:T(8,128)(2,1)} %copy-done.10) | copy-start | bytes 786436
  200.6 10.1 %copy-start.13 = (bf16[128,1024]{1,0:T(8,128)(2,1)S(1)}, bf16[128,1024]{1,0:T(8,128)(2,1)}, u32[]{:S(2)}) copy-start(bf16[128,1024]{1,0:T(8,128)(2,1)} %copy-done.12) | copy-start | bytes 786436
  200.6 10.1 %copy-start.15 = (bf16[128,1024]{1,0:T(8,128)(2,1)S(1)}, bf16[128,1024]{1,0:T(8,128)(2,1)}, u32[]{:S(2)}) copy-start(bf16[128,1024]{1,0:T(8,128)(2,1)} %copy-done.14) | copy-start | bytes 786436
  200.6 38.7 %all-to-all-start.4 = ((bf16[64,16,512]{2,1,0:T(8,128)(2,1)}), bf16[64,16,512]{2,1,0:T(8,128)(2,1)S(1)}, u32[]{:S(2)}, u32[]{:S(2)}) async-start(bf16[64,16,512]{2,1,0:T(8,128)(2,1)} %bitcast.27), calls=%async_computation.4 | async-start | bytes 2097152 | tf_op jit(solution)/shard_map/all_to_all | solution.py:33
  (22 other events, 42.6 us)

commit v4 on v3

--- a/solution.py
+++ b/solution.py
@@ -515,12 +515,14 @@
     dq_back, dkv_back = [], []
     for part in range(PARTS):
         *dq, dkv = attention(meta, qg_in[part], kv_in[part], cos_t, sin_t)
+        for earlier in dq_back:
+            dkv = after(dkv, *earlier)
         dkv_back.append(swap(dkv, "sp", HALF_GROUPS))
         dq_back.append([dq[0]] + quad_swap(dq[1:]))
 
     dk, dv, partial = [], [], ()
     for part in range(PARTS):
-        back = after(dkv_back[part], *dq_back[part])
+        back = after(dkv_back[part], *dq_back[part], *partial)
         dk_part, dv_part, same, other = key_post(core_at, back, cos, sin)
         dk.append(dk_part)
         dv.append(dv_part)

time: 242 us -> 228 us (0.942)
  waiting for transfers between devices: 83.9 us -> 72.3 us
    ppermute x12, waiting for transfers between devices: 41.9 us -> 18.7 us  [quad_send(): return lax.ppermute(array, 'sp', [(s, s ^ flip) for s in range(SP)])]
    ppermute x21, waiting for transfers between devices: 0.55 us -> 16.8 us  [y_send(): return lax.ppermute(array, ('sp', 'dp'), pairs)]
    ppermute x21, starting transfers between devices: 23.8 us -> 17.9 us  [y_send(): return lax.ppermute(array, ('sp', 'dp'), pairs)]
    all_to_all x5, waiting for transfers between devices: 41.5 us -> 36.7 us  [swap(): lax.all_to_all(array, axes, split_axis=0, concat_axis=0, axis_index_group...]
    ppermute x12, starting transfers between devices: 8.29 us -> 11.8 us  [quad_send(): return lax.ppermute(array, 'sp', [(s, s ^ flip) for s in range(SP)])]
    unnamed x64 -> x76, local copies, waits for them, and re-layouts: 10.2 us -> 10.7 us
  transfers between devices with their start and end apart: 38 -> 38, of which waited for: 9 -> 12; matrix products, arithmetic and copies ran while one was open for 1% -> 1% of each run, Pallas kernels for 20% -> 20%
where the time goes in v4:
time: 228 us
  starting transfers between devices  77.4 us (34%)
  waiting for transfers between devices  72.3 us (32%)
  Pallas kernels  56.8 us (25%)
  local copies, waits for them, and re-layouts  15.4 us (7%)
  other arithmetic  3.9 us (2%)
    all_to_all x5, starting transfers between devices, swap(): lax.all_to_all(array, axes, split_axis=0, concat_axis=0, axis_index_group...  47.7 us
    all_to_all x5, waiting for transfers between devices, swap(): lax.all_to_all(array, axes, split_axis=0, concat_axis=0, axis_index_group...  36.7 us
    pallas_call x2, Pallas kernels, attention(): pl.pallas_call(attention_kernel, grid=(REP // STACK,), in_specs=[pl.Block...  34.1 us
    ppermute x12, waiting for transfers between devices, quad_send(): return lax.ppermute(array, 'sp', [(s, s ^ flip) for s in range(SP)])  18.7 us
    ppermute x21, starting transfers between devices, y_send(): return lax.ppermute(array, ('sp', 'dp'), pairs)  17.9 us
    ppermute x21, waiting for transfers between devices, y_send(): return lax.ppermute(array, ('sp', 'dp'), pairs)  16.8 us
    ppermute x12, starting transfers between devices, quad_send(): return lax.ppermute(array, 'sp', [(s, s ^ flip) for s in range(SP)])  11.8 us
    unnamed x76, local copies, waits for them, and re-layouts  10.7 us
  transfers between devices with their start and end apart: 38, of which 12 were waited for; matrix products, arithmetic and copies ran while one was open for 1% of the time, Pallas kernels for 20%

profile of v4, /device:TPU:1, one launch (start us, length us, event | category | flops | bytes accessed | tf_op | source)
XLA Modules:
  0.0 227.6 jit_solution(6738036359391315701)
XLA Ops:
  0.7 1.3 constant_dynamic-slice_fusion
  4.2 0.7 pad_maximum_fusion.cos_ref
  7.0 3.9 %query_prep.5 = (bf16[2,128,1024]{2,1,0:T(8,128)(2,1)}, bf16[2,128,1024]{2,1,0:T(8,128)(2,1)}, bf16[2,128,1024]{2,1,0:T(8,128)(2,1)}) custom-call(s32[1]{0:T(128)} %bitcast.me_ref, bf16[128,8192]{1,0:T(8,128)(2,1)} %bitcast.31, bf16[128,8192]{1,0:T(8,128)(2,1)} %bitcast.35, f32[128,128]{1,0:T(8,128)} %pad_maximum_fusion.cos_ref, ...), custom_call_target="tpu_custom_call" | custom-call | flops 3145728 | bytes 3145728 | tf_op jit(solution)/shard_map/query_prep/pallas_call | solution.py:125
  11.0 2.0 key_prep.1
  13.0 1.0 copy-done.7
  14.0 8.4 %all-to-all-start = ((bf16[16,2,128,128]{3,2,1,0:T(8,128)(2,1)}), bf16[16,2,128,128]{3,2,1,0:T(8,128)(2,1)}, u32[]{:S(2)}, u32[]{:S(2)}) async-start(bf16[16,2,128,128]{3,2,1,0:T(8,128)(2,1)} %bitcast.43), calls=%async_computation | async-start | bytes 2097152 | tf_op jit(solution)/shard_map/all_to_all | solution.py:33
  22.6 1.5 collective-permute-start.1
  26.9 3.1 %input_prep.1 = (bf16[32,32,128]{2,1,0:T(8,128)(2,1)}, bf16[32,32,128]{2,1,0:T(8,128)(2,1)S(1)}, bf16[32,32,128]{2,1,0:T(8,128)(2,1)S(1)}, bf16[32,32,128]{2,1,0:T(8,128)(2,1)S(1)}) custom-call(s32[1]{0:T(128)} %bitcast.13.me_ref, bf16[128,4096]{1,0:T(8,128)(2,1)S(1)} %bitcast.42), custom_call_target="tpu_custom_call" | custom-call | flops 1048576 | bytes 2097152 | tf_op jit(solution)/shard_map/input_prep/pallas_call | solution.py:150
  30.0 1.3 collective-permute-start.3
  31.4 2.7 %collective-permute-start.4 = (bf16[1024,128]{1,0:T(8,128)(2,1)S(1)}, bf16[1024,128]{1,0:T(8,128)(2,1)}, u32[]{:S(2)}, u32[]{:S(2)}) collective-permute-start(bf16[1024,128]{1,0:T(8,128)(2,1)S(1)} %bitcast.47), channel_id=1, source_target_pairs={{0,4},{1,5},{2,6},{3,7},{4,0},{5,1},{6,2},{7,3},{8,12},{9,13},{10,... | collective-permute-start | bytes 786440 | tf_op jit(solution)/shard_map/ppermute | solution.py:49
  34.1 1.1 collective-permute-start.5
  35.2 12.2 %collective-permute-done.1.refs_2_ = bf16[2,128,1024]{2,1,0:T(8,128)(2,1)} collective-permute-done((bf16[2,128,1024]{2,1,0:T(8,128)(2,1)}, bf16[2,128,1024]{2,1,0:T(8,128)(2,1)}, u32[]{:S(2)}, u32[]{:S(2)}) %collective-permute-start.1) | collective-permute-done | bytes 524320 | tf_op jit(solution)/shard_map/ppermute | solution.py:40
  47.3 1.3 collective-permute-start.12
  48.8 1.6 copy-done.2
  50.9 2.2 query_prep.7
  53.7 5.1 %collective-permute-done.2.refs_3_ = bf16[2,128,1024]{2,1,0:T(8,128)(2,1)} collective-permute-done((bf16[2,128,1024]{2,1,0:T(8,128)(2,1)}, bf16[2,128,1024]{2,1,0:T(8,128)(2,1)}, u32[]{:S(2)}, u32[]{:S(2)}) %collective-permute-start.2) | collective-permute-done | bytes 524320 | tf_op jit(solution)/shard_map/ppermute | solution.py:40
  58.9 1.7 collective-permute-start.11
  60.6 5.5 %all-to-all-start.1 = ((bf16[16,2,128,128]{3,2,1,0:T(8,128)(2,1)}), bf16[16,2,128,128]{3,2,1,0:T(8,128)(2,1)S(1)}, u32[]{:S(2)}, u32[]{:S(2)}) async-start(bf16[16,2,128,128]{3,2,1,0:T(8,128)(2,1)} %bitcast.20), calls=%async_computation.1 | async-start | bytes 2097152 | tf_op jit(solution)/shard_map/all_to_all | solution.py:33
  66.7 17.3 %attention.2 = (bf16[128,1024]{1,0:T(8,128)(2,1)S(1)}, bf16[128,1024]{1,0:T(8,128)(2,1)}, bf16[128,1024]{1,0:T(8,128)(2,1)}, bf16[128,1024]{1,0:T(8,128)(2,1)S(1)}, bf16[16,2,128,128]{3,2,1,0:T(8,128)(2,1)}) custom-call(s32[2,4]{1,0:T(2,128)S(1)} %add_add_fusion.meta_ref, bf16[2,128,1024]{2,1,0:T(8,128)(2,1)S(1)} %query_prep.4.refs_0_, ...), custom_call_target="tpu_custom_call" | custom-call | flops 24999999488 | bytes 6291456 | tf_op jit(solution)/shard_map/attention/pallas_call | solution.py:274
  87.1 1.5 collective-permute-start.7
  88.6 7.1 %all-to-all-done.1.refs_4_ = bf16[16,2,128,128]{3,2,1,0:T(8,128)(2,1)S(1)} async-done(((bf16[16,2,128,128]{3,2,1,0:T(8,128)(2,1)}), bf16[16,2,128,128]{3,2,1,0:T(8,128)(2,1)S(1)}, u32[]{:S(2)}, u32[]{:S(2)}) %all-to-all-start.1) | async-done | bytes 1048608 | tf_op jit(solution)/shard_map/all_to_all | solution.py:33
  95.7 10.7 %all-to-all-start.2 = ((bf16[16,2,128,128]{3,2,1,0:T(8,128)(2,1)}), bf16[16,2,128,128]{3,2,1,0:T(8,128)(2,1)S(1)}, u32[]{:S(2)}, u32[]{:S(2)}) async-start(bf16[16,2,128,128]{3,2,1,0:T(8,128)(2,1)} %get-tuple-element.75), calls=%async_computation.2 | async-start | bytes 2097152 | tf_op jit(solution)/shard_map/all_to_all | solution.py:33
  106.4 1.7 collective-permute-start.8
  108.2 0.9 copy-done.25
  109.1 16.8 %attention.3 = (bf16[128,1024]{1,0:T(8,128)(2,1)S(1)}, bf16[128,1024]{1,0:T(8,128)(2,1)S(1)}, bf16[128,1024]{1,0:T(8,128)(2,1)S(1)}, bf16[128,1024]{1,0:T(8,128)(2,1)S(1)}, bf16[16,2,128,128]{3,2,1,0:T(8,128)(2,1)}) custom-call(s32[2,4]{1,0:T(2,128)S(1)} %add_add_fusion.meta_ref, bf16[2,128,1024]{2,1,0:T(8,128)(2,1)S(1)} %query_prep.6.refs_0_, ...), custom_call_target="tpu_custom_call" | custom-call | flops 24999999488 | bytes 6291456 | tf_op jit(solution)/shard_map/attention/pallas_call | solution.py:274
  127.6 3.9 %all-to-all-done.2 = bf16[16,2,128,128]{3,2,1,0:T(8,128)(2,1)S(1)} async-done(((bf16[16,2,128,128]{3,2,1,0:T(8,128)(2,1)}), bf16[16,2,128,128]{3,2,1,0:T(8,128)(2,1)S(1)}, u32[]{:S(2)}, u32[]{:S(2)}) %all-to-all-start.2) | async-done | bytes 1048608 | tf_op jit(solution)/shard_map/all_to_all | solution.py:33
  131.4 13.6 %all-to-all-start.3 = ((bf16[16,2,128,128]{3,2,1,0:T(8,128)(2,1)}), bf16[16,2,128,128]{3,2,1,0:T(8,128)(2,1)S(1)}, u32[]{:S(2)}, u32[]{:S(2)}) async-start(bf16[16,2,128,128]{3,2,1,0:T(8,128)(2,1)} %get-tuple-element.79), calls=%async_computation.3 | async-start | bytes 2097152 | tf_op jit(solution)/shard_map/all_to_all | solution.py:33
  146.4 2.7 %collective-permute-start.21 = (bf16[128,256]{1,0:T(8,128)(2,1)S(1)}, bf16[128,256]{1,0:T(8,128)(2,1)S(1)}, u32[]{:S(2)}, u32[]{:S(2)}) collective-permute-start(bf16[128,256]{1,0:T(8,128)(2,1)S(1)} %get-tuple-element.80.refs_8_), channel_id=1, source_target_pairs={{0,6},{1,7},{2,0},{3,1},{4,2},{5,3},{6,4},{7,5},{8,14},{9,15},{10,... | collective-permute-start | bytes 196616 | tf_op jit(solution)/shard_map/ppermute | solution.py:49
  149.8 1.6 collective-permute-start.17
  151.4 1.4 collective-permute-done.19.refs_9_
  152.8 2.0 collective-permute-start.18
  154.9 1.2 collective-permute-done.22.refs_12_
  156.0 1.3 collective-permute-start.24
  157.3 4.6 %collective-permute-done.23.refs_13_ = bf16[128,256]{1,0:T(8,128)(2,1)S(1)} collective-permute-done((bf16[128,256]{1,0:T(8,128)(2,1)S(1)}, bf16[128,256]{1,0:T(8,128)(2,1)S(1)}, u32[]{:S(2)}, u32[]{:S(2)}) %collective-permute-start.23) | collective-permute-done | bytes 65568 | tf_op jit(solution)/shard_map/ppermute | solution.py:49
  161.9 4.0 %collective-permute-done.25.refs_15_ = bf16[128,256]{1,0:T(8,128)(2,1)S(1)} collective-permute-done((bf16[128,256]{1,0:T(8,128)(2,1)S(1)}, bf16[128,256]{1,0:T(8,128)(2,1)S(1)}, u32[]{:S(2)}, u32[]{:S(2)}) %collective-permute-start.25) | collective-permute-done | bytes 65568 | tf_op jit(solution)/shard_map/ppermute | solution.py:49
  165.9 2.6 %project.2.refs_16_ = bf16[1024,256]{1,0:T(8,128)(2,1)S(1)} custom-call(bf16[1024,128]{1,0:T(8,128)(2,1)} %bitcast.15.refs_0_, bf16[1024,128]{1,0:T(8,128)(2,1)} %collective-permute-done.3.refs_1_, bf16[1024,128]{1,0:T(8,128)(2,1)} %collective-permute-done.4.refs_2_, bf16[1024,128]{1,0:T(8,128)(2,1)} %collective-permute-done.5.refs_3_, ...), custom_call_target="tpu_custom_call" | custom-call | flops 1000000000 | bytes 3145728 | tf_op jit(solution)/shard_map/project/pallas_call | solution.py:412
  168.6 1.5 collective-permute-done.18.refs_7_
  172.7 2.7 %collective-permute-start.28 = (bf16[128,256]{1,0:T(8,128)(2,1)S(1)}, bf16[128,256]{1,0:T(8,128)(2,1)S(1)}, u32[]{:S(2)}, u32[]{:S(2)}) collective-permute-start(bf16[128,256]{1,0:T(8,128)(2,1)S(1)} %get-tuple-element.88.refs_8_), channel_id=1, source_target_pairs={{0,6},{1,7},{2,0},{3,1},{4,2},{5,3},{6,4},{7,5},{8,14},{9,15},{10,... | collective-permute-start | bytes 196616 | tf_op jit(solution)/shard_map/ppermute | solution.py:49
  175.4 0.8 collective-permute-start.29
  176.6 2.5 %collective-permute-done.26.refs_9_ = bf16[128,256]{1,0:T(8,128)(2,1)S(1)} collective-permute-done((bf16[128,256]{1,0:T(8,128)(2,1)S(1)}, bf16[128,256]{1,0:T(8,128)(2,1)S(1)}, u32[]{:S(2)}, u32[]{:S(2)}) %collective-permute-start.26) | collective-permute-done | bytes 65568 | tf_op jit(solution)/shard_map/ppermute | solution.py:49
  179.1 2.9 %collective-permute-start.32 = (bf16[128,256]{1,0:T(8,128)(2,1)S(1)}, bf16[128,256]{1,0:T(8,128)(2,1)S(1)}, u32[]{:S(2)}, u32[]{:S(2)}) collective-permute-start(bf16[128,256]{1,0:T(8,128)(2,1)S(1)} %get-tuple-element.89), channel_id=1, source_target_pairs={{0,14},{1,15},{2,8},{3,9},{4,10},{5,11},{6,12},{7,13},{8,6},{9,7},... | collective-permute-start | bytes 196616 | tf_op jit(solution)/shard_map/ppermute | solution.py:49
  182.0 3.2 %collective-permute-done.31.refs_14_ = bf16[128,256]{1,0:T(8,128)(2,1)S(1)} collective-permute-done((bf16[128,256]{1,0:T(8,128)(2,1)S(1)}, bf16[128,256]{1,0:T(8,128)(2,1)S(1)}, u32[]{:S(2)}, u32[]{:S(2)}) %collective-permute-start.31) | collective-permute-done | bytes 65568 | tf_op jit(solution)/shard_map/ppermute | solution.py:49
  185.2 3.4 %project.3 = bf16[1024,512]{1,0:T(8,128)(2,1)} custom-call(bf16[1024,128]{1,0:T(8,128)(2,1)} %bitcast.15.refs_0_, bf16[1024,128]{1,0:T(8,128)(2,1)} %collective-permute-done.3.refs_1_, bf16[1024,128]{1,0:T(8,128)(2,1)} %collective-permute-done.4.refs_2_, bf16[1024,128]{1,0:T(8,128)(2,1)} %collective-permute-done.5.refs_3_, ...), custom_call_target="tpu_custom_call" | custom-call | flops 1000000000 | bytes 3145728 | tf_op jit(solution)/shard_map/project/pallas_call | solution.py:412
  188.7 9.5 %all-to-all-start.4 = ((bf16[64,16,512]{2,1,0:T(8,128)(2,1)}), bf16[64,16,512]{2,1,0:T(8,128)(2,1)S(1)}, u32[]{:S(2)}, u32[]{:S(2)}) async-start(bf16[64,16,512]{2,1,0:T(8,128)(2,1)} %bitcast.27), calls=%async_computation.4 | async-start | bytes 2097152 | tf_op jit(solution)/shard_map/all_to_all | solution.py:33
  198.3 1.9 query_post.1
  200.2 0.9 join.1
  201.1 25.7 %all-to-all-done.4 = bf16[64,16,512]{2,1,0:T(8,128)(2,1)S(1)} async-done(((bf16[64,16,512]{2,1,0:T(8,128)(2,1)}), bf16[64,16,512]{2,1,0:T(8,128)(2,1)S(1)}, u32[]{:S(2)}, u32[]{:S(2)}) %all-to-all-start.4) | async-done | bytes 1048608 | tf_op jit(solution)/shard_map/all_to_all | solution.py:33
  226.8 0.8 final_sum.1
  (143 shorter events, 18.8 us)
Async XLA Ops:
  11.0 13.7 %copy-start.36 = (s32[1,32]{1,0:T(1,128)S(1)}, s32[1,32]{1,0:T(1,128)}, u32[]{:S(2)}) copy-start(s32[1,32]{1,0:T(1,128)} %param.13) | copy-start | bytes 388
  11.0 15.1 %copy-start.37 = (s32[1,32]{1,0:T(1,128)S(1)}, s32[1,32]{1,0:T(1,128)}, u32[]{:S(2)}) copy-start(s32[1,32]{1,0:T(1,128)} %param.14) | copy-start | bytes 388
  11.0 15.9 %copy-start.6 = (bf16[1,128,4096]{2,1,0:T(8,128)(2,1)S(1)}, bf16[1,128,4096]{2,1,0:T(8,128)(2,1)}, u32[]{:S(2)}) copy-start(bf16[1,128,4096]{2,1,0:T(8,128)(2,1)} %param.12) | copy-start | bytes 3145732
  14.0 34.8 %copy-start.1 = (bf16[1,128,8192]{2,1,0:T(8,128)(2,1)S(1)}, bf16[1,128,8192]{2,1,0:T(8,128)(2,1)}, u32[]{:S(2)}) copy-start(bf16[1,128,8192]{2,1,0:T(8,128)(2,1)} %param.8) | copy-start | bytes 6291460
  14.0 34.8 %copy-start.5 = (f32[128,128]{1,0:T(8,128)S(1)}, f32[128,128]{1,0:T(8,128)}, u32[]{:S(2)}) copy-start(f32[128,128]{1,0:T(8,128)} %broadcast_in_dim.8.valid_ref) | copy-start | bytes 196612
  14.0 46.6 %all-to-all-start = ((bf16[16,2,128,128]{3,2,1,0:T(8,128)(2,1)}), bf16[16,2,128,128]{3,2,1,0:T(8,128)(2,1)}, u32[]{:S(2)}, u32[]{:S(2)}) async-start(bf16[16,2,128,128]{3,2,1,0:T(8,128)(2,1)} %bitcast.43), calls=%async_computation | async-start | bytes 2097152 | tf_op jit(solution)/shard_map/all_to_all | solution.py:33
  22.4 4.5 %collective-permute-start = (bf16[2,128,1024]{2,1,0:T(8,128)(2,1)}, bf16[2,128,1024]{2,1,0:T(8,128)(2,1)}, u32[]{:S(2)}, u32[]{:S(2)}) collective-permute-start(bf16[2,128,1024]{2,1,0:T(8,128)(2,1)} %get-tuple-element.47), channel_id=1, source_target_pairs={{0,8},{8,0},{16,24},{24,16},{32,40},{40,32},{48,56},{56,48},{64,72... | collective-permute-start | bytes 1572872 | tf_op jit(solution)/shard_map/ppermute | solution.py:40
  22.6 24.7 %collective-permute-start.1 = (bf16[2,128,1024]{2,1,0:T(8,128)(2,1)}, bf16[2,128,1024]{2,1,0:T(8,128)(2,1)}, u32[]{:S(2)}, u32[]{:S(2)}) collective-permute-start(bf16[2,128,1024]{2,1,0:T(8,128)(2,1)} %get-tuple-element.48), channel_id=1, source_target_pairs={{0,64},{8,72},{16,80},{24,88},{32,96},{40,104},{48,112},{56,120},{... | collective-permute-start | bytes 1572872 | tf_op jit(solution)/shard_map/ppermute | solution.py:40
  24.1 34.6 %collective-permute-start.2 = (bf16[2,128,1024]{2,1,0:T(8,128)(2,1)}, bf16[2,128,1024]{2,1,0:T(8,128)(2,1)}, u32[]{:S(2)}, u32[]{:S(2)}) collective-permute-start(bf16[2,128,1024]{2,1,0:T(8,128)(2,1)} %get-tuple-element.49), channel_id=1, source_target_pairs={{0,72},{8,64},{16,88},{24,80},{32,104},{40,96},{48,120},{56,112},{... | collective-permute-start | bytes 1572872 | tf_op jit(solution)/shard_map/ppermute | solution.py:40
  30.0 18.7 %collective-permute-start.3 = (bf16[1024,128]{1,0:T(8,128)(2,1)S(1)}, bf16[1024,128]{1,0:T(8,128)(2,1)}, u32[]{:S(2)}, u32[]{:S(2)}) collective-permute-start(bf16[1024,128]{1,0:T(8,128)(2,1)S(1)} %bitcast.48), channel_id=1, source_target_pairs={{0,2},{1,3},{2,4},{3,5},{4,6},{5,7},{6,0},{7,1},{8,10},{9,11},{10,... | collective-permute-start | bytes 786440 | tf_op jit(solution)/shard_map/ppermute | solution.py:49
  31.4 27.5 %collective-permute-start.4 = (bf16[1024,128]{1,0:T(8,128)(2,1)S(1)}, bf16[1024,128]{1,0:T(8,128)(2,1)}, u32[]{:S(2)}, u32[]{:S(2)}) collective-permute-start(bf16[1024,128]{1,0:T(8,128)(2,1)S(1)} %bitcast.47), channel_id=1, source_target_pairs={{0,4},{1,5},{2,6},{3,7},{4,0},{5,1},{6,2},{7,3},{8,12},{9,13},{10,... | collective-permute-start | bytes 786440 | tf_op jit(solution)/shard_map/ppermute | solution.py:49
  34.1 26.5 %collective-permute-start.5 = (bf16[1024,128]{1,0:T(8,128)(2,1)S(1)}, bf16[1024,128]{1,0:T(8,128)(2,1)}, u32[]{:S(2)}, u32[]{:S(2)}) collective-permute-start(bf16[1024,128]{1,0:T(8,128)(2,1)S(1)} %bitcast.46), channel_id=1, source_target_pairs={{0,6},{1,7},{2,0},{3,1},{4,2},{5,3},{6,4},{7,5},{8,14},{9,15},{10,... | collective-permute-start | bytes 786440 | tf_op jit(solution)/shard_map/ppermute | solution.py:49
  47.3 18.8 %collective-permute-start.12 = (bf16[1024,128]{1,0:T(8,128)(2,1)}, bf16[1024,128]{1,0:T(8,128)(2,1)}, u32[]{:S(2)}, u32[]{:S(2)}) collective-permute-start(bf16[1024,128]{1,0:T(8,128)(2,1)} %bitcast.15.refs_0_), channel_id=1, source_target_pairs={{0,8},{1,9},{2,10},{3,11},{4,12},{5,13},{6,14},{7,15},{8,0},{9,1},... | collective-permute-start | bytes 786440 | tf_op jit(solution)/shard_map/ppermute | solution.py:49
  48.7 17.6 %collective-permute-start.13 = (bf16[1024,128]{1,0:T(8,128)(2,1)}, bf16[1024,128]{1,0:T(8,128)(2,1)}, u32[]{:S(2)}, u32[]{:S(2)}) collective-permute-start(bf16[1024,128]{1,0:T(8,128)(2,1)} %collective-permute-done.3.refs_1_), channel_id=1, source_target_pairs={{0,8},{1,9},{2,10},{3,11},{4,12},{5,13},{6,14},{7,15},{8,0},{9,1},... | collective-permute-start | bytes 786440 | tf_op jit(solution)/shard_map/ppermute | solution.py:49
  53.6 30.3 %copy-start.24 = (f32[2,64,256]{2,1,0:T(8,128)}, f32[2,64,256]{2,1,0:T(8,128)S(1)}, u32[]{:S(2)}) copy-start(f32[2,64,256]{2,1,0:T(8,128)S(1)} %get-tuple-element.91.refs_5_) | copy-start | bytes 393220
  58.7 47.7 %collective-permute-start.10 = (bf16[2,128,1024]{2,1,0:T(8,128)(2,1)}, bf16[2,128,1024]{2,1,0:T(8,128)(2,1)}, u32[]{:S(2)}, u32[]{:S(2)}) collective-permute-start(bf16[2,128,1024]{2,1,0:T(8,128)(2,1)} %get-tuple-element.65), channel_id=1, source_target_pairs={{0,64},{8,72},{16,80},{24,88},{32,96},{40,104},{48,112},{56,120},{... | collective-permute-start | bytes 1572872 | tf_op jit(solution)/shard_map/ppermute | solution.py:40
  58.9 49.2 %collective-permute-start.11 = (bf16[2,128,1024]{2,1,0:T(8,128)(2,1)}, bf16[2,128,1024]{2,1,0:T(8,128)(2,1)}, u32[]{:S(2)}, u32[]{:S(2)}) collective-permute-start(bf16[2,128,1024]{2,1,0:T(8,128)(2,1)} %get-tuple-element.67), channel_id=1, source_target_pairs={{0,72},{8,64},{16,88},{24,80},{32,104},{40,96},{48,120},{56,112},{... | collective-permute-start | bytes 1572872 | tf_op jit(solution)/shard_map/ppermute | solution.py:40
  60.6 47.6 %collective-permute-start.9 = (bf16[2,128,1024]{2,1,0:T(8,128)(2,1)}, bf16[2,128,1024]{2,1,0:T(8,128)(2,1)}, u32[]{:S(2)}, u32[]{:S(2)}) collective-permute-start(bf16[2,128,1024]{2,1,0:T(8,128)(2,1)} %get-tuple-element.63), channel_id=1, source_target_pairs={{0,8},{8,0},{16,24},{24,16},{32,40},{40,32},{48,56},{56,48},{64,72... | collective-permute-start | bytes 1572872 | tf_op jit(solution)/shard_map/ppermute | solution.py:40
  60.6 35.1 %all-to-all-start.1 = ((bf16[16,2,128,128]{3,2,1,0:T(8,128)(2,1)}), bf16[16,2,128,128]{3,2,1,0:T(8,128)(2,1)S(1)}, u32[]{:S(2)}, u32[]{:S(2)}) async-start(bf16[16,2,128,128]{3,2,1,0:T(8,128)(2,1)} %bitcast.20), calls=%async_computation.1 | async-start | bytes 2097152 | tf_op jit(solution)/shard_map/all_to_all | solution.py:33
  66.1 19.3 %collective-permute-start.14 = (bf16[1024,128]{1,0:T(8,128)(2,1)}, bf16[1024,128]{1,0:T(8,128)(2,1)S(1)}, u32[]{:S(2)}, u32[]{:S(2)}) collective-permute-start(bf16[1024,128]{1,0:T(8,128)(2,1)} %collective-permute-done.4.refs_2_), channel_id=1, source_target_pairs={{0,8},{1,9},{2,10},{3,11},{4,12},{5,13},{6,14},{7,15},{8,0},{9,1},... | collective-permute-start | bytes 786440 | tf_op jit(solution)/shard_map/ppermute | solution.py:49
  66.3 20.1 %collective-permute-start.15 = (bf16[1024,128]{1,0:T(8,128)(2,1)}, bf16[1024,128]{1,0:T(8,128)(2,1)S(1)}, u32[]{:S(2)}, u32[]{:S(2)}) collective-permute-start(bf16[1024,128]{1,0:T(8,128)(2,1)} %collective-permute-done.5.refs_3_), channel_id=1, source_target_pairs={{0,8},{1,9},{2,10},{3,11},{4,12},{5,13},{6,14},{7,15},{8,0},{9,1},... | collective-permute-start | bytes 786440 | tf_op jit(solution)/shard_map/ppermute | solution.py:49
  86.1 40.5 %collective-permute-start.6 = (bf16[128,1024]{1,0:T(8,128)(2,1)}, bf16[128,1024]{1,0:T(8,128)(2,1)S(1)}, u32[]{:S(2)}, u32[]{:S(2)}) collective-permute-start(bf16[128,1024]{1,0:T(8,128)(2,1)} %get-tuple-element.59), channel_id=1, source_target_pairs={{0,8},{8,0},{16,24},{24,16},{32,40},{40,32},{48,56},{56,48},{64,72... | collective-permute-start | bytes 786440 | tf_op jit(solution)/shard_map/ppermute | solution.py:40
  87.1 39.5 %collective-permute-start.7 = (bf16[128,1024]{1,0:T(8,128)(2,1)}, bf16[128,1024]{1,0:T(8,128)(2,1)S(1)}, u32[]{:S(2)}, u32[]{:S(2)}) collective-permute-start(bf16[128,1024]{1,0:T(8,128)(2,1)} %get-tuple-element.60), channel_id=1, source_target_pairs={{0,64},{8,72},{16,80},{24,88},{32,96},{40,104},{48,112},{56,120},{... | collective-permute-start | bytes 786440 | tf_op jit(solution)/shard_map/ppermute | solution.py:40
  95.7 35.7 %all-to-all-start.2 = ((bf16[16,2,128,128]{3,2,1,0:T(8,128)(2,1)}), bf16[16,2,128,128]{3,2,1,0:T(8,128)(2,1)S(1)}, u32[]{:S(2)}, u32[]{:S(2)}) async-start(bf16[16,2,128,128]{3,2,1,0:T(8,128)(2,1)} %get-tuple-element.75), calls=%async_computation.2 | async-start | bytes 2097152 | tf_op jit(solution)/shard_map/all_to_all | solution.py:33
  106.4 20.2 %collective-permute-start.8 = (bf16[128,1024]{1,0:T(8,128)(2,1)}, bf16[128,1024]{1,0:T(8,128)(2,1)S(1)}, u32[]{:S(2)}, u32[]{:S(2)}) collective-permute-start(bf16[128,1024]{1,0:T(8,128)(2,1)} %copy-done.35), channel_id=1, source_target_pairs={{0,72},{8,64},{16,88},{24,80},{32,104},{40,96},{48,120},{56,112},{... | collective-permute-start | bytes 786440 | tf_op jit(solution)/shard_map/ppermute | solution.py:40
  126.6 39.3 %copy-start.11 = (bf16[1024,128]{1,0:T(8,128)(2,1)S(1)}, bf16[1024,128]{1,0:T(8,128)(2,1)}, u32[]{:S(2)}) copy-start(bf16[1024,128]{1,0:T(8,128)(2,1)} %copy-done.10) | copy-start | bytes 786436
  126.6 39.3 %copy-start.13 = (bf16[1024,128]{1,0:T(8,128)(2,1)S(1)}, bf16[1024,128]{1,0:T(8,128)(2,1)}, u32[]{:S(2)}) copy-start(bf16[1024,128]{1,0:T(8,128)(2,1)} %copy-done.12) | copy-start | bytes 786436
  131.4 39.3 %all-to-all-start.3 = ((bf16[16,2,128,128]{3,2,1,0:T(8,128)(2,1)}), bf16[16,2,128,128]{3,2,1,0:T(8,128)(2,1)S(1)}, u32[]{:S(2)}, u32[]{:S(2)}) async-start(bf16[16,2,128,128]{3,2,1,0:T(8,128)(2,1)} %get-tuple-element.79), calls=%async_computation.3 | async-start | bytes 2097152 | tf_op jit(solution)/shard_map/all_to_all | solution.py:33
  146.4 6.4 %collective-permute-start.19 = (bf16[128,256]{1,0:T(8,128)(2,1)S(1)}, bf16[128,256]{1,0:T(8,128)(2,1)S(1)}, u32[]{:S(2)}, u32[]{:S(2)}) collective-permute-start(bf16[128,256]{1,0:T(8,128)(2,1)S(1)} %get-tuple-element.80.refs_8_), channel_id=1, source_target_pairs={{0,2},{1,3},{2,4},{3,5},{4,6},{5,7},{6,0},{7,1},{8,10},{9,11},{10,... | collective-permute-start | bytes 196616 | tf_op jit(solution)/shard_map/ppermute | solution.py:49
  146.4 8.4 %collective-permute-start.20 = (bf16[128,256]{1,0:T(8,128)(2,1)S(1)}, bf16[128,256]{1,0:T(8,128)(2,1)S(1)}, u32[]{:S(2)}, u32[]{:S(2)}) collective-permute-start(bf16[128,256]{1,0:T(8,128)(2,1)S(1)} %get-tuple-element.80.refs_8_), channel_id=1, source_target_pairs={{0,4},{1,5},{2,6},{3,7},{4,0},{5,1},{6,2},{7,3},{8,12},{9,13},{10,... | collective-permute-start | bytes 196616 | tf_op jit(solution)/shard_map/ppermute | solution.py:49
  146.4 8.4 %collective-permute-start.21 = (bf16[128,256]{1,0:T(8,128)(2,1)S(1)}, bf16[128,256]{1,0:T(8,128)(2,1)S(1)}, u32[]{:S(2)}, u32[]{:S(2)}) collective-permute-start(bf16[128,256]{1,0:T(8,128)(2,1)S(1)} %get-tuple-element.80.refs_8_), channel_id=1, source_target_pairs={{0,6},{1,7},{2,0},{3,1},{4,2},{5,3},{6,4},{7,5},{8,14},{9,15},{10,... | collective-permute-start | bytes 196616 | tf_op jit(solution)/shard_map/ppermute | solution.py:49
  149.0 19.5 %collective-permute-start.16 = (bf16[128,1024]{1,0:T(8,128)(2,1)}, bf16[128,1024]{1,0:T(8,128)(2,1)S(1)}, u32[]{:S(2)}, u32[]{:S(2)}) collective-permute-start(bf16[128,1024]{1,0:T(8,128)(2,1)} %copy-done.34), channel_id=1, source_target_pairs={{0,8},{8,0},{16,24},{24,16},{32,40},{40,32},{48,56},{56,48},{64,72... | collective-permute-start | bytes 786440 | tf_op jit(solution)/shard_map/ppermute | solution.py:40
  149.8 18.8 %collective-permute-start.17 = (bf16[128,1024]{1,0:T(8,128)(2,1)}, bf16[128,1024]{1,0:T(8,128)(2,1)S(1)}, u32[]{:S(2)}, u32[]{:S(2)}) collective-permute-start(bf16[128,1024]{1,0:T(8,128)(2,1)} %copy-done.33), channel_id=1, source_target_pairs={{0,64},{8,72},{16,80},{24,88},{32,96},{40,104},{48,112},{56,120},{... | collective-permute-start | bytes 786440 | tf_op jit(solution)/shard_map/ppermute | solution.py:40
  152.8 17.3 %collective-permute-start.18 = (bf16[128,1024]{1,0:T(8,128)(2,1)}, bf16[128,1024]{1,0:T(8,128)(2,1)S(1)}, u32[]{:S(2)}, u32[]{:S(2)}) collective-permute-start(bf16[128,1024]{1,0:T(8,128)(2,1)} %copy-done.32), channel_id=1, source_target_pairs={{0,72},{8,64},{16,88},{24,80},{32,104},{40,96},{48,120},{56,112},{... | collective-permute-start | bytes 786440 | tf_op jit(solution)/shard_map/ppermute | solution.py:40
  154.8 1.3 collective-permute-start.22
  154.8 7.1 %collective-permute-start.23 = (bf16[128,256]{1,0:T(8,128)(2,1)S(1)}, bf16[128,256]{1,0:T(8,128)(2,1)S(1)}, u32[]{:S(2)}, u32[]{:S(2)}) collective-permute-start(bf16[128,256]{1,0:T(8,128)(2,1)S(1)} %get-tuple-element.81), channel_id=1, source_target_pairs={{0,10},{1,11},{2,12},{3,13},{4,14},{5,15},{6,8},{7,9},{8,2},{9,3},... | collective-permute-start | bytes 196616 | tf_op jit(solution)/shard_map/ppermute | solution.py:49
  156.0 5.9 %collective-permute-start.24 = (bf16[128,256]{1,0:T(8,128)(2,1)S(1)}, bf16[128,256]{1,0:T(8,128)(2,1)S(1)}, u32[]{:S(2)}, u32[]{:S(2)}) collective-permute-start(bf16[128,256]{1,0:T(8,128)(2,1)S(1)} %get-tuple-element.81), channel_id=1, source_target_pairs={{0,12},{1,13},{2,14},{3,15},{4,8},{5,9},{6,10},{7,11},{8,4},{9,5},... | collective-permute-start | bytes 196616 | tf_op jit(solution)/shard_map/ppermute | solution.py:49
  161.9 4.0 %collective-permute-start.25 = (bf16[128,256]{1,0:T(8,128)(2,1)S(1)}, bf16[128,256]{1,0:T(8,128)(2,1)S(1)}, u32[]{:S(2)}, u32[]{:S(2)}) collective-permute-start(bf16[128,256]{1,0:T(8,128)(2,1)S(1)} %get-tuple-element.81), channel_id=1, source_target_pairs={{0,14},{1,15},{2,8},{3,9},{4,10},{5,11},{6,12},{7,13},{8,6},{9,7},... | collective-permute-start | bytes 196616 | tf_op jit(solution)/shard_map/ppermute | solution.py:49
  168.6 16.7 %copy-start.18 = (bf16[128,1024]{1,0:T(8,128)(2,1)}, bf16[128,1024]{1,0:T(8,128)(2,1)S(1)}, u32[]{:S(2)}) copy-start(bf16[128,1024]{1,0:T(8,128)(2,1)S(1)} %collective-permute-done.17.refs_6_) | copy-start | bytes 786436
  172.7 6.4 %collective-permute-start.26 = (bf16[128,256]{1,0:T(8,128)(2,1)S(1)}, bf16[128,256]{1,0:T(8,128)(2,1)S(1)}, u32[]{:S(2)}, u32[]{:S(2)}) collective-permute-start(bf16[128,256]{1,0:T(8,128)(2,1)S(1)} %get-tuple-element.88.refs_8_), channel_id=1, source_target_pairs={{0,2},{1,3},{2,4},{3,5},{4,6},{5,7},{6,0},{7,1},{8,10},{9,11},{10,... | collective-permute-start | bytes 196616 | tf_op jit(solution)/shard_map/ppermute | solution.py:49
  172.7 6.4 %collective-permute-start.27 = (bf16[128,256]{1,0:T(8,128)(2,1)S(1)}, bf16[128,256]{1,0:T(8,128)(2,1)S(1)}, u32[]{:S(2)}, u32[]{:S(2)}) collective-permute-start(bf16[128,256]{1,0:T(8,128)(2,1)S(1)} %get-tuple-element.88.refs_8_), channel_id=1, source_target_pairs={{0,4},{1,5},{2,6},{3,7},{4,0},{5,1},{6,2},{7,3},{8,12},{9,13},{10,... | collective-permute-start | bytes 196616 | tf_op jit(solution)/shard_map/ppermute | solution.py:49
  172.7 9.3 %collective-permute-start.28 = (bf16[128,256]{1,0:T(8,128)(2,1)S(1)}, bf16[128,256]{1,0:T(8,128)(2,1)S(1)}, u32[]{:S(2)}, u32[]{:S(2)}) collective-permute-start(bf16[128,256]{1,0:T(8,128)(2,1)S(1)} %get-tuple-element.88.refs_8_), channel_id=1, source_target_pairs={{0,6},{1,7},{2,0},{3,1},{4,2},{5,3},{6,4},{7,5},{8,14},{9,15},{10,... | collective-permute-start | bytes 196616 | tf_op jit(solution)/shard_map/ppermute | solution.py:49
  175.4 6.6 %collective-permute-start.29 = (bf16[128,256]{1,0:T(8,128)(2,1)S(1)}, bf16[128,256]{1,0:T(8,128)(2,1)S(1)}, u32[]{:S(2)}, u32[]{:S(2)}) collective-permute-start(bf16[128,256]{1,0:T(8,128)(2,1)S(1)} %get-tuple-element.89), channel_id=1, source_target_pairs={{0,8},{1,9},{2,10},{3,11},{4,12},{5,13},{6,14},{7,15},{8,0},{9,1},... | collective-permute-start | bytes 196616 | tf_op jit(solution)/shard_map/ppermute | solution.py:49
  176.2 5.9 %collective-permute-start.30 = (bf16[128,256]{1,0:T(8,128)(2,1)S(1)}, bf16[128,256]{1,0:T(8,128)(2,1)S(1)}, u32[]{:S(2)}, u32[]{:S(2)}) collective-permute-start(bf16[128,256]{1,0:T(8,128)(2,1)S(1)} %get-tuple-element.89), channel_id=1, source_target_pairs={{0,10},{1,11},{2,12},{3,13},{4,14},{5,15},{6,8},{7,9},{8,2},{9,3},... | collective-permute-start | bytes 196616 | tf_op jit(solution)/shard_map/ppermute | solution.py:49
  179.1 6.1 %collective-permute-start.31 = (bf16[128,256]{1,0:T(8,128)(2,1)S(1)}, bf16[128,256]{1,0:T(8,128)(2,1)S(1)}, u32[]{:S(2)}, u32[]{:S(2)}) collective-permute-start(bf16[128,256]{1,0:T(8,128)(2,1)S(1)} %get-tuple-element.89), channel_id=1, source_target_pairs={{0,12},{1,13},{2,14},{3,15},{4,8},{5,9},{6,10},{7,11},{8,4},{9,5},... | collective-permute-start | bytes 196616 | tf_op jit(solution)/shard_map/ppermute | solution.py:49
  179.1 6.1 %collective-permute-start.32 = (bf16[128,256]{1,0:T(8,128)(2,1)S(1)}, bf16[128,256]{1,0:T(8,128)(2,1)S(1)}, u32[]{:S(2)}, u32[]{:S(2)}) collective-permute-start(bf16[128,256]{1,0:T(8,128)(2,1)S(1)} %get-tuple-element.89), channel_id=1, source_target_pairs={{0,14},{1,15},{2,8},{3,9},{4,10},{5,11},{6,12},{7,13},{8,6},{9,7},... | collective-permute-start | bytes 196616 | tf_op jit(solution)/shard_map/ppermute | solution.py:49
  188.7 9.5 %copy-start.17 = (bf16[128,1024]{1,0:T(8,128)(2,1)S(1)}, bf16[128,1024]{1,0:T(8,128)(2,1)}, u32[]{:S(2)}) copy-start(bf16[128,1024]{1,0:T(8,128)(2,1)} %copy-done.16) | copy-start | bytes 786436
  188.7 38.1 %all-to-all-start.4 = ((bf16[64,16,512]{2,1,0:T(8,128)(2,1)}), bf16[64,16,512]{2,1,0:T(8,128)(2,1)S(1)}, u32[]{:S(2)}, u32[]{:S(2)}) async-start(bf16[64,16,512]{2,1,0:T(8,128)(2,1)} %bitcast.27), calls=%async_computation.4 | async-start | bytes 2097152 | tf_op jit(solution)/shard_map/all_to_all | solution.py:33
  (28 other events, 74.7 us)
